TPU v7x, 32 devices: a whole 2x2x4 slice. The times are simulated.
32 devices in a mesh: section: 2 (over x), dp: 16 (over z, y, core).
Axes of the slice: x: 2, y: 2, z: 4, core: 2. Of those that a mesh axis runs over, the one named last changes fastest.
Arguments:
- sources: bfloat16 [13824, 1024], P('dp'), may hold values from -6 to 6
- targets: bfloat16 [8192, 1024], P('dp'), may hold values from -6 to 6
- cotangent: bfloat16 [8192, 1024], P('dp'), may hold values from -6 to 6
- source_lengths: int32 [16, 2], P('dp'), may hold values from 48 to 768, as said below
- target_lengths: int32 [16, 2], P('dp'), may hold values from 128 to 256, as said below
- attn_qkv: bfloat16 [2, 1024, 3072], P('section'), may hold values from -0.1875 to 0.1875
- attn_out: bfloat16 [2, 1024, 1024], P('section'), may hold values from -0.75 to 0.75
- ffn_in: bfloat16 [2, 1024, 4096], P('section'), may hold values from -0.1875 to 0.1875
- ffn_out: bfloat16 [2, 4096, 1024], P('section'), may hold values from -0.09375 to 0.09375
- norm_gains: float32 [2, 2, 1024], P('section'), may hold values from 0.5 to 1.5
- prefix_pairs: bfloat16 [2, 2, 30, 1024], P('section'), may hold values from -6 to 6
- adapt_down: bfloat16 [2, 1024, 512], P('section'), may hold values from -0.1875 to 0.1875
- adapt_down_bias: float32 [2, 512], P('section'), may hold values from -3 to 3
- adapt_up: bfloat16 [2, 512, 1024], P('section'), may hold values from -0.0625 to 0.0625
- adapt_up_bias: float32 [2, 1024], P('section'), may hold values from -0.6 to 0.6
- cross_query: bfloat16 [1024, 1024], replicated, may hold values from -0.1875 to 0.1875
- cross_pairs: bfloat16 [1024, 2048], replicated, may hold values from -0.1875 to 0.1875
- cross_out: bfloat16 [1024, 1024], replicated, may hold values from -0.75 to 0.75
- cross_gain: float32 [1024], replicated, may hold values from 0.5 to 1.5
Outputs:
- decoder_output: bfloat16 [8192, 1024], P('dp', 'section')
- source_grad: bfloat16 [13824, 1024], P('dp', 'section')
- target_grad: bfloat16 [8192, 1024], P('dp', 'section')
- prefix_grad: float32 [2, 2, 30, 1024], P('section')
- down_grad: float32 [2, 1024, 512], P('section')
- down_bias_grad: float32 [2, 512], P('section')
- up_grad: float32 [2, 512, 1024], P('section')
- up_bias_grad: float32 [2, 1024], P('section')
Inputs may be any that keep to these rules, and one draw needn't show every extreme that they name: `source_lengths`: row i holds data index i's lengths: the first column (long bucket) lies from 97 to 768 and equals 768 for some i; the second (short bucket) lies from 48 to 96 and equals 96 for some i. `target_lengths`: each column equals 256 for some row.
All inputs are finite; a program needn't handle non-finite values.
Results may differ from a plain program's by a relative error of at most 0.023.
Values may be sent and summed in bfloat16 or wider, within the bound.
A program may use at most 448 MiB of HBM per device.

v0:
```python
import functools

import jax
import jax.numpy as jnp
from jax import lax
from jax.experimental import pallas as pl
from jax.experimental.pallas import tpu as pltpu
from jax.sharding import PartitionSpec as P

HD = 64
PRE = 30
PRE_PAD = 32
SRC_LONG = 768
SRC_SHORT = 96
TGT = 256
LANES = 128

BF = jnp.bfloat16
F32 = jnp.float32
norm_eps = 1e-05
big_negative = -1e30
adapter_scale = 4.0
chunk = 512
wide = 1024
ENC_ROWS = (SRC_LONG + SRC_SHORT) // 3
vmem_bytes = 56 * 2**20

phi_poly = (
    0.797869713181688,
    0.036392283539041996,
    -8.782472977701046e-05,
    -3.669384069669515e-05,
    1.4250308145882202e-06,
)


def nn(left, right):
    return lax.dot_general(left, right, (((1,), (0,)), ((), ())), preferred_element_type=F32)


def nt(left, right):
    return lax.dot_general(left, right, (((1,), (1,)), ((), ())), preferred_element_type=F32)


def tn(left, right):
    return lax.dot_general(left, right, (((0,), (0,)), ((), ())), preferred_element_type=F32)


def gelu_pair(values):
    square = values * values
    poly = phi_poly[4]
    for coefficient in phi_poly[3::-1]:
        poly = poly * square + coefficient
    half = 0.5 * jnp.tanh(values * poly) + 0.5
    density = jnp.exp(square * -0.5) * 0.3989422804014327
    return values * half, half + values * density


def row_tiles(rows, most=288):
    count = -(-rows // most)
    size = rows // count
    return [(i * size, size) for i in range(count)]


def norm_rows(values):
    centered = values - jnp.mean(values, axis=-1, keepdims=True)
    scale = lax.rsqrt(jnp.mean(centered * centered, axis=-1, keepdims=True) + norm_eps)
    return centered * scale, scale


def norm_rows_back(hat, scale, grad_hat):
    mean_grad = jnp.mean(grad_hat, axis=-1, keepdims=True)
    mean_dot = jnp.mean(grad_hat * hat, axis=-1, keepdims=True)
    return scale * (grad_hat - mean_grad - hat * mean_dot)


def params(limit=vmem_bytes):
    return pltpu.CompilerParams(vmem_limit_bytes=limit)


def whole(shape):
    return pl.BlockSpec(shape, lambda *g: (0,) * len(shape))


def product_kernel(x_ref, w_ref, o_ref):
    o_ref[...] = nn(x_ref[...], w_ref[...]).astype(BF)


def product(x, w, tile=1024):
    rows, depth = x.shape
    width = w.shape[1]
    return pl.pallas_call(
        product_kernel,
        grid=(width // tile,),
        in_specs=[whole((rows, depth)), pl.BlockSpec((depth, tile), lambda i: (0, i))],
        out_specs=pl.BlockSpec((rows, tile), lambda i: (0, i)),
        out_shape=jax.ShapeDtypeStruct((rows, width), BF),
        compiler_params=params(),
        name="product",
    )(x, w)


def back_product_kernel(*refs, parts, residual, cuts):
    grads = refs[:parts]
    w_ref = refs[parts]
    outs = refs[-len(cuts) :]
    total = None
    width = grads[0].shape[1]
    for i, grad in enumerate(grads):
        term = nt(grad[...], w_ref[:, i * width : (i + 1) * width])
        total = term if total is None else total + term
    if residual:
        total = total + refs[parts + 1][...]
    for (start, size), o_ref in zip(cuts, outs):
        o_ref[...] = total[start : start + size].astype(BF)


def back_product(grads, w, residual=None, tile=512, cuts=None):
    rows, width = grads[0].shape
    depth = w.shape[0]
    parts = len(grads)
    cuts = cuts or ((0, rows),)
    specs = [whole((rows, width))] * parts + [
        pl.BlockSpec((tile, parts * width), lambda i: (i, 0))
    ]
    args = list(grads) + [w]
    if residual is not None:
        specs.append(pl.BlockSpec((rows, tile), lambda i: (0, i)))
        args.append(residual)
    return pl.pallas_call(
        functools.partial(
            back_product_kernel, parts=parts, residual=residual is not None, cuts=cuts
        ),
        grid=(depth // tile,),
        in_specs=specs,
        out_specs=[pl.BlockSpec((size, tile), lambda i: (0, i)) for _, size in cuts],
        out_shape=[jax.ShapeDtypeStruct((size, depth), BF) for _, size in cuts],
        compiler_params=params(),
        name="back_product",
    )(*args)


def head_lanes(head):
    lane = lax.broadcasted_iota(jnp.int32, (1, LANES), 1)
    own = (lane < HD) if head == 0 else (lane >= HD)
    first = HD if head == 0 else 0
    return own, lane == first, lane == first + 1


def bf(value):
    return jnp.asarray(value, BF)


def rows_of(refs, start, count):
    parts = []
    for ref in refs:
        size = ref.shape[0]
        low, high = max(start, 0), min(start + count, size)
        if low < high:
            parts.append(ref[low:high])
        start -= size
    return parts


def stacked(refs, prefix_ref, start, count):
    parts = rows_of(refs, start, count)
    if prefix_ref is not None:
        parts.append(prefix_ref[...])
    return parts[0] if len(parts) == 1 else jnp.concatenate(parts, 0)


def attend_pair(*refs, segs, prefix, causal, pieces, which):
    len_ref, q_ref = refs[:2]
    k_refs, v_refs = refs[2 : 2 + pieces], refs[2 + pieces : 2 + 2 * pieces]
    at = 2 + 2 * pieces
    pk_ref = pv_ref = None
    if prefix:
        pk_ref, pv_ref = refs[at : at + 2]
        at += 2
    o_ref, inv_ref = refs[at : at + 2]
    p_refs = refs[at + 2 :]
    for seg, (q0, nq, k0, nk) in enumerate(segs):
        keys = stacked(k_refs, pk_ref, k0, nk)
        values = stacked(v_refs, pv_ref, k0, nk)
        count = keys.shape[0]
        row = lax.broadcasted_iota(jnp.int32, (count, 1), 0)
        seen = row < jnp.minimum(len_ref[0, which + seg], nk)
        if prefix:
            seen = seen | ((row >= nk) & (row < nk + PRE))
        queries = q_ref[q0 : q0 + nq] * bf(HD**-0.5)
        out = inv = None
        for head in range(2):
            own, first, _ = head_lanes(head)
            k_own = jnp.where(own, keys, jnp.where(first & ~seen, bf(big_negative), bf(0)))
            q_own = jnp.where(own, queries, jnp.where(first, bf(1), bf(0)))
            v_own = jnp.where(own, values, bf(1))
            scores = nt(k_own, q_own)
            if causal:
                key_at = lax.broadcasted_iota(jnp.int32, scores.shape, 0)
                query_at = lax.broadcasted_iota(jnp.int32, scores.shape, 1)
                allowed = (key_at <= query_at) | (key_at >= nk)
                scores = jnp.where(allowed, scores, big_negative)
            peak = jnp.max(scores, axis=0, keepdims=True)
            weights = jnp.exp(scores - peak).astype(BF)
            p_refs[seg][head] = weights
            mixed = tn(weights, v_own)
            inverse = 1.0 / pltpu.roll(mixed, HD, 1)
            mixed = mixed * inverse
            out = mixed if out is None else jnp.where(own, mixed, out)
            inv = inverse if inv is None else jnp.where(own, inverse, inv)
        o_ref[q0 : q0 + nq] = out.astype(BF)
        inv_ref[q0 : q0 + nq] = inv


def lane_views(refs, group, j):
    views = []
    for ref in refs:
        if len(ref.shape) == 2:
            views.append(ref.at[:, j * LANES : (j + 1) * LANES])
        else:
            views.append(ref.at[2 * j : 2 * j + 2])
    return views


def attend_kernel(len_ref, *refs, group, **kw):
    for j in range(group):
        attend_pair(len_ref, *lane_views(refs, group, j), **kw)


def column_spec(rows, offset, row_block=0, group=1):
    return pl.BlockSpec((rows, group * LANES), lambda h: (row_block, h + offset // group))


def attend(lengths, q, keys, values, prefixes, segs, causal, which=0, group=1):
    pairs = 8
    q_rows = q[1]
    prefix = prefixes is not None
    extra = PRE_PAD if prefix else 0
    specs = [pl.BlockSpec(memory_space=pltpu.SMEM)]
    args = [lengths]
    for array, rows, block, offset in [q, *keys, *values]:
        specs.append(column_spec(rows, offset, block, group))
        args.append(array)
    if prefix:
        specs += [column_spec(PRE_PAD, 0, 0, group)] * 2
        args += list(prefixes)
    weight_shapes = [(2 * pairs, nk + extra, nq) for _, nq, _, nk in segs]
    return pl.pallas_call(
        functools.partial(
            attend_kernel, group=group, segs=segs, prefix=prefix, causal=causal, pieces=len(keys), which=which
        ),
        grid=(pairs // group,),
        in_specs=specs,
        out_specs=[column_spec(q_rows, 0, 0, group)] * 2
        + [pl.BlockSpec((2 * group,) + s[1:], lambda h: (h, 0, 0)) for s in weight_shapes],
        out_shape=[
            jax.ShapeDtypeStruct((q_rows, pairs * LANES), BF),
            jax.ShapeDtypeStruct((q_rows, pairs * LANES), F32),
        ]
        + [jax.ShapeDtypeStruct(s, BF) for s in weight_shapes],
        compiler_params=params(),
        name="attend",
    )(*args)


def attend_back_pair(
    q_ref, k_refs, v_refs, o_ref, inv_ref, g_refs, pk_ref, pv_ref, p_refs, dq_ref, dk_ref, dv_ref, segs
):
    prefix_totals = [None, None]
    scale = HD**-0.5
    for seg, (q0, nq, k0, nk) in enumerate(segs):
        keys = stacked(k_refs, pk_ref, k0, nk)
        values = stacked(v_refs, pv_ref, k0, nk)
        queries = q_ref[q0 : q0 + nq]
        grads = stacked(g_refs, None, q0, nq).astype(F32) * inv_ref[q0 : q0 + nq]
        grads_low = grads.astype(BF)
        dots = grads * o_ref[q0 : q0 + nq].astype(F32)
        dq = dk = dv = None
        for head in range(2):
            own, first, second = head_lanes(head)
            row_dot = -jnp.sum(jnp.where(own, dots, 0.0), axis=1, keepdims=True)
            high = row_dot.astype(BF)
            rest = (row_dot - high.astype(F32)).astype(BF)
            g_own = jnp.where(
                own, grads_low, jnp.where(first, high, jnp.where(second, rest, bf(0)))
            )
            v_own = jnp.where(own, values, jnp.where(first | second, bf(1), bf(0)))
            weights = p_refs[seg][head]
            score_grad = (weights.astype(F32) * nt(v_own, g_own)).astype(BF)
            dv_head = nn(weights, grads_low)
            dk_head = nn(score_grad, queries)
            dq_head = tn(score_grad, keys)
            dq = dq_head if dq is None else jnp.where(own, dq_head, dq)
            dk = dk_head if dk is None else jnp.where(own, dk_head, dk)
            dv = dv_head if dv is None else jnp.where(own, dv_head, dv)
        dk = dk * scale
        dq_ref[q0 : q0 + nq] = (dq * scale).astype(BF)
        at = k0 - segs[0][2]
        dk_ref[at : at + nk] = dk[:nk].astype(BF)
        dv_ref[at : at + nk] = dv[:nk].astype(BF)
        if pk_ref is not None:
            for i, grad in enumerate((dk, dv)):
                part = grad[nk:]
                prefix_totals[i] = part if seg == 0 else prefix_totals[i] + part
    return prefix_totals


def attend_back_kernel(*refs, group, **kw):
    for j in range(group):
        attend_back_views(*lane_views(refs, group, j), **kw)


def attend_back_views(*refs, segs, prefix, pieces):
    q_ref, o_ref, inv_ref, g_ref = refs[:4]
    k_refs, v_refs = refs[4 : 4 + pieces], refs[4 + pieces : 4 + 2 * pieces]
    at = 4 + 2 * pieces
    pk_ref = pv_ref = None
    if prefix:
        pk_ref, pv_ref = refs[at : at + 2]
        at += 2
    outs = refs[at + len(segs) :]
    totals = attend_back_pair(
        q_ref, k_refs, v_refs, o_ref, inv_ref, [g_ref], pk_ref, pv_ref,
        refs[at : at + len(segs)], *outs[:3], segs,
    )
    if prefix:
        outs[3][...] = totals[0]
        outs[4][...] = totals[1]


def attend_back(q, keys, values, prefixes, attended, inverse, grad, weights, segs, group=2):
    pairs = 8
    q_rows = q[1]
    k_rows = sum(nk for _, _, _, nk in segs)
    prefix = prefixes is not None
    specs, args = [], []
    own = [(a, q_rows, 0, 0) for a in (attended, inverse, grad)]
    for array, rows, block, offset in [q, *own, *keys, *values]:
        specs.append(column_spec(rows, offset, block, group))
        args.append(array)
    if prefix:
        specs += [column_spec(PRE_PAD, 0, 0, group)] * 2
        args += list(prefixes)
    specs += [pl.BlockSpec((2 * group,) + w.shape[1:], lambda h: (h, 0, 0)) for w in weights]
    args += list(weights)
    out_specs = [column_spec(n, 0, 0, group) for n in (q_rows, k_rows, k_rows)]
    out_shape = [
        jax.ShapeDtypeStruct((q_rows, pairs * LANES), BF),
        jax.ShapeDtypeStruct((k_rows, pairs * LANES), BF),
        jax.ShapeDtypeStruct((k_rows, pairs * LANES), BF),
    ]
    if prefix:
        out_specs += [column_spec(PRE_PAD, 0, 0, group)] * 2
        out_shape += [jax.ShapeDtypeStruct((PRE_PAD, pairs * LANES), F32)] * 2
    return pl.pallas_call(
        functools.partial(
            attend_back_kernel, group=group, segs=segs, prefix=prefix, pieces=len(keys)
        ),
        grid=(pairs // group,),
        in_specs=specs,
        out_specs=out_specs,
        out_shape=out_shape,
        compiler_params=params(),
        name="attend_back",
    )(*args)


def ffn_step(low_ref, acc_ref, in_ref, out_ref, slope_ref, act_ref, bias_ref, scale):
    for start, size in row_tiles(low_ref.shape[0]):
        rows = slice(start, start + size)
        hidden = nn(low_ref[rows], in_ref[...])
        if bias_ref is not None:
            hidden = hidden + bias_ref[...]
        active, slope = gelu_pair(hidden)
        slope_ref[rows] = slope.astype(BF)
        active = active.astype(BF)
        if act_ref is not None:
            act_ref[rows] = active
        term = nn(active, out_ref[...])
        acc_ref[rows] += term if scale is None else scale * term


def enc_ffn_kernel(
    x_ref, att_ref, wo_ref, gain_ref, in_ref, out_ref, down_ref, downb_ref, up_ref, upb_ref,
    mem_ref, slope_ref, pre_slope_ref, act_ref, low_ref, scales_ref, acc_ref,
):
    step = pl.program_id(0)
    last = pl.num_programs(0) - 1

    @pl.when(step == 0)
    def _():
        first = x_ref[...].astype(F32) + nn(att_ref[...], wo_ref[...])
        hat, scale = norm_rows(first)
        normed = hat * gain_ref[0:1]
        acc_ref[...] = normed
        low_ref[...] = normed.astype(BF)
        scales_ref[:, 0:1] = scale

    @pl.when((step > 0) & (step < last))
    def _():
        ffn_step(low_ref, acc_ref, in_ref, out_ref, slope_ref, None, None, None)

    @pl.when(step == last)
    def _():
        ffn_step(
            low_ref, acc_ref, down_ref, up_ref, pre_slope_ref, act_ref, downb_ref, adapter_scale
        )
        hat, scale = norm_rows(acc_ref[...] + adapter_scale * upb_ref[...])
        mem_ref[...] = (hat * gain_ref[1:2]).astype(BF)
        scales_ref[:, 1:2] = scale


def enc_ffn(x, att, w, part):
    width = x.shape[1]
    rows = ENC_ROWS
    hidden = w["ffn_in"].shape[1]
    steps = hidden // wide

    def at(i):
        return jnp.clip(i - 1, 0, steps - 1)

    return pl.pallas_call(
        enc_ffn_kernel,
        grid=(steps + 2,),
        in_specs=[
            pl.BlockSpec((rows, width), lambda i: (part, 0)),
            pl.BlockSpec((rows, width), lambda i: (part, 0)),
            whole((width, width)),
            whole((2, width)),
            pl.BlockSpec((width, wide), lambda i: (0, at(i))),
            pl.BlockSpec((wide, width), lambda i: (at(i), 0)),
            whole((width, chunk)),
            whole((1, chunk)),
            whole((chunk, width)),
            whole((1, width)),
        ],
        out_specs=[
            whole((rows, width)),
            pl.BlockSpec((rows, wide), lambda i: (0, at(i))),
            whole((rows, chunk)),
            whole((rows, chunk)),
            whole((rows, width)),
            whole((rows, LANES)),
        ],
        out_shape=[
            jax.ShapeDtypeStruct((rows, width), BF),
            jax.ShapeDtypeStruct((rows, hidden), BF),
            jax.ShapeDtypeStruct((rows, chunk), BF),
            jax.ShapeDtypeStruct((rows, chunk), BF),
            jax.ShapeDtypeStruct((rows, width), BF),
            jax.ShapeDtypeStruct((rows, LANES), F32),
        ],
        scratch_shapes=[pltpu.VMEM((rows, width), F32)],
        compiler_params=params(),
        name="enc_ffn",
    )(
        x, att, w["out"], w["gains"], w["ffn_in"], w["ffn_out"],
        w["down"], w["down_bias"], w["up"], w["up_bias"],
    )


def ffn_back_step(grad_ref, acc_ref, in_ref, out_ref, slope_ref):
    for start, size in row_tiles(grad_ref.shape[0]):
        rows = slice(start, start + size)
        pre = (nt(grad_ref[rows], out_ref[...]) * slope_ref[rows].astype(F32)).astype(BF)
        acc_ref[rows] += nt(pre, in_ref[...])


def adapter_back(grad_ref, acc_ref, low_ref, act_ref, slope_ref, down_ref, up_ref, outs, pre_ref):
    ddown_ref, ddownb_ref, dup_ref, dupb_ref = outs
    total = None
    for start, size in row_tiles(grad_ref.shape[0]):
        rows = slice(start, start + size)
        back = adapter_scale * nt(grad_ref[rows], up_ref[...])
        pre = (back * slope_ref[rows].astype(F32)).astype(BF)
        pre_ref[rows] = pre
        sums = jnp.sum(pre.astype(F32), axis=0, keepdims=True)
        total = sums if total is None else total + sums
        acc_ref[rows] += nt(pre, down_ref[...])
    ddownb_ref[...] = total
    ddown_ref[...] = tn(low_ref[...], pre_ref[...])
    dup_ref[...] = adapter_scale * tn(act_ref[...], grad_ref[...])
    dupb_ref[...] = adapter_scale * jnp.sum(grad_ref[...].astype(F32), axis=0, keepdims=True)


def enc_ffn_back_kernel(
    *refs, pieces,
):
    enc_ffn_back_body(refs[:pieces], *refs[pieces:])


def enc_ffn_back_body(
    dmem_refs, mem_ref, low_ref, scales_ref, gain_ref, slope_ref, pre_slope_ref,
    in_ref, out_ref, down_ref, up_ref, wo_ref,
    dfirst_ref, datt_ref, grad_ref, pre_ref,
    acc_ref,
):
    step = pl.program_id(0)
    last = pl.num_programs(0) - 1

    @pl.when(step == 0)
    def _():
        gain = gain_ref[1:2]
        hat = mem_ref[...].astype(F32) / gain
        grad = norm_rows_back(hat, scales_ref[:, 1:2], stacked(dmem_refs, None, 0, ENC_ROWS).astype(F32) * gain)
        low = grad.astype(BF)
        grad_ref[...] = low
        back = adapter_scale * nt(low, up_ref[...])
        pre = (back * pre_slope_ref[...].astype(F32)).astype(BF)
        pre_ref[...] = pre
        acc_ref[...] = grad + nt(pre, down_ref[...])

    ffn_back_step(grad_ref, acc_ref, in_ref, out_ref, slope_ref)

    @pl.when(step == last)
    def _():
        gain = gain_ref[0:1]
        hat = low_ref[...].astype(F32) / gain
        grad = norm_rows_back(hat, scales_ref[:, 0:1], acc_ref[...] * gain)
        dfirst_ref[...] = grad
        datt_ref[...] = nt(grad.astype(BF), wo_ref[...]).astype(BF)


def enc_ffn_back(dmems, saved, w):
    mem, slope, pre_slope, act, low, scales = saved
    rows, width = mem.shape
    hidden = w["ffn_in"].shape[1]
    steps = hidden // wide
    return pl.pallas_call(
        functools.partial(enc_ffn_back_kernel, pieces=len(dmems)),
        grid=(steps,),
        in_specs=[whole(d.shape) for d in dmems]
        + [
            whole((rows, width)),
            whole((rows, width)),
            whole((rows, LANES)),
            whole((2, width)),
            pl.BlockSpec((rows, wide), lambda i: (0, i)),
            whole((rows, chunk)),
            pl.BlockSpec((width, wide), lambda i: (0, i)),
            pl.BlockSpec((wide, width), lambda i: (i, 0)),
            whole((width, chunk)),
            whole((chunk, width)),
            whole((width, width)),
        ],
        out_specs=[
            whole((rows, width)),
            whole((rows, width)),
            whole((rows, width)),
            whole((rows, chunk)),
        ],
        out_shape=[
            jax.ShapeDtypeStruct((rows, width), F32),
            jax.ShapeDtypeStruct((rows, width), BF),
            jax.ShapeDtypeStruct((rows, width), BF),
            jax.ShapeDtypeStruct((rows, chunk), BF),
        ],
        scratch_shapes=[pltpu.VMEM((rows, width), F32)],
        compiler_params=params(),
        name="enc_ffn_back",
    )(
        *dmems, mem, low, scales, w["gains"], slope, pre_slope,
        w["ffn_in"], w["ffn_out"], w["down"], w["up"], w["out"],
    )


def adapter_grads_kernel(*refs, parts):
    groups = [refs[n * parts : (n + 1) * parts] for n in range(4)]
    low, act, grad, pre = [jnp.concatenate([r[...] for r in g], 0) for g in groups]
    ddown_ref, ddownb_ref, dup_ref, dupb_ref = refs[4 * parts :]
    ddown_ref[...] = tn(low, pre)
    ddownb_ref[...] = jnp.sum(pre.astype(F32), axis=0, keepdims=True)
    dup_ref[...] = adapter_scale * tn(act, grad)
    dupb_ref[...] = adapter_scale * jnp.sum(grad.astype(F32), axis=0, keepdims=True)


def adapter_grads(lows, acts, grads, pres):
    width = lows[0].shape[1]
    return pl.pallas_call(
        functools.partial(adapter_grads_kernel, parts=len(lows)),
        out_shape=[
            jax.ShapeDtypeStruct((width, chunk), F32),
            jax.ShapeDtypeStruct((1, chunk), F32),
            jax.ShapeDtypeStruct((chunk, width), F32),
            jax.ShapeDtypeStruct((1, width), F32),
        ],
        compiler_params=params(),
        name="adapter_grads",
    )(*lows, *acts, *grads, *pres)


def dec_mid_kernel(x_ref, att_ref, wo_ref, gain_ref, wq_ref, n_ref, scale_ref, cq_ref):
    for start, size in row_tiles(x_ref.shape[0], 256):
        rows = slice(start, start + size)
        first = x_ref[rows].astype(F32) + nn(att_ref[rows], wo_ref[...])
        hat, scale = norm_rows(first)
        normed = hat * gain_ref[0:1]
        n_ref[rows] = normed
        scale_ref[rows, 0:1] = scale
        cq_ref[rows] = nn(normed.astype(BF), wq_ref[...]).astype(BF)


def dec_mid(x, att, w, cross):
    rows, width = x.shape
    return pl.pallas_call(
        dec_mid_kernel,
        out_shape=[
            jax.ShapeDtypeStruct((rows, width), F32),
            jax.ShapeDtypeStruct((rows, LANES), F32),
            jax.ShapeDtypeStruct((rows, width), BF),
        ],
        compiler_params=params(),
        name="dec_mid",
    )(x, att, w["out"], w["gains"], cross["query"])


def dec_ffn_kernel(
    len_ref, n_ref, catt_ref, cot_ref, wco_ref, cgain_ref, gain_ref,
    in_ref, out_ref, down_ref, downb_ref, up_ref, upb_ref,
    y_ref, dsecond_ref, dcatt_ref, ddown_ref, ddownb_ref, dup_ref, dupb_ref,
    acc_ref, low_ref, grad_ref, slope_ref, pre_slope_ref, act_ref, pre_ref, scale_ref,
    *, steps, which,
):
    step = pl.program_id(0)
    tiles = row_tiles(n_ref.shape[0], TGT)

    @pl.when(step == 0)
    def _():
        for start, size in tiles:
            rows = slice(start, start + size)
            second = n_ref[rows] + nn(catt_ref[rows], wco_ref[...])
            hat, scale = norm_rows(second)
            middle = hat * cgain_ref[...]
            acc_ref[rows] = middle
            low_ref[rows] = middle.astype(BF)
            scale_ref[rows, 0:1] = scale

    @pl.when((step > 0) & (step <= steps))
    def _():
        ffn_step(low_ref, acc_ref, in_ref, out_ref, slope_ref.at[step - 1], None, None, None)

    @pl.when(step == steps + 1)
    def _():
        ffn_step(
            low_ref, acc_ref, down_ref, up_ref, pre_slope_ref, act_ref, downb_ref,
            adapter_scale,
        )
        for start, size in tiles:
            rows = slice(start, start + size)
            gain = gain_ref[1:2]
            hat, scale = norm_rows(acc_ref[rows] + adapter_scale * upb_ref[...])
            valid = lax.broadcasted_iota(jnp.int32, (size, 1), 0) < len_ref[0, which]
            y_ref[rows] = jnp.where(valid, hat * gain, 0.0).astype(BF)
            cot = jnp.where(valid, cot_ref[rows].astype(F32), 0.0)
            grad = norm_rows_back(hat, scale, cot * gain)
            acc_ref[rows] = grad
            grad_ref[rows] = grad.astype(BF)
        adapter_back(
            grad_ref, acc_ref, low_ref, act_ref, pre_slope_ref, down_ref, up_ref,
            (ddown_ref, ddownb_ref, dup_ref, dupb_ref), pre_ref,
        )

    @pl.when(step > steps + 1)
    def _():
        ffn_back_step(grad_ref, acc_ref, in_ref, out_ref, slope_ref.at[2 * steps + 1 - step])

    @pl.when(step == 2 * steps + 1)
    def _():
        for start, size in tiles:
            rows = slice(start, start + size)
            gain = cgain_ref[...]
            hat = low_ref[rows].astype(F32) / gain
            grad = norm_rows_back(hat, scale_ref[rows, 0:1], acc_ref[rows] * gain)
            dsecond_ref[rows] = grad
            dcatt_ref[rows] = nt(grad.astype(BF), wco_ref[...]).astype(BF)


def dec_ffn(lengths, n, catt, cot, w, cross, which):
    rows, width = catt.shape
    hidden = w["ffn_in"].shape[1]
    steps = hidden // wide

    def at(i):
        return jnp.where(i <= steps, jnp.clip(i - 1, 0, steps - 1), jnp.clip(2 * steps + 1 - i, 0, steps - 1))

    return pl.pallas_call(
        functools.partial(dec_ffn_kernel, steps=steps, which=which),
        grid=(2 * steps + 2,),
        in_specs=[
            pl.BlockSpec(memory_space=pltpu.SMEM),
            pl.BlockSpec((rows, width), lambda i: (which, 0)),
            whole((rows, width)),
            pl.BlockSpec((rows, width), lambda i: (which, 0)),
            whole((width, width)),
            whole((1, width)),
            whole((2, width)),
            pl.BlockSpec((width, wide), lambda i: (0, at(i))),
            pl.BlockSpec((wide, width), lambda i: (at(i), 0)),
            whole((width, chunk)),
            whole((1, chunk)),
            whole((chunk, width)),
            whole((1, width)),
        ],
        out_specs=[
            whole((rows, width)),
            whole((rows, width)),
            whole((rows, width)),
            whole((width, chunk)),
            whole((1, chunk)),
            whole((chunk, width)),
            whole((1, width)),
        ],
        out_shape=[
            jax.ShapeDtypeStruct((rows, width), BF),
            jax.ShapeDtypeStruct((rows, width), F32),
            jax.ShapeDtypeStruct((rows, width), BF),
            jax.ShapeDtypeStruct((width, chunk), F32),
            jax.ShapeDtypeStruct((1, chunk), F32),
            jax.ShapeDtypeStruct((chunk, width), F32),
            jax.ShapeDtypeStruct((1, width), F32),
        ],
        scratch_shapes=[
            pltpu.VMEM((rows, width), F32),
            pltpu.VMEM((rows, width), BF),
            pltpu.VMEM((rows, width), BF),
            pltpu.VMEM((steps, rows, wide), BF),
            pltpu.VMEM((rows, chunk), BF),
            pltpu.VMEM((rows, chunk), BF),
            pltpu.VMEM((rows, chunk), BF),
            pltpu.VMEM((rows, LANES), F32),
        ],
        compiler_params=params(),
        name="dec_ffn",
    )(
        lengths, n, catt, cot, cross["out"], cross["gain"], w["gains"],
        w["ffn_in"], w["ffn_out"], w["down"], w["down_bias"], w["up"], w["up_bias"],
    )


def dec_mid_back_kernel(
    dsecond0_ref, dsecond1_ref, dcq0_ref, dcq1_ref, wq_ref, n_ref, scale_ref, gain_ref, wo_ref,
    dfirst_ref, datt_ref,
):
    for pair, (dsecond_ref, dcq_ref) in enumerate(
        ((dsecond0_ref, dcq0_ref), (dsecond1_ref, dcq1_ref))
    ):
        rows = slice(pair * TGT, (pair + 1) * TGT)
        gain = gain_ref[0:1]
        total = dsecond_ref[...] + nt(dcq_ref[...], wq_ref[...])
        grad = norm_rows_back(n_ref[rows] / gain, scale_ref[rows, 0:1], total * gain)
        dfirst_ref[rows] = grad
        datt_ref[rows] = nt(grad.astype(BF), wo_ref[...]).astype(BF)


def dec_mid_back(dseconds, dcqs, n, scale, w, cross):
    rows, width = n.shape
    return pl.pallas_call(
        dec_mid_back_kernel,
        out_shape=[
            jax.ShapeDtypeStruct((rows, width), F32),
            jax.ShapeDtypeStruct((rows, width), BF),
        ],
        compiler_params=params(),
        name="dec_mid_back",
    )(*dseconds, *dcqs, cross["query"], n, scale, w["gains"], w["out"])


enc_segs = ((0, SRC_LONG, 0, SRC_LONG), (SRC_LONG, SRC_SHORT, SRC_LONG, SRC_SHORT))
dec_segs = ((0, TGT, 0, TGT), (TGT, TGT, TGT, TGT))
cross_segs = (((0, TGT, 0, SRC_LONG),), ((0, TGT, SRC_LONG % ENC_ROWS, SRC_SHORT),))


def self_columns(qkv):
    rows = qkv.shape[0]
    return (qkv, rows, 0, 0), [(qkv, rows, 0, 8)], [(qkv, rows, 0, 16)]


def cross_columns(cq, kvs, which):
    return (
        (cq, TGT, which, 0),
        [(kv, ENC_ROWS, 0, 0) for kv in kvs],
        [(kv, ENC_ROWS, 0, 8) for kv in kvs],
    )


def decoder_self(t, lengths, w, cross):
    qkv = product(t, w["qkv"])
    att, inv, *weights = attend(lengths, *self_columns(qkv), w["prefix"], dec_segs, True, group=2)
    n, scale, cq = dec_mid(t, att, w, cross)
    return cq, (qkv, att, inv, weights, n, scale)


def cross_forward(lengths, cq, kvs, which):
    return attend(
        lengths, *cross_columns(cq, kvs, which), None, cross_segs[which], False, which, group=2
    )


def cross_backward(cq, kvs, forward, dcatt, which):
    catt, inv, *weights = forward
    return attend_back(
        *cross_columns(cq, kvs, which), None, catt, inv, dcatt, weights, cross_segs[which]
    )


def decoder_self_back(kept, dseconds, dcqs, w, cross):
    qkv, att, inv, weights, n, scale = kept
    dfirst, datt = dec_mid_back(dseconds, dcqs, n, scale, w, cross)
    dq, dk, dv, *dprefix = attend_back(
        *self_columns(qkv), w["prefix"], att, inv, datt, weights, dec_segs
    )
    return back_product([dq, dk, dv], w["qkv"], dfirst)[0], dprefix


def small_shape(devices):
    return 8, 8 * (2 * chunk) // devices


def finish_kernel(
    q_ref, k_ref, v_ref, o_ref, inv_ref, g0_ref, g1_ref, g2_ref, pk_ref, pv_ref, pl_ref, ps_ref,
    dfirst0_ref, dfirst1_ref, dfirst2_ref, wqkv_ref,
    enc_down, enc_downb, enc_up, enc_upb, long_down, long_downb, long_up, long_upb,
    short_down, short_downb, short_up, short_upb, dpk_ref, dpv_ref,
    y0_ref, y1_ref, dt_ref,
    source_ref, y_ref, target_ref, o_sums_ref, o_small_ref,
    dq, dk, dv, small, ups, downs, mine, theirs, half_sum, across_y, y_sum, landed, total, result,
    small_landed, small_total, small_result, dx_low, dx_high, dx_landed, lows, lows_landed,
    load_sems, pair_sems, y_sems, z_sems, gather_sems, share_y_sems, back_sems,
    small_sems, share_sems, cross_sems,
    *, devices,
):
    step = pl.program_id(0)
    pairs = 8
    section = lax.axis_index("section")
    is_encoder = section == 0
    chips = devices // 2
    line = chips // 2
    slices = 16 // line
    rows = 2 * chunk
    half = rows // 2
    size = half // slices
    side = size // 2
    part = side // line
    place = lax.axis_index("dp")
    core, chip = lax.rem(place, 2), place // 2
    bit, at_line = lax.rem(chip, 2), chip // 2
    partner = place + 1 - 2 * core
    beside = place + 2 - 4 * bit
    small_rows, small_cols = small_shape(devices)
    tile = 256
    width = 2 * chunk
    scale = 1.0 / devices

    def aligned(value, unit=16):
        return pl.multiple_of(value, unit)

    def along(distance):
        return (lax.rem(at_line + distance, line) * 2 + bit) * 2 + core

    def remote(source, target, send_sem, recv_sem, other):
        return pltpu.make_async_remote_copy(
            src_ref=source, dst_ref=target, send_sem=send_sem, recv_sem=recv_sem,
            device_id=other, device_id_type=pl.DeviceIdType.MESH,
        )

    def in_group(other):
        return {"dp": other}

    across = {"section": 1 - section}
    kept = aligned(core * half)
    given = aligned((1 - core) * half)

    def swap():
        return remote(
            mine.at[pl.ds(given, half)], theirs, pair_sems.at[0], pair_sems.at[1],
            in_group(partner),
        )

    def y_send(j):
        there = pl.ds(aligned(j * size + (1 - bit) * side), side)
        return remote(
            half_sum.at[there], across_y.at[j], y_sems.at[0, j], y_sems.at[1, j], in_group(beside)
        )

    def z_send(j, s):
        there = pl.ds(aligned(lax.rem(at_line + s, line) * part), part)
        return remote(
            y_sum.at[j].at[there], landed.at[j, s - 1],
            z_sems.at[0, j, s - 1], z_sems.at[1, j, s - 1], in_group(along(s)),
        )

    def own_rows(j):
        return pl.ds(aligned(kept + j * size + bit * side + at_line * part), part)

    def own_side(j):
        return pl.ds(aligned(kept + j * size + bit * side), side)

    def other_side(j):
        return pl.ds(aligned(kept + j * size + (1 - bit) * side), side)

    def gather(j, s):
        return remote(
            total.at[j], result.at[own_rows(j)],
            gather_sems.at[0, j, s - 1], gather_sems.at[1, j, s - 1], in_group(along(s)),
        )

    def y_share(j):
        return remote(
            result.at[own_side(j)], result.at[own_side(j)],
            share_y_sems.at[0, j], share_y_sems.at[1, j], in_group(beside),
        )

    def back(j, i):
        there = own_side(j) if i == 0 else other_side(j)
        return remote(
            result.at[there], result.at[there],
            back_sems.at[0, j, i], back_sems.at[1, j, i], in_group(partner),
        )

    def piece(index):
        row = aligned(lax.rem(index, 8) * small_rows, 8)
        col = aligned((index // 8) * small_cols, LANES)
        return pl.ds(row, small_rows), pl.ds(col, small_cols)

    def small_out(s):
        return remote(
            small.at[piece(lax.rem(place + s, devices))], small_landed.at[s - 1],
            small_sems.at[0, s - 1], small_sems.at[1, s - 1],
            in_group(lax.rem(place + s, devices)),
        )

    def small_share(s):
        return remote(
            small_total, small_result.at[piece(place)],
            share_sems.at[0, s - 1], share_sems.at[1, s - 1],
            in_group(lax.rem(place + s, devices)),
        )

    def send_low():
        return remote(lows, lows_landed, cross_sems.at[0, 0], cross_sems.at[1, 0], across)

    def send_high(i):
        return remote(
            dx_high.at[i], dx_landed.at[i], cross_sems.at[0, 1 + i], cross_sems.at[1, 1 + i], across
        )

    def greet(barrier, other):
        pl.semaphore_signal(
            barrier, inc=1, device_id=other, device_id_type=pl.DeviceIdType.MESH
        )

    def load(source, target, i):
        return pltpu.make_async_copy(source, target, load_sems.at[i])

    @pl.when(step == 0)
    def _():
        barrier = pltpu.get_barrier_semaphore()
        for s in range(1, devices):
            greet(barrier, in_group(lax.rem(place + s, devices)))

        def pack(up, down):
            mine[0:chunk] = (up * scale).astype(BF)
            down = (down * scale).astype(BF)
            mine[chunk:width, 0:chunk] = down[0:chunk]
            mine[chunk:width, chunk:width] = down[chunk:width]

        @pl.when(is_encoder)
        def _():
            loads = [load(enc_up, ups.at[0], 0), load(enc_down, downs.at[0], 1)]
            for copy in loads:
                copy.start()
            for copy in loads:
                copy.wait()
            pack(ups[0], downs[0])
            pl.semaphore_wait(barrier, devices - 1)
            greet(barrier, across)

        @pl.when(jnp.logical_not(is_encoder))
        def _():
            loads = [
                load(long_up, ups.at[0], 0), load(long_down, downs.at[0], 1),
                load(short_up, ups.at[1], 2), load(short_down, downs.at[1], 3),
            ]
            for copy in loads:
                copy.start()
            for copy in loads:
                copy.wait()
            pack(ups[0] + ups[1], downs[0] + downs[1])
            pl.semaphore_wait(barrier, devices)
            greet(barrier, across)

        swap().start()

        @pl.when(jnp.logical_not(is_encoder))
        def _():
            low = width // 2
            lows[0, 0:TGT] = y0_ref[:, 0:low]
            lows[0, TGT : 2 * TGT] = y1_ref[:, 0:low]
            lows[1] = dt_ref[:, 0:low]
            send_low().start()
            small[0:PRE_PAD] = dpk_ref[...] * scale
            small[PRE_PAD : 2 * PRE_PAD] = dpv_ref[...] * scale

        swap().wait()
        half_sum[...] = (
            mine[pl.ds(kept, half)].astype(F32) + theirs[...].astype(F32)
        ).astype(BF)
        for j in range(slices):
            y_send(j).start()

    @pl.when(is_encoder & (step < pairs))
    def _():
        at = aligned(step * LANES, LANES)
        lanes = pl.ds(at, LANES)
        prefix_totals = attend_back_pair(
            q_ref, [k_ref], [v_ref], o_ref, inv_ref, [g0_ref, g1_ref, g2_ref], pk_ref, pv_ref,
            (pl_ref, ps_ref), dq.at[:, lanes], dk.at[:, lanes], dv.at[:, lanes], enc_segs,
        )
        small[0:PRE_PAD, lanes] = prefix_totals[0] * scale
        small[PRE_PAD : 2 * PRE_PAD, lanes] = prefix_totals[1] * scale

    for j in range(slices):

        @pl.when(step == j)
        def _(j=j):
            y_send(j).wait()
            own = pl.ds(aligned(j * size + bit * side), side)
            y_sum[j] = (half_sum[own].astype(F32) + across_y[j].astype(F32)).astype(BF)
            for s in range(1, line):
                z_send(j, s).start()

        @pl.when(step == j + 1)
        def _(j=j):
            summed = y_sum[j, pl.ds(aligned(at_line * part), part)].astype(F32)
            for s in range(1, line):
                z_send(j, s).wait()
                summed = summed + landed[j, s - 1].astype(F32)
            total[j] = summed.astype(BF)
            result[own_rows(j)] = total[j]
            for s in range(1, line):
                gather(j, s).start()

        @pl.when(step == j + 2)
        def _(j=j):
            for s in range(1, line):
                gather(j, s).wait()
            y_share(j).start()
            back(j, 0).start()

        @pl.when(step == j + 3)
        def _(j=j):
            y_share(j).wait()
            back(j, 1).start()

    @pl.when(step == pairs - 1)
    def _():
        @pl.when(is_encoder)
        def _():
            down_row = jnp.concatenate([enc_downb[...], jnp.zeros_like(enc_downb)], 1)
            small[PRE : PRE + 1] = enc_upb[...] * scale
            small[PRE + 1 : PRE + 2] = down_row * scale

        @pl.when(jnp.logical_not(is_encoder))
        def _():
            down_row = long_downb[...] + short_downb[...]
            down_row = jnp.concatenate([down_row, jnp.zeros_like(down_row)], 1)
            small[PRE : PRE + 1] = (long_upb[...] + short_upb[...]) * scale
            small[PRE + 1 : PRE + 2] = down_row * scale

        for s in range(1, devices):
            small_out(s).start()

    @pl.when(is_encoder & (step == pairs))
    def _():
        pl.semaphore_wait(pltpu.get_barrier_semaphore(), 1)

    for i in range(4):

        @pl.when(is_encoder & (step == pairs + i))
        def _(i=i):
            acc = jnp.concatenate([dfirst0_ref[...], dfirst1_ref[...], dfirst2_ref[...]], 0)
            for n, grad in enumerate((dq, dk, dv)):
                acc = acc + nt(grad[...], wqkv_ref[:, n * width : (n + 1) * width])
            if i < 2:
                dx_high[i] = acc.astype(BF)
                send_high(i).start()
            else:
                dx_low[:, (i - 2) * tile : (i - 1) * tile] = acc.astype(BF)

    @pl.when(step == pairs + 1)
    def _():
        own_rows_, own_cols = piece(place)
        summed = small[own_rows_, own_cols]
        for s in range(1, devices):
            small_out(s).wait()
            summed = summed + small_landed[s - 1]
        small_total[...] = summed
        small_result[own_rows_, own_cols] = summed
        for s in range(1, devices):
            small_share(s).start()

    @pl.when(step == pairs + 3)
    def _():
        for j in range(slices):
            for i in range(2):
                back(j, i).wait()
        o_sums_ref[...] = result[...]
        for s in range(1, devices):
            small_share(s).wait()
        o_small_ref[...] = small_result[...]

        @pl.when(is_encoder)
        def _():
            source_ref[...] = dx_low[...]
            send_low().wait_recv()
            y_ref[...] = lows_landed[0]
            target_ref[...] = lows_landed[1]
            for i in range(2):
                send_high(i).wait_send()

        @pl.when(jnp.logical_not(is_encoder))
        def _():
            low = width // 2
            y_ref[0:TGT] = y0_ref[:, low:width]
            y_ref[TGT : 2 * TGT] = y1_ref[:, low:width]
            target_ref[...] = dt_ref[:, low:width]
            send_low().wait_send()
            for i in range(2):
                send_high(i).wait_recv()
                source_ref[:, i * tile : (i + 1) * tile] = dx_landed[i]


def finish(saved, datts, dfirsts, w, adapters, dec_prefix, ys, dt):
    qkv, att, inv, weights = saved
    devices = lax.axis_size("dp")
    line = devices // 4
    slices = 16 // line
    rows, width = att.shape
    targets = dt.shape[0]
    pairs, tile = 8, 256
    half = width // 2
    side = half // slices // 2
    part = side // line
    small_rows, small_cols = small_shape(devices)

    def pair(offset):
        return pl.BlockSpec((rows, LANES), lambda i: (0, jnp.minimum(i, pairs - 1) + offset))

    def at(i):
        return jnp.where(i < pairs + 2, 2 + jnp.maximum(i - pairs, 0), i - pairs - 2)

    def once(shape):
        return pl.BlockSpec(shape, lambda i: (0,) * len(shape), pipeline_mode=pl.Buffered(1))

    anywhere = pl.BlockSpec(memory_space=pl.ANY)
    prefix_pair = pl.BlockSpec((PRE_PAD, LANES), lambda i: (0, jnp.minimum(i, pairs - 1)))
    vmem = pltpu.VMEM
    dma = pltpu.SemaphoreType.DMA
    flat = [a for group in adapters for a in group]
    return pl.pallas_call(
        functools.partial(finish_kernel, devices=devices),
        grid=(pairs + 4,),
        in_specs=[pair(0), pair(8), pair(16), pair(0), pair(0)]
        + [pl.BlockSpec((ENC_ROWS, LANES), lambda i: (0, jnp.minimum(i, pairs - 1)))] * 3
        + [prefix_pair] * 2
        + [
            pl.BlockSpec((2,) + p.shape[1:], lambda i: (jnp.minimum(i, pairs - 1), 0, 0))
            for p in weights
        ]
        + [
            pl.BlockSpec((ENC_ROWS, tile), lambda i: (0, at(i))),
        ]
        * 3
        + [
            pl.BlockSpec((tile, 3 * width), lambda i: (at(i), 0)),
        ]
        + [anywhere if a.shape[0] > 1 else once(a.shape) for a in flat]
        + [once(a.shape) for a in (*dec_prefix, *ys, dt)],
        out_specs=[
            once((rows, half)), once((targets, half)), once((targets, half)), once((width, width)),
            once((2 * PRE_PAD, width)),
        ],
        out_shape=[
            jax.ShapeDtypeStruct((rows, half), BF),
            jax.ShapeDtypeStruct((targets, half), BF),
            jax.ShapeDtypeStruct((targets, half), BF),
            jax.ShapeDtypeStruct((width, width), BF),
            jax.ShapeDtypeStruct((2 * PRE_PAD, width), F32),
        ],
        scratch_shapes=[
            vmem((rows, width), BF), vmem((rows, width), BF), vmem((rows, width), BF),
            vmem((2 * PRE_PAD, width), F32),
            vmem((2, chunk, width), F32), vmem((2, width, chunk), F32),
            vmem((width, width), BF), vmem((half, width), BF), vmem((half, width), BF),
            vmem((slices, side, width), BF), vmem((slices, side, width), BF),
            vmem((slices, line - 1, part, width), BF), vmem((slices, part, width), BF),
            vmem((width, width), BF),
            vmem((devices - 1, small_rows, small_cols), F32), vmem((small_rows, small_cols), F32),
            vmem((2 * PRE_PAD, width), F32),
            vmem((rows, half), BF), vmem((2, rows, tile), BF), vmem((2, rows, tile), BF),
            vmem((2, targets, half), BF), vmem((2, targets, half), BF),
            dma((4,)), dma((2,)), dma((2, slices)), dma((2, slices, line - 1)),
            dma((2, slices, line - 1)), dma((2, slices)), dma((2, slices, 2)),
            dma((2, devices - 1)), dma((2, devices - 1)), dma((2, 3)),
        ],
        compiler_params=pltpu.CompilerParams(
            vmem_limit_bytes=60 * 2**20, collective_id=0, has_side_effects=True
        ),
        name="finish",
    )(
        qkv, qkv, qkv, att, inv, *datts, *w["prefix"], *weights,
        *dfirsts, w["qkv"], *flat, *dec_prefix, *ys, dt,
    )


def blank_kernel(*refs):
    pass


def blanks(shapes):
    return pl.pallas_call(
        blank_kernel,
        out_shape=list(shapes),
        out_specs=[pl.BlockSpec(memory_space=pl.ANY)] * len(shapes),
        name="blank",
    )()


def on_section(is_encoder, encoder_work, decoder_work, *operands):
    enc_shapes, _ = jax.eval_shape(encoder_work, *operands)
    dec_shapes, _ = jax.eval_shape(decoder_work, *operands)

    def blank_like(shapes):
        leaves, tree = jax.tree.flatten(shapes)
        if not leaves:
            return shapes
        return jax.tree.unflatten(tree, blanks(leaves))

    def encoder_branch(*a):
        own, shared = encoder_work(*a)
        return own, blank_like(dec_shapes), shared

    def decoder_branch(*a):
        own, shared = decoder_work(*a)
        return blank_like(enc_shapes), own, shared

    return lax.cond(is_encoder, encoder_branch, decoder_branch, *operands)


def to_decoder(block):
    return lax.ppermute(block, "section", [(0, 1)])


def to_encoder(block):
    return lax.ppermute(block, "section", [(1, 0)])


def per_device(
    sources, targets, cotangent, source_lengths, target_lengths,
    attn_qkv, attn_out, ffn_in, ffn_out, norm_gains, prefix_pairs,
    adapt_down, adapt_down_bias, adapt_up, adapt_up_bias,
    cross_query, cross_pairs, cross_out, cross_gain,
):
    is_encoder = lax.axis_index("section") == 0
    prefix = jnp.pad(prefix_pairs[0], ((0, 0), (0, PRE_PAD - PRE), (0, 0)))
    w = dict(
        qkv=attn_qkv[0], out=attn_out[0], ffn_in=ffn_in[0], ffn_out=ffn_out[0],
        gains=norm_gains[0], prefix=(prefix[0], prefix[1]),
        down=adapt_down[0], down_bias=adapt_down_bias,
        up=adapt_up[0], up_bias=adapt_up_bias,
    )
    cross = dict(query=cross_query, pairs=cross_pairs, out=cross_out, gain=cross_gain[None])

    def at_encoder(work, *operands):
        return on_section(is_encoder, lambda *a: (work(*a), ()), lambda *a: ((), ()), *operands)[0]

    def at_decoder(work, *operands):
        return on_section(is_encoder, lambda *a: ((), ()), lambda *a: (work(*a), ()), *operands)[1]

    def at_both(enc_work, dec_work, *operands):
        return on_section(
            is_encoder, lambda *a: (enc_work(*a), ()), lambda *a: (dec_work(*a), ()), *operands
        )[:2]

    def encoder_start():
        qkv = product(sources, w["qkv"])
        att, inv, *weights = attend(
            source_lengths, *self_columns(qkv), w["prefix"], enc_segs, False
        )
        return (qkv, att, inv, weights), enc_ffn(sources, att, w, 2)

    (saved, part2), (cq, kept) = at_both(
        encoder_start, lambda: decoder_self(targets, target_lengths, w, cross)
    )
    mem2 = to_decoder(part2[0])
    part1 = at_encoder(lambda saved: enc_ffn(sources, saved[1], w, 1), saved)
    mem1 = to_decoder(part1[0])

    def decoder_short(saved, mem2, cq):
        kv2 = product(mem2, cross["pairs"])
        return kv2, cross_forward(source_lengths, cq, [kv2], 1)

    part0, (kv2, short) = at_both(
        lambda saved, mem2, cq: enc_ffn(sources, saved[1], w, 0), decoder_short, saved, mem2, cq
    )
    mem0 = to_decoder(part0[0])
    kv1 = at_decoder(lambda mem1: product(mem1, cross["pairs"]), mem1)

    def decoder_long(mem0, kv1, kv2, cq, kept):
        kvs = [product(mem0, cross["pairs"]), kv1, kv2]
        long = cross_forward(source_lengths, cq, kvs, 0)
        y, dsecond, dcatt, *adapter = dec_ffn(
            target_lengths, kept[4], long[0], cotangent, w, cross, 0
        )
        dcq, dck, dcv = cross_backward(cq, kvs, long, dcatt, 0)
        cuts = ((0, ENC_ROWS), (ENC_ROWS, ENC_ROWS), (2 * ENC_ROWS, SRC_LONG - 2 * ENC_ROWS))
        return back_product([dck, dcv], cross["pairs"], cuts=cuts), y, dsecond, dcq, adapter

    dmems, *long = at_decoder(decoder_long, mem0, kv1, kv2, cq, kept)
    dmem0, dmem1, dmem2 = [to_encoder(block) for block in dmems]

    def decoder_short_back(kv2, cq, kept, short):
        y, dsecond, dcatt, *adapter = dec_ffn(
            target_lengths, kept[4], short[0], cotangent, w, cross, 1
        )
        dcq, dck, dcv = cross_backward(cq, [kv2], short, dcatt, 1)
        return back_product([dck, dcv], cross["pairs"])[0], y, dsecond, dcq, adapter

    dmem_short, *short = at_decoder(decoder_short_back, kv2, cq, kept, short)
    dmem_short = to_encoder(dmem_short)

    def decoder_end(kept, *grads):
        return decoder_self_back(kept, grads[:2], grads[2:], w, cross)

    (long_y, long_second, long_cq, long_adapter) = long
    (short_y, short_second, short_cq, short_adapter) = short
    dt, dec_prefix = at_decoder(
        decoder_end, kept, long_second, short_second, long_cq, short_cq
    )
    dmem0, dt = lax.optimization_barrier((dmem0, dt))
    back0 = at_encoder(lambda dmem0, part0: enc_ffn_back([dmem0], part0, w), dmem0, part0)
    back1 = at_encoder(lambda dmem1, part1: enc_ffn_back([dmem1], part1, w), dmem1, part1)

    def encoder_end(dmem2, dmem_short, part0, part1, part2, back0, back1):
        back2 = enc_ffn_back([dmem2, dmem_short], part2, w)
        parts, backs = (part0, part1, part2), (back0, back1, back2)
        adapter = adapter_grads(
            [p[4] for p in parts], [p[3] for p in parts],
            [b[2] for b in backs], [b[3] for b in backs],
        )
        return back2, adapter

    back2, enc_adapter = at_encoder(
        encoder_end, dmem2, dmem_short, part0, part1, part2, back0, back1
    )
    backs = (back0, back1, back2)
    source_grad, y, target_grad, sums, small = finish(
        saved, [b[1] for b in backs], [b[0] for b in backs], w,
        [enc_adapter, long_adapter, short_adapter], dec_prefix, [long_y, short_y], dt,
    )
    sums = sums.astype(F32)
    return (
        y,
        source_grad,
        target_grad,
        jnp.stack([small[:PRE], small[PRE_PAD : PRE_PAD + PRE]])[None],
        jnp.concatenate([sums[chunk:, :chunk], sums[chunk:, chunk:]], 0)[None],
        small[PRE + 1 : PRE + 2, :chunk],
        sums[None, :chunk],
        small[PRE : PRE + 1],
    )


def solution(mesh):
    layer2, layer3, rows = P("section", None), P("section", None, None), P("dp", None)
    return jax.shard_map(
        per_device,
        mesh=mesh,
        in_specs=(
            rows, rows, rows, rows, rows,
            layer3, layer3, layer3, layer3, layer3,
            P("section", None, None, None),
            layer3, layer2, layer3, layer2,
            P(), P(), P(), P(),
        ),
        out_specs=(
            P("dp", "section"), P("dp", "section"), P("dp", "section"),
            P("section", None, None, None), layer3, layer2, layer3, layer2,
        ),
        check_vma=False,
    )
```

profile of v0, /device:TPU:0, one launch (start us, length us, event | category | flops | bytes accessed | tf_op | source)
XLA Modules:
  0.0 341.6 jit_solution(14989739397056814327)
XLA Ops:
  1.6 51.8 %conditional.10 = (bf16[864,3072]{1,0:T(8,128)(2,1)}, bf16[864,1024]{1,0:T(8,128)(2,1)}, f32[864,1024]{1,0:T(8,128)}, bf16[16,800,768]{2,1,0:T(8,128)(2,1)}, bf1...) conditional(s32[]{:T(128)} %convert_element_type.6, ...), branch_computations={%region_0.1_spmd, %region_1.2_spmd} | conditional | bytes 16834880 | solution.py:1247
  2.0 9.6 %product.6.refs_0_.refs_1_.refs_2_ = bf16[864,3072]{1,0:T(8,128)(2,1)} custom-call(bf16[864,1024]{1,0:T(8,128)(2,1)} %get-tuple-element.321.x_ref, bf16[1024,3072]{1,0:T(8,128)(2,1)} %get-tuple-element.322.w_ref), custom_call_target="tpu_custom_call" | custom-call | tf_op jit(solution)/shard_map/cond/branch_1_fun/product/pallas_call | solution.py:92
  11.7 26.2 %attend.5 = (bf16[864,1024]{1,0:T(8,128)(2,1)}, f32[864,1024]{1,0:T(8,128)}, bf16[16,800,768]{2,1,0:T(8,128)(2,1)}, bf16[16,128,96]{2,1,0:T(8,128)(2,1)}) custom-call(s32[1,2]{1,0:T(1,128)} %get-tuple-element.323.len_ref, bf16[864,3072]{1,0:T(8,128)(2,1)} %product.6.refs_0_.refs_1_.refs_2_, bf16[864,3072]{1,0:T(8,128)(2,1)} %product.6.refs_0_.refs_1_.refs_2_, ...), custom_call_target="tpu_custom_call" | custom-call | tf_op jit(solution)/shard_map/cond/branch_1_fun/attend/pallas_call | solution.py:248
  37.9 15.4 %enc_ffn.3 = (bf16[288,1024]{1,0:T(8,128)(2,1)}, bf16[288,4096]{1,0:T(8,128)(2,1)}, bf16[288,512]{1,0:T(8,128)(2,1)}, bf16[288,512]{1,0:T(8,128)(2,1)}, bf16[288,1024]{1,0:T(8,128)(2,1)}, /*index=5*/f32[288,128]{1,0:T(8,128)}) custom-call(bf16[864,1024]{1,0:T(8,128)(2,1)} %get-tuple-element.321.x_ref, bf16[864,1024]{1,0:T(8,128)(2,1)} %get-tuple-element.741.att_ref, ...), custom_call_target="tpu_custom_call" | custom-call | tf_op jit(solution)/shard_map/cond/branch_1_fun/enc_ffn/pallas_call | solution.py:422
  53.4 2.1 collective-permute-start
  55.5 16.6 %conditional.12 = ((bf16[288,1024]{1,0:T(8,128)(2,1)}, bf16[288,4096]{1,0:T(8,128)(2,1)}, bf16[288,512]{1,0:T(8,128)(2,1)}, bf16[288,512]{1,0:T(8,128)(2,1)}, bf...) conditional(s32[]{:T(128)} %convert_element_type.6, () %tuple.83, (bf16[864,1024]{1,0:T(8,128)(2,1)}, ...), branch_computations={%region_4.5_spmd, %region_5.6_spmd} | conditional | bytes 8 | solution.py:1247
  55.5 16.6 %enc_ffn.5 = (bf16[288,1024]{1,0:T(8,128)(2,1)}, bf16[288,4096]{1,0:T(8,128)(2,1)}, bf16[288,512]{1,0:T(8,128)(2,1)}, bf16[288,512]{1,0:T(8,128)(2,1)}, bf16[288,1024]{1,0:T(8,128)(2,1)}, /*index=5*/f32[288,128]{1,0:T(8,128)}) custom-call(bf16[864,1024]{1,0:T(8,128)(2,1)} %get-tuple-element.385.x_ref, bf16[864,1024]{1,0:T(8,128)(2,1)} %get-tuple-element.386.att_ref, ...), custom_call_target="tpu_custom_call" | custom-call | tf_op jit(solution)/shard_map/cond/branch_1_fun/enc_ffn/pallas_call | solution.py:422
  72.1 2.1 collective-permute-start.2
  74.2 29.6 %conditional.11 = (bf16[288,1024]{1,0:T(8,128)(2,1)}, bf16[288,4096]{1,0:T(8,128)(2,1)}, bf16[288,512]{1,0:T(8,128)(2,1)}, bf16[288,512]{1,0:T(8,128)(2,1)}, bf1...) conditional(s32[]{:T(128)} %convert_element_type.6, ...), branch_computations={%region_2.3_spmd, %region_3.4_spmd} | conditional | bytes 8913032 | solution.py:1247
  87.1 16.7 %enc_ffn.4 = (bf16[288,1024]{1,0:T(8,128)(2,1)}, bf16[288,4096]{1,0:T(8,128)(2,1)}, bf16[288,512]{1,0:T(8,128)(2,1)}, bf16[288,512]{1,0:T(8,128)(2,1)}, bf16[288,1024]{1,0:T(8,128)(2,1)}, /*index=5*/f32[288,128]{1,0:T(8,128)}) custom-call(bf16[864,1024]{1,0:T(8,128)(2,1)} %get-tuple-element.365.x_ref, bf16[864,1024]{1,0:T(8,128)(2,1)} %get-tuple-element.366.att_ref, ...), custom_call_target="tpu_custom_call" | custom-call | tf_op jit(solution)/shard_map/cond/branch_1_fun/enc_ffn/pallas_call | solution.py:422
  103.9 2.1 collective-permute-start.1
  106.0 12.9 %collective-permute-done.1 = bf16[288,1024]{1,0:T(8,128)(2,1)} collective-permute-done((bf16[288,1024]{1,0:T(8,128)(2,1)}, bf16[288,1024]{1,0:T(8,128)(2,1)}, u32[]{:S(2)}, u32[]{:S(2)}) %collective-permute-start.1) | collective-permute-done | bytes 589856 | tf_op jit(solution)/shard_map/ppermute | solution.py:1251
  124.6 2.0 conditional.16
  126.6 72.3 %collective-permute-done.3 = bf16[288,1024]{1,0:T(8,128)(2,1)} collective-permute-done((bf16[288,1024]{1,0:T(8,128)(2,1)}, bf16[288,1024]{1,0:T(8,128)(2,1)}, u32[]{:S(2)}, u32[]{:S(2)}) %collective-permute-start.3) | collective-permute-done | bytes 589856 | tf_op jit(solution)/shard_map/ppermute | solution.py:1255
  198.9 15.9 %conditional.17 = ((f32[288,1024]{1,0:T(8,128)}, bf16[288,1024]{1,0:T(8,128)(2,1)}, bf16[288,1024]{1,0:T(8,128)(2,1)}, bf16[288,512]{1,0:T(8,128)(2,1)})) conditional(s32[]{:T(128)} %convert_element_type.6, () %tuple.80, (bf16[288,1024]{1,0:T(8,128)(2,1)}, bf16[288,1024]{1,0:T(8,128)(2,1)}, bf16[288,1024]{1,0:T(8,128)(2,1)}, ...), branch_computations={%region_14.15_spmd, %region_15.16_spmd} | conditional | bytes 8 | solution.py:1247
  198.9 15.9 %enc_ffn_back.3 = (f32[288,1024]{1,0:T(8,128)}, bf16[288,1024]{1,0:T(8,128)(2,1)}, bf16[288,1024]{1,0:T(8,128)(2,1)}, bf16[288,512]{1,0:T(8,128)(2,1)}) custom-call(bf16[288,1024]{1,0:T(8,128)(2,1)} %get-tuple-element.483.refs_0_, bf16[288,1024]{1,0:T(8,128)(2,1)} %get-tuple-element.484.refs_1_, bf16[288,1024]{1,0:T(8,128)(2,1)} %get-tuple-element.485.refs_2_, ...), custom_call_target="tpu_custom_call" | custom-call | tf_op jit(solution)/shard_map/cond/branch_1_fun/enc_ffn_back/pallas_call | solution.py:529
  214.9 15.6 %conditional.18 = ((f32[288,1024]{1,0:T(8,128)}, bf16[288,1024]{1,0:T(8,128)(2,1)}, bf16[288,1024]{1,0:T(8,128)(2,1)}, bf16[288,512]{1,0:T(8,128)(2,1)})) conditional(s32[]{:T(128)} %convert_element_type.6, () %tuple.94, (bf16[288,1024]{1,0:T(8,128)(2,1)}, bf16[288,1024]{1,0:T(8,128)(2,1)S(1)}, bf16[288,1024]{1,0:T(8,128)(2,1)S(1)}, ...), branch_computations={%region_16.17_spmd, %region_17.18_spmd} | conditional | bytes 8 | solution.py:1247
  215.1 15.3 %enc_ffn_back.4 = (f32[288,1024]{1,0:T(8,128)}, bf16[288,1024]{1,0:T(8,128)(2,1)}, bf16[288,1024]{1,0:T(8,128)(2,1)}, bf16[288,512]{1,0:T(8,128)(2,1)}) custom-call(bf16[288,1024]{1,0:T(8,128)(2,1)} %get-tuple-element.495.refs_0_, bf16[288,1024]{1,0:T(8,128)(2,1)S(1)} %get-tuple-element.496.refs_1_, bf16[288,1024]{1,0:T(8,128)(2,1)S(1)} %get-tuple-element.497.refs_2_, ...), custom_call_target="tpu_custom_call" | custom-call | tf_op jit(solution)/shard_map/cond/branch_1_fun/enc_ffn_back/pallas_call | solution.py:529
  230.5 2.7 collective-permute-done.6
  233.2 21.5 %conditional.19 = (f32[288,1024]{1,0:T(8,128)}, bf16[288,1024]{1,0:T(8,128)(2,1)}, f32[1024,512]{1,0:T(8,128)}, f32[1,512]{1,0:T(1,128)S(1)}, f32[512,1024]{1,0:T(8,128)}, /*index=5*/f32[1,1024]{1,0:T(1,128)S(1)}) conditional(s32[]{:T(128)} %convert_element_type.6, () %tuple.96, (bf16[192,1024]{1,0:T(8,128)(2,1)}, bf16[96,1024]{1,0:T(8,128)(2,1)}, ...), branch_computations={%region_18.19_spmd, %region_19.20_spmd} | conditional | bytes 16515372 | solution.py:1247
  233.4 15.9 %enc_ffn_back.5 = (f32[288,1024]{1,0:T(8,128)}, bf16[288,1024]{1,0:T(8,128)(2,1)}, bf16[288,1024]{1,0:T(8,128)(2,1)}, bf16[288,512]{1,0:T(8,128)(2,1)}) custom-call(bf16[192,1024]{1,0:T(8,128)(2,1)} %get-tuple-element.513.refs_0_, bf16[96,1024]{1,0:T(8,128)(2,1)} %get-tuple-element.514.refs_1_, bf16[288,1024]{1,0:T(8,128)(2,1)} %get-tuple-element.515.refs_2_, ...), custom_call_target="tpu_custom_call" | custom-call | tf_op jit(solution)/shard_map/cond/branch_1_fun/enc_ffn_back/pallas_call | solution.py:529
  249.4 5.2 %adapter_grads.1 = (f32[1024,512]{1,0:T(8,128)}, f32[1,512]{1,0:T(1,128)S(1)}, f32[512,1024]{1,0:T(8,128)}, f32[1,1024]{1,0:T(1,128)S(1)}) custom-call(bf16[288,1024]{1,0:T(8,128)(2,1)S(1)} %copy-done.18, bf16[288,1024]{1,0:T(8,128)(2,1)S(1)} %copy-done.20, bf16[288,1024]{1,0:T(8,128)(2,1)S(1)} %copy-done.17, bf16[288,512]{1,0:T(8,128)(2,1)S(1)} %copy-done.32, ...), custom_call_target="tpu_custom_call" | custom-call | tf_op jit(solution)/shard_map/cond/branch_1_fun/adapter_grads/pallas_call | solution.py:579
  254.8 74.1 %finish.1 = (bf16[864,512]{1,0:T(8,128)(2,1)}, bf16[512,512]{1,0:T(8,128)(2,1)}, bf16[512,512]{1,0:T(8,128)(2,1)}, bf16[1024,1024]{1,0:T(8,128)(2,1)}, f32[64,1024]{1,0:T(8,128)}) custom-call(bf16[864,3072]{1,0:T(8,128)(2,1)} %get-tuple-element.628.q_ref.k_ref.v_ref, bf16[864,3072]{1,0:T(8,128)(2,1)} %get-tuple-element.628.q_ref.k_ref.v_ref, ...), custom_call_target="tpu_custom_call" | custom-call | tf_op jit(solution)/shard_map/finish/pallas_call | solution.py:1160
  332.6 1.5 fusion.2
  (98 shorter events, 17.5 us)
Async XLA Ops:
  11.6 26.3 %copy-start.1 = (bf16[1024,1024]{1,0:T(8,128)(2,1)S(1)}, bf16[1024,1024]{1,0:T(8,128)(2,1)}, u32[]{:S(2)}) copy-start(bf16[1024,1024]{1,0:T(8,128)(2,1)} %get-tuple-element.330.wo_ref) | copy-start | bytes 6291460 | tf_op jit(solution)/shard_map/cond
  11.6 26.3 %copy-start.6 = (bf16[1024,512]{1,0:T(8,128)(2,1)S(1)}, bf16[1024,512]{1,0:T(8,128)(2,1)}, u32[]{:S(2)}) copy-start(bf16[1024,512]{1,0:T(8,128)(2,1)} %get-tuple-element.334.down_ref) | copy-start | bytes 3145732 | tf_op jit(solution)/shard_map/cond
  11.6 26.3 %copy-start.8 = (bf16[512,1024]{1,0:T(8,128)(2,1)S(1)}, bf16[512,1024]{1,0:T(8,128)(2,1)}, u32[]{:S(2)}) copy-start(bf16[512,1024]{1,0:T(8,128)(2,1)} %get-tuple-element.336.up_ref) | copy-start | bytes 3145732 | tf_op jit(solution)/shard_map/cond
  11.6 26.3 %copy-start.25 = (f32[2,1024]{1,0:T(2,128)S(1)}, f32[2,1024]{1,0:T(2,128)}, u32[]{:S(2)}) copy-start(f32[2,1024]{1,0:T(2,128)} %get-tuple-element.331.gain_ref) | copy-start | bytes 24580 | tf_op jit(solution)/shard_map/cond
  11.6 26.3 %copy-start.40 = (f32[1,1024]{1,0:T(1,128)S(1)}, f32[1,1024]{1,0:T(1,128)}, u32[]{:S(2)}) copy-start(f32[1,1024]{1,0:T(1,128)} %get-tuple-element.337.upb_ref) | copy-start | bytes 12292 | tf_op jit(solution)/shard_map/cond
  11.6 26.3 %copy-start.42 = (f32[1,512]{1,0:T(1,128)S(1)}, f32[1,512]{1,0:T(1,128)}, u32[]{:S(2)}) copy-start(f32[1,512]{1,0:T(1,128)} %get-tuple-element.335.downb_ref) | copy-start | bytes 6148 | tf_op jit(solution)/shard_map/cond
  53.4 20.9 %collective-permute-start = (bf16[288,1024]{1,0:T(8,128)(2,1)}, bf16[288,1024]{1,0:T(8,128)(2,1)}, u32[]{:S(2)}, u32[]{:S(2)}) collective-permute-start(bf16[288,1024]{1,0:T(8,128)(2,1)} %get-tuple-element.631), channel_id=1, source_target_pairs={{0,16},{1,17},{2,18},{3,19},{4,20},{5,21},{6,22},{7,23},{8,24},{9,... | collective-permute-start | bytes 1769480 | tf_op jit(solution)/shard_map/ppermute | solution.py:1251
  55.5 18.8 %copy-start.46 = (s32[1,2]{1,0:T(1,128)S(1)}, s32[1,2]{1,0:T(1,128)}, u32[]{:S(2)}) copy-start(s32[1,2]{1,0:T(1,128)} %param.42) | copy-start | bytes 28
  72.1 33.9 %collective-permute-start.2 = (bf16[288,1024]{1,0:T(8,128)(2,1)}, bf16[288,1024]{1,0:T(8,128)(2,1)}, u32[]{:S(2)}, u32[]{:S(2)}) collective-permute-start(bf16[288,1024]{1,0:T(8,128)(2,1)} %get-tuple-element.634), channel_id=1, source_target_pairs={{0,16},{1,17},{2,18},{3,19},{4,20},{5,21},{6,22},{7,23},{8,24},{9,... | collective-permute-start | bytes 1769480 | tf_op jit(solution)/shard_map/ppermute | solution.py:1251
  103.9 15.1 %collective-permute-start.1 = (bf16[288,1024]{1,0:T(8,128)(2,1)}, bf16[288,1024]{1,0:T(8,128)(2,1)}, u32[]{:S(2)}, u32[]{:S(2)}) collective-permute-start(bf16[288,1024]{1,0:T(8,128)(2,1)} %get-tuple-element.633), channel_id=1, source_target_pairs={{0,16},{1,17},{2,18},{3,19},{4,20},{5,21},{6,22},{7,23},{8,24},{9,... | collective-permute-start | bytes 1769480 | tf_op jit(solution)/shard_map/ppermute | solution.py:1251
  119.3 79.6 %collective-permute-start.3 = (bf16[288,1024]{1,0:T(8,128)(2,1)}, bf16[288,1024]{1,0:T(8,128)(2,1)}, u32[]{:S(2)}, u32[]{:S(2)}) collective-permute-start(bf16[288,1024]{1,0:T(8,128)(2,1)} %get-tuple-element.637), channel_id=1, source_target_pairs={{16,0},{17,1},{18,2},{19,3},{20,4},{21,5},{22,6},{23,7},{24,8},{25... | collective-permute-start | bytes 1769480 | tf_op jit(solution)/shard_map/ppermute | solution.py:1255
  120.6 94.2 %collective-permute-start.4 = (bf16[288,1024]{1,0:T(8,128)(2,1)}, bf16[288,1024]{1,0:T(8,128)(2,1)}, u32[]{:S(2)}, u32[]{:S(2)}) collective-permute-start(bf16[288,1024]{1,0:T(8,128)(2,1)} %get-tuple-element.658), channel_id=1, source_target_pairs={{16,0},{17,1},{18,2},{19,3},{20,4},{21,5},{22,6},{23,7},{24,8},{25... | collective-permute-start | bytes 1769480 | tf_op jit(solution)/shard_map/ppermute | solution.py:1255
  121.9 111.2 %collective-permute-start.5 = (bf16[192,1024]{1,0:T(8,128)(2,1)}, bf16[192,1024]{1,0:T(8,128)(2,1)}, u32[]{:S(2)}, u32[]{:S(2)}) collective-permute-start(bf16[192,1024]{1,0:T(8,128)(2,1)} %get-tuple-element.664), channel_id=1, source_target_pairs={{16,0},{17,1},{18,2},{19,3},{20,4},{21,5},{22,6},{23,7},{24,8},{25... | collective-permute-start | bytes 1179656 | tf_op jit(solution)/shard_map/ppermute | solution.py:1255
  123.3 109.9 %collective-permute-start.6 = (bf16[96,1024]{1,0:T(8,128)(2,1)}, bf16[96,1024]{1,0:T(8,128)(2,1)}, u32[]{:S(2)}, u32[]{:S(2)}) collective-permute-start(bf16[96,1024]{1,0:T(8,128)(2,1)} %get-tuple-element.665), channel_id=1, source_target_pairs={{16,0},{17,1},{18,2},{19,3},{20,4},{21,5},{22,6},{23,7},{24,8},{25... | collective-permute-start | bytes 589832 | tf_op jit(solution)/shard_map/ppermute | solution.py:1255
  214.9 18.3 %copy-start.31 = (bf16[288,512]{1,0:T(8,128)(2,1)S(1)}, bf16[288,512]{1,0:T(8,128)(2,1)}, u32[]{:S(2)}) copy-start(bf16[288,512]{1,0:T(8,128)(2,1)} %get-tuple-element.672) | copy-start | bytes 884740
  214.9 18.3 %copy-start.37 = (f32[288,128]{1,0:T(8,128)S(1)}, f32[288,128]{1,0:T(8,128)}, u32[]{:S(2)}) copy-start(f32[288,128]{1,0:T(8,128)} %get-tuple-element.667) | copy-start | bytes 442372
  233.2 21.6 %copy-start.11 = (bf16[864,1024]{1,0:T(8,128)(2,1)S(1)}, bf16[864,1024]{1,0:T(8,128)(2,1)}, u32[]{:S(2)}) copy-start(bf16[864,1024]{1,0:T(8,128)(2,1)} %get-tuple-element.629.o_ref) | copy-start | bytes 5308420
  233.2 21.6 %copy-start.48 = (f32[1,1024]{1,0:T(1,128)S(1)}, f32[1,1024]{1,0:T(1,128)}, u32[]{:S(2)}) copy-start(f32[1,1024]{1,0:T(1,128)} %get-tuple-element.690.long_upb) | copy-start | bytes 12292
  233.2 21.6 %copy-start.49 = (f32[1,1024]{1,0:T(1,128)S(1)}, f32[1,1024]{1,0:T(1,128)}, u32[]{:S(2)}) copy-start(f32[1,1024]{1,0:T(1,128)} %get-tuple-element.694.short_upb) | copy-start | bytes 12292
  233.2 21.6 %copy-start.50 = (f32[1,512]{1,0:T(1,128)S(1)}, f32[1,512]{1,0:T(1,128)}, u32[]{:S(2)}) copy-start(f32[1,512]{1,0:T(1,128)} %get-tuple-element.688.long_downb) | copy-start | bytes 6148
  233.2 21.6 %copy-start.51 = (f32[1,512]{1,0:T(1,128)S(1)}, f32[1,512]{1,0:T(1,128)}, u32[]{:S(2)}) copy-start(f32[1,512]{1,0:T(1,128)} %get-tuple-element.692.short_downb) | copy-start | bytes 6148
  233.3 16.0 %copy-start.17 = (bf16[288,1024]{1,0:T(8,128)(2,1)S(1)}, bf16[288,1024]{1,0:T(8,128)(2,1)}, u32[]{:S(2)}) copy-start(bf16[288,1024]{1,0:T(8,128)(2,1)} %get-tuple-element.516.refs_3_.refs_2_) | copy-start | bytes 1769476 | tf_op jit(solution)/shard_map/cond
  233.3 16.0 %copy-start.18 = (bf16[288,1024]{1,0:T(8,128)(2,1)S(1)}, bf16[288,1024]{1,0:T(8,128)(2,1)}, u32[]{:S(2)}) copy-start(bf16[288,1024]{1,0:T(8,128)(2,1)} %get-tuple-element.528.refs_0_) | copy-start | bytes 1769476 | tf_op jit(solution)/shard_map/cond
  233.3 16.0 %copy-start.20 = (bf16[288,1024]{1,0:T(8,128)(2,1)S(1)}, bf16[288,1024]{1,0:T(8,128)(2,1)}, u32[]{:S(2)}) copy-start(bf16[288,1024]{1,0:T(8,128)(2,1)} %get-tuple-element.529.refs_1_) | copy-start | bytes 1769476 | tf_op jit(solution)/shard_map/cond
  (17 other events, 206.2 us)
where the time goes:
time: 344 us; the launch traced here: 342 us
  Pallas kernels  211 us (61%)
  waiting for transfers between devices  88 us (26%)
  loops' own time  16.4 us (5%)
  starting transfers between devices  11.5 us (3%)
  local copies, waits for them, and re-layouts  11.4 us (3%)
    ppermute x4, waiting for transfers between devices, to_encoder(): return lax.ppermute(block, 'section', [(1, 0)])  75.1 us
    pallas_call x1, Pallas kernels, finish(): pl.pallas_call(functools.partial(finish_kernel, devices=devices), grid=(p...  74.1 us
    pallas_call x3, Pallas kernels, enc_ffn(): pl.pallas_call(enc_ffn_kernel, grid=(steps + 2,), in_specs=[pl.BlockSpec(...  48.8 us
    pallas_call x3, Pallas kernels, enc_ffn_back(): pl.pallas_call(functools.partial(enc_ffn_back_kernel, pieces=len(dmems)),...  47.2 us
    pallas_call x1, Pallas kernels, attend(): pl.pallas_call(functools.partial(attend_kernel, group=group, segs=segs, p...  26.2 us
    another operation x10, loops' own time, on_section(): return lax.cond(is_encoder, encoder_branch, decoder_branch, *operands)  16.4 us
    ppermute x3, waiting for transfers between devices, to_decoder(): return lax.ppermute(block, 'section', [(0, 1)])  12.9 us
    pallas_call x1, Pallas kernels, product(): pl.pallas_call(product_kernel, grid=(width // tile,), in_specs=[whole((ro...  9.62 us
  transfers between devices with their start and end apart: 7, of which 3 were waited for; matrix products, arithmetic and copies ran while one was open for 0% of the time, Pallas kernels for 19%

commit v1 on v0

--- a/solution.py
+++ b/solution.py
@@ -822,7 +822,7 @@
     enc_down, enc_downb, enc_up, enc_upb, long_down, long_downb, long_up, long_upb,
     short_down, short_downb, short_up, short_upb, dpk_ref, dpv_ref,
     y0_ref, y1_ref, dt_ref,
-    source_ref, y_ref, target_ref, o_sums_ref, o_small_ref,
+    source_ref, y_ref, target_ref, o_up_ref, o_down_ref, o_small_ref,
     dq, dk, dv, small, ups, downs, mine, theirs, half_sum, across_y, y_sum, landed, total, result,
     small_landed, small_total, small_result, dx_low, dx_high, dx_landed, lows, lows_landed,
     load_sems, pair_sems, y_sems, z_sems, gather_sems, share_y_sems, back_sems,
@@ -952,11 +952,42 @@
     def load(source, target, i):
         return pltpu.make_async_copy(source, target, load_sems.at[i])
 
+    enc_loads = [load(enc_up, ups.at[0], 0), load(enc_down, downs.at[0], 1)]
+    dec_loads = [
+        load(long_up, ups.at[0], 0), load(long_down, downs.at[0], 1),
+        load(short_up, ups.at[1], 2), load(short_down, downs.at[1], 3),
+    ]
+
     @pl.when(step == 0)
     def _():
         barrier = pltpu.get_barrier_semaphore()
         for s in range(1, devices):
             greet(barrier, in_group(lax.rem(place + s, devices)))
+
+        @pl.when(is_encoder)
+        def _():
+            for copy in enc_loads:
+                copy.start()
+
+        @pl.when(jnp.logical_not(is_encoder))
+        def _():
+            for copy in dec_loads:
+                copy.start()
+
+    @pl.when(is_encoder & (step < pairs))
+    def _():
+        at = aligned(step * LANES, LANES)
+        lanes = pl.ds(at, LANES)
+        prefix_totals = attend_back_pair(
+            q_ref, [k_ref], [v_ref], o_ref, inv_ref, [g0_ref, g1_ref, g2_ref], pk_ref, pv_ref,
+            (pl_ref, ps_ref), dq.at[:, lanes], dk.at[:, lanes], dv.at[:, lanes], enc_segs,
+        )
+        small[0:PRE_PAD, lanes] = prefix_totals[0] * scale
+        small[PRE_PAD : 2 * PRE_PAD, lanes] = prefix_totals[1] * scale
+
+    @pl.when(step == 0)
+    def _():
+        barrier = pltpu.get_barrier_semaphore()
 
         def pack(up, down):
             mine[0:chunk] = (up * scale).astype(BF)
@@ -966,10 +997,7 @@
 
         @pl.when(is_encoder)
         def _():
-            loads = [load(enc_up, ups.at[0], 0), load(enc_down, downs.at[0], 1)]
-            for copy in loads:
-                copy.start()
-            for copy in loads:
+            for copy in enc_loads:
                 copy.wait()
             pack(ups[0], downs[0])
             pl.semaphore_wait(barrier, devices - 1)
@@ -977,13 +1005,7 @@
 
         @pl.when(jnp.logical_not(is_encoder))
         def _():
-            loads = [
-                load(long_up, ups.at[0], 0), load(long_down, downs.at[0], 1),
-                load(short_up, ups.at[1], 2), load(short_down, downs.at[1], 3),
-            ]
-            for copy in loads:
-                copy.start()
-            for copy in loads:
+            for copy in dec_loads:
                 copy.wait()
             pack(ups[0] + ups[1], downs[0] + downs[1])
             pl.semaphore_wait(barrier, devices)
@@ -1001,35 +1023,28 @@
             small[0:PRE_PAD] = dpk_ref[...] * scale
             small[PRE_PAD : 2 * PRE_PAD] = dpv_ref[...] * scale
 
+    @pl.when(step == 1)
+    def _():
         swap().wait()
         half_sum[...] = (
             mine[pl.ds(kept, half)].astype(F32) + theirs[...].astype(F32)
         ).astype(BF)
-        for j in range(slices):
+        for j in range(min(2, slices)):
             y_send(j).start()
 
-    @pl.when(is_encoder & (step < pairs))
-    def _():
-        at = aligned(step * LANES, LANES)
-        lanes = pl.ds(at, LANES)
-        prefix_totals = attend_back_pair(
-            q_ref, [k_ref], [v_ref], o_ref, inv_ref, [g0_ref, g1_ref, g2_ref], pk_ref, pv_ref,
-            (pl_ref, ps_ref), dq.at[:, lanes], dk.at[:, lanes], dv.at[:, lanes], enc_segs,
-        )
-        small[0:PRE_PAD, lanes] = prefix_totals[0] * scale
-        small[PRE_PAD : 2 * PRE_PAD, lanes] = prefix_totals[1] * scale
-
     for j in range(slices):
 
-        @pl.when(step == j)
+        @pl.when(step == 2 + j)
         def _(j=j):
             y_send(j).wait()
+            if j + 2 < slices:
+                y_send(j + 2).start()
             own = pl.ds(aligned(j * size + bit * side), side)
             y_sum[j] = (half_sum[own].astype(F32) + across_y[j].astype(F32)).astype(BF)
             for s in range(1, line):
                 z_send(j, s).start()
 
-        @pl.when(step == j + 1)
+        @pl.when(step == 4 + j)
         def _(j=j):
             summed = y_sum[j, pl.ds(aligned(at_line * part), part)].astype(F32)
             for s in range(1, line):
@@ -1040,14 +1055,14 @@
             for s in range(1, line):
                 gather(j, s).start()
 
-        @pl.when(step == j + 2)
+        @pl.when(step == 6 + j)
         def _(j=j):
             for s in range(1, line):
                 gather(j, s).wait()
             y_share(j).start()
             back(j, 0).start()
 
-        @pl.when(step == j + 3)
+        @pl.when(step == 8 + j)
         def _(j=j):
             y_share(j).wait()
             back(j, 1).start()
@@ -1104,7 +1119,9 @@
         for j in range(slices):
             for i in range(2):
                 back(j, i).wait()
-        o_sums_ref[...] = result[...]
+        o_up_ref[...] = result[0:chunk]
+        o_down_ref[0:chunk] = result[chunk:width, 0:chunk]
+        o_down_ref[chunk:width] = result[chunk:width, chunk:width]
         for s in range(1, devices):
             small_share(s).wait()
         o_small_ref[...] = small_result[...]
@@ -1143,17 +1160,23 @@
     part = side // line
     small_rows, small_cols = small_shape(devices)
 
+    def mine(value):
+        return jnp.where(lax.axis_index("section") == 0, value, 0)
+
+    def head(i):
+        return mine(jnp.minimum(i, pairs - 1))
+
     def pair(offset):
-        return pl.BlockSpec((rows, LANES), lambda i: (0, jnp.minimum(i, pairs - 1) + offset))
+        return pl.BlockSpec((rows, LANES), lambda i: (0, head(i) + offset))
 
     def at(i):
-        return jnp.where(i < pairs + 2, 2 + jnp.maximum(i - pairs, 0), i - pairs - 2)
+        return mine(jnp.where(i < pairs + 2, 2 + jnp.maximum(i - pairs, 0), i - pairs - 2))
 
     def once(shape):
         return pl.BlockSpec(shape, lambda i: (0,) * len(shape), pipeline_mode=pl.Buffered(1))
 
     anywhere = pl.BlockSpec(memory_space=pl.ANY)
-    prefix_pair = pl.BlockSpec((PRE_PAD, LANES), lambda i: (0, jnp.minimum(i, pairs - 1)))
+    prefix_pair = pl.BlockSpec((PRE_PAD, LANES), lambda i: (0, head(i)))
     vmem = pltpu.VMEM
     dma = pltpu.SemaphoreType.DMA
     flat = [a for group in adapters for a in group]
@@ -1161,10 +1184,10 @@
         functools.partial(finish_kernel, devices=devices),
         grid=(pairs + 4,),
         in_specs=[pair(0), pair(8), pair(16), pair(0), pair(0)]
-        + [pl.BlockSpec((ENC_ROWS, LANES), lambda i: (0, jnp.minimum(i, pairs - 1)))] * 3
+        + [pl.BlockSpec((ENC_ROWS, LANES), lambda i: (0, head(i)))] * 3
         + [prefix_pair] * 2
         + [
-            pl.BlockSpec((2,) + p.shape[1:], lambda i: (jnp.minimum(i, pairs - 1), 0, 0))
+            pl.BlockSpec((2,) + p.shape[1:], lambda i: (head(i), 0, 0))
             for p in weights
         ]
         + [
@@ -1177,14 +1200,16 @@
         + [anywhere if a.shape[0] > 1 else once(a.shape) for a in flat]
         + [once(a.shape) for a in (*dec_prefix, *ys, dt)],
         out_specs=[
-            once((rows, half)), once((targets, half)), once((targets, half)), once((width, width)),
+            once((rows, half)), once((targets, half)), once((targets, half)),
+            once((chunk, width)), once((width, chunk)),
             once((2 * PRE_PAD, width)),
         ],
         out_shape=[
             jax.ShapeDtypeStruct((rows, half), BF),
             jax.ShapeDtypeStruct((targets, half), BF),
             jax.ShapeDtypeStruct((targets, half), BF),
-            jax.ShapeDtypeStruct((width, width), BF),
+            jax.ShapeDtypeStruct((chunk, width), BF),
+            jax.ShapeDtypeStruct((width, chunk), BF),
             jax.ShapeDtypeStruct((2 * PRE_PAD, width), F32),
         ],
         scratch_shapes=[
@@ -1354,19 +1379,18 @@
         encoder_end, dmem2, dmem_short, part0, part1, part2, back0, back1
     )
     backs = (back0, back1, back2)
-    source_grad, y, target_grad, sums, small = finish(
+    source_grad, y, target_grad, up, down, small = finish(
         saved, [b[1] for b in backs], [b[0] for b in backs], w,
         [enc_adapter, long_adapter, short_adapter], dec_prefix, [long_y, short_y], dt,
     )
-    sums = sums.astype(F32)
     return (
         y,
         source_grad,
         target_grad,
         jnp.stack([small[:PRE], small[PRE_PAD : PRE_PAD + PRE]])[None],
-        jnp.concatenate([sums[chunk:, :chunk], sums[chunk:, chunk:]], 0)[None],
+        down.astype(F32)[None],
         small[PRE + 1 : PRE + 2, :chunk],
-        sums[None, :chunk],
+        up.astype(F32)[None],
         small[PRE : PRE + 1],
     )
 

time: 344 us -> 332 us (0.965)
  Pallas kernels: 211 us -> 200 us
    pallas_call x1, Pallas kernels: 74.1 us -> 62.8 us  [finish(): pl.pallas_call(functools.partial(finish_kernel, devices=devices), grid=(p...]
  transfers between devices with their start and end apart: 7 -> 7, of which waited for: 3 -> 3; matrix products, arithmetic and copies ran while one was open for 0% -> 0% of each run, Pallas kernels for 19% -> 20%
where the time goes in v1:
time: 332 us; the launch traced here: 328 us
  Pallas kernels  200 us (60%)
  waiting for transfers between devices  88 us (27%)
  loops' own time  16.4 us (5%)
  starting transfers between devices  11.5 us (3%)
  local copies, waits for them, and re-layouts  8.2 us (2%)
    ppermute x4, waiting for transfers between devices, to_encoder(): return lax.ppermute(block, 'section', [(1, 0)])  75.1 us
    pallas_call x1, Pallas kernels, finish(): pl.pallas_call(functools.partial(finish_kernel, devices=devices), grid=(p...  62.8 us
    pallas_call x3, Pallas kernels, enc_ffn(): pl.pallas_call(enc_ffn_kernel, grid=(steps + 2,), in_specs=[pl.BlockSpec(...  48.8 us
    pallas_call x3, Pallas kernels, enc_ffn_back(): pl.pallas_call(functools.partial(enc_ffn_back_kernel, pieces=len(dmems)),...  47.2 us
    pallas_call x1, Pallas kernels, attend(): pl.pallas_call(functools.partial(attend_kernel, group=group, segs=segs, p...  26.2 us
    another operation x10, loops' own time, on_section(): return lax.cond(is_encoder, encoder_branch, decoder_branch, *operands)  16.4 us
    ppermute x3, waiting for transfers between devices, to_decoder(): return lax.ppermute(block, 'section', [(0, 1)])  12.9 us
    pallas_call x1, Pallas kernels, product(): pl.pallas_call(product_kernel, grid=(width // tile,), in_specs=[whole((ro...  9.62 us
  transfers between devices with their start and end apart: 7, of which 3 were waited for; matrix products, arithmetic and copies ran while one was open for 0% of the time, Pallas kernels for 20%

profile of v1, /device:TPU:0, one launch (start us, length us, event | category | flops | bytes accessed | tf_op | source)
XLA Modules:
  0.0 328.2 jit_solution(803888004179850974)
XLA Ops:
  1.6 51.8 %conditional.10 = (bf16[864,3072]{1,0:T(8,128)(2,1)}, bf16[864,1024]{1,0:T(8,128)(2,1)}, f32[864,1024]{1,0:T(8,128)}, bf16[16,800,768]{2,1,0:T(8,128)(2,1)}, bf1...) conditional(s32[]{:T(128)} %convert_element_type.4, ...), branch_computations={%region_0.1_spmd, %region_1.2_spmd} | conditional | bytes 16834880 | solution.py:1272
  2.0 9.6 %product.6.refs_0_.refs_1_.refs_2_ = bf16[864,3072]{1,0:T(8,128)(2,1)} custom-call(bf16[864,1024]{1,0:T(8,128)(2,1)} %get-tuple-element.321.x_ref, bf16[1024,3072]{1,0:T(8,128)(2,1)} %get-tuple-element.322.w_ref), custom_call_target="tpu_custom_call" | custom-call | tf_op jit(solution)/shard_map/cond/branch_1_fun/product/pallas_call | solution.py:92
  11.7 26.2 %attend.5 = (bf16[864,1024]{1,0:T(8,128)(2,1)}, f32[864,1024]{1,0:T(8,128)}, bf16[16,800,768]{2,1,0:T(8,128)(2,1)}, bf16[16,128,96]{2,1,0:T(8,128)(2,1)}) custom-call(s32[1,2]{1,0:T(1,128)} %get-tuple-element.323.len_ref, bf16[864,3072]{1,0:T(8,128)(2,1)} %product.6.refs_0_.refs_1_.refs_2_, bf16[864,3072]{1,0:T(8,128)(2,1)} %product.6.refs_0_.refs_1_.refs_2_, ...), custom_call_target="tpu_custom_call" | custom-call | tf_op jit(solution)/shard_map/cond/branch_1_fun/attend/pallas_call | solution.py:248
  37.9 15.4 %enc_ffn.3 = (bf16[288,1024]{1,0:T(8,128)(2,1)}, bf16[288,4096]{1,0:T(8,128)(2,1)}, bf16[288,512]{1,0:T(8,128)(2,1)}, bf16[288,512]{1,0:T(8,128)(2,1)}, bf16[288,1024]{1,0:T(8,128)(2,1)}, /*index=5*/f32[288,128]{1,0:T(8,128)}) custom-call(bf16[864,1024]{1,0:T(8,128)(2,1)} %get-tuple-element.321.x_ref, bf16[864,1024]{1,0:T(8,128)(2,1)} %get-tuple-element.741.att_ref, ...), custom_call_target="tpu_custom_call" | custom-call | tf_op jit(solution)/shard_map/cond/branch_1_fun/enc_ffn/pallas_call | solution.py:422
  53.4 2.1 collective-permute-start
  55.5 16.6 %conditional.12 = ((bf16[288,1024]{1,0:T(8,128)(2,1)}, bf16[288,4096]{1,0:T(8,128)(2,1)}, bf16[288,512]{1,0:T(8,128)(2,1)}, bf16[288,512]{1,0:T(8,128)(2,1)}, bf...) conditional(s32[]{:T(128)} %convert_element_type.4, () %tuple.83, (bf16[864,1024]{1,0:T(8,128)(2,1)}, ...), branch_computations={%region_4.5_spmd, %region_5.6_spmd} | conditional | bytes 8 | solution.py:1272
  55.5 16.6 %enc_ffn.5 = (bf16[288,1024]{1,0:T(8,128)(2,1)}, bf16[288,4096]{1,0:T(8,128)(2,1)}, bf16[288,512]{1,0:T(8,128)(2,1)}, bf16[288,512]{1,0:T(8,128)(2,1)}, bf16[288,1024]{1,0:T(8,128)(2,1)}, /*index=5*/f32[288,128]{1,0:T(8,128)}) custom-call(bf16[864,1024]{1,0:T(8,128)(2,1)} %get-tuple-element.385.x_ref, bf16[864,1024]{1,0:T(8,128)(2,1)} %get-tuple-element.386.att_ref, ...), custom_call_target="tpu_custom_call" | custom-call | tf_op jit(solution)/shard_map/cond/branch_1_fun/enc_ffn/pallas_call | solution.py:422
  72.1 2.1 collective-permute-start.2
  74.2 29.6 %conditional.11 = (bf16[288,1024]{1,0:T(8,128)(2,1)}, bf16[288,4096]{1,0:T(8,128)(2,1)}, bf16[288,512]{1,0:T(8,128)(2,1)}, bf16[288,512]{1,0:T(8,128)(2,1)}, bf1...) conditional(s32[]{:T(128)} %convert_element_type.4, ...), branch_computations={%region_2.3_spmd, %region_3.4_spmd} | conditional | bytes 8913032 | solution.py:1272
  87.1 16.7 %enc_ffn.4 = (bf16[288,1024]{1,0:T(8,128)(2,1)}, bf16[288,4096]{1,0:T(8,128)(2,1)}, bf16[288,512]{1,0:T(8,128)(2,1)}, bf16[288,512]{1,0:T(8,128)(2,1)}, bf16[288,1024]{1,0:T(8,128)(2,1)}, /*index=5*/f32[288,128]{1,0:T(8,128)}) custom-call(bf16[864,1024]{1,0:T(8,128)(2,1)} %get-tuple-element.365.x_ref, bf16[864,1024]{1,0:T(8,128)(2,1)} %get-tuple-element.366.att_ref, ...), custom_call_target="tpu_custom_call" | custom-call | tf_op jit(solution)/shard_map/cond/branch_1_fun/enc_ffn/pallas_call | solution.py:422
  103.9 2.1 collective-permute-start.1
  106.0 12.9 %collective-permute-done.1 = bf16[288,1024]{1,0:T(8,128)(2,1)} collective-permute-done((bf16[288,1024]{1,0:T(8,128)(2,1)}, bf16[288,1024]{1,0:T(8,128)(2,1)}, u32[]{:S(2)}, u32[]{:S(2)}) %collective-permute-start.1) | collective-permute-done | bytes 589856 | tf_op jit(solution)/shard_map/ppermute | solution.py:1276
  124.6 2.0 conditional.16
  126.6 72.3 %collective-permute-done.3 = bf16[288,1024]{1,0:T(8,128)(2,1)} collective-permute-done((bf16[288,1024]{1,0:T(8,128)(2,1)}, bf16[288,1024]{1,0:T(8,128)(2,1)}, u32[]{:S(2)}, u32[]{:S(2)}) %collective-permute-start.3) | collective-permute-done | bytes 589856 | tf_op jit(solution)/shard_map/ppermute | solution.py:1280
  198.9 15.9 %conditional.17 = ((f32[288,1024]{1,0:T(8,128)}, bf16[288,1024]{1,0:T(8,128)(2,1)}, bf16[288,1024]{1,0:T(8,128)(2,1)}, bf16[288,512]{1,0:T(8,128)(2,1)})) conditional(s32[]{:T(128)} %convert_element_type.4, () %tuple.80, (bf16[288,1024]{1,0:T(8,128)(2,1)}, bf16[288,1024]{1,0:T(8,128)(2,1)}, bf16[288,1024]{1,0:T(8,128)(2,1)}, ...), branch_computations={%region_14.15_spmd, %region_15.16_spmd} | conditional | bytes 8 | solution.py:1272
  198.9 15.9 %enc_ffn_back.3 = (f32[288,1024]{1,0:T(8,128)}, bf16[288,1024]{1,0:T(8,128)(2,1)}, bf16[288,1024]{1,0:T(8,128)(2,1)}, bf16[288,512]{1,0:T(8,128)(2,1)}) custom-call(bf16[288,1024]{1,0:T(8,128)(2,1)} %get-tuple-element.483.refs_0_, bf16[288,1024]{1,0:T(8,128)(2,1)} %get-tuple-element.484.refs_1_, bf16[288,1024]{1,0:T(8,128)(2,1)} %get-tuple-element.485.refs_2_, ...), custom_call_target="tpu_custom_call" | custom-call | tf_op jit(solution)/shard_map/cond/branch_1_fun/enc_ffn_back/pallas_call | solution.py:529
  214.9 15.6 %conditional.18 = ((f32[288,1024]{1,0:T(8,128)}, bf16[288,1024]{1,0:T(8,128)(2,1)}, bf16[288,1024]{1,0:T(8,128)(2,1)}, bf16[288,512]{1,0:T(8,128)(2,1)})) conditional(s32[]{:T(128)} %convert_element_type.4, () %tuple.94, (bf16[288,1024]{1,0:T(8,128)(2,1)}, bf16[288,1024]{1,0:T(8,128)(2,1)S(1)}, bf16[288,1024]{1,0:T(8,128)(2,1)S(1)}, ...), branch_computations={%region_16.17_spmd, %region_17.18_spmd} | conditional | bytes 8 | solution.py:1272
  215.1 15.3 %enc_ffn_back.4 = (f32[288,1024]{1,0:T(8,128)}, bf16[288,1024]{1,0:T(8,128)(2,1)}, bf16[288,1024]{1,0:T(8,128)(2,1)}, bf16[288,512]{1,0:T(8,128)(2,1)}) custom-call(bf16[288,1024]{1,0:T(8,128)(2,1)} %get-tuple-element.495.refs_0_, bf16[288,1024]{1,0:T(8,128)(2,1)S(1)} %get-tuple-element.496.refs_1_, bf16[288,1024]{1,0:T(8,128)(2,1)S(1)} %get-tuple-element.497.refs_2_, ...), custom_call_target="tpu_custom_call" | custom-call | tf_op jit(solution)/shard_map/cond/branch_1_fun/enc_ffn_back/pallas_call | solution.py:529
  230.5 2.7 collective-permute-done.6
  233.2 21.5 %conditional.19 = (f32[288,1024]{1,0:T(8,128)}, bf16[288,1024]{1,0:T(8,128)(2,1)}, f32[1024,512]{1,0:T(8,128)}, f32[1,512]{1,0:T(1,128)S(1)}, f32[512,1024]{1,0:T(8,128)}, /*index=5*/f32[1,1024]{1,0:T(1,128)S(1)}) conditional(s32[]{:T(128)} %convert_element_type.4, () %tuple.96, (bf16[192,1024]{1,0:T(8,128)(2,1)}, bf16[96,1024]{1,0:T(8,128)(2,1)}, ...), branch_computations={%region_18.19_spmd, %region_19.20_spmd} | conditional | bytes 16515372 | solution.py:1272
  233.4 15.9 %enc_ffn_back.5 = (f32[288,1024]{1,0:T(8,128)}, bf16[288,1024]{1,0:T(8,128)(2,1)}, bf16[288,1024]{1,0:T(8,128)(2,1)}, bf16[288,512]{1,0:T(8,128)(2,1)}) custom-call(bf16[192,1024]{1,0:T(8,128)(2,1)} %get-tuple-element.513.refs_0_, bf16[96,1024]{1,0:T(8,128)(2,1)} %get-tuple-element.514.refs_1_, bf16[288,1024]{1,0:T(8,128)(2,1)} %get-tuple-element.515.refs_2_, ...), custom_call_target="tpu_custom_call" | custom-call | tf_op jit(solution)/shard_map/cond/branch_1_fun/enc_ffn_back/pallas_call | solution.py:529
  249.4 5.2 %adapter_grads.1 = (f32[1024,512]{1,0:T(8,128)}, f32[1,512]{1,0:T(1,128)S(1)}, f32[512,1024]{1,0:T(8,128)}, f32[1,1024]{1,0:T(1,128)S(1)}) custom-call(bf16[288,1024]{1,0:T(8,128)(2,1)S(1)} %copy-done.17, bf16[288,1024]{1,0:T(8,128)(2,1)S(1)} %copy-done.19, bf16[288,1024]{1,0:T(8,128)(2,1)S(1)} %copy-done.16, bf16[288,512]{1,0:T(8,128)(2,1)S(1)} %copy-done.33, ...), custom_call_target="tpu_custom_call" | custom-call | tf_op jit(solution)/shard_map/cond/branch_1_fun/adapter_grads/pallas_call | solution.py:579
  254.8 62.8 %finish.1 = (bf16[864,512]{1,0:T(8,128)(2,1)}, bf16[512,512]{1,0:T(8,128)(2,1)}, bf16[512,512]{1,0:T(8,128)(2,1)}, bf16[512,1024]{1,0:T(8,128)(2,1)}, bf16[1024,512]{1,0:T(8,128)(2,1)}, /*index=5*/f32[64,1024]{1,0:T(8,128)}) custom-call(bf16[864,3072]{1,0:T(8,128)(2,1)} %get-tuple-element.629.q_ref.k_ref.v_ref, ...), custom_call_target="tpu_custom_call" | custom-call | tf_op jit(solution)/shard_map/finish/pallas_call | solution.py:1183
  322.3 1.6 bitcast_convert_fusion.1
  (98 shorter events, 15.4 us)
Async XLA Ops:
  11.6 26.3 %copy-start.1 = (bf16[1024,1024]{1,0:T(8,128)(2,1)S(1)}, bf16[1024,1024]{1,0:T(8,128)(2,1)}, u32[]{:S(2)}) copy-start(bf16[1024,1024]{1,0:T(8,128)(2,1)} %get-tuple-element.330.wo_ref) | copy-start | bytes 6291460 | tf_op jit(solution)/shard_map/cond
  11.6 26.3 %copy-start.6 = (bf16[1024,512]{1,0:T(8,128)(2,1)S(1)}, bf16[1024,512]{1,0:T(8,128)(2,1)}, u32[]{:S(2)}) copy-start(bf16[1024,512]{1,0:T(8,128)(2,1)} %get-tuple-element.334.down_ref) | copy-start | bytes 3145732 | tf_op jit(solution)/shard_map/cond
  11.6 26.3 %copy-start.8 = (bf16[512,1024]{1,0:T(8,128)(2,1)S(1)}, bf16[512,1024]{1,0:T(8,128)(2,1)}, u32[]{:S(2)}) copy-start(bf16[512,1024]{1,0:T(8,128)(2,1)} %get-tuple-element.336.up_ref) | copy-start | bytes 3145732 | tf_op jit(solution)/shard_map/cond
  11.6 26.3 %copy-start.26 = (f32[2,1024]{1,0:T(2,128)S(1)}, f32[2,1024]{1,0:T(2,128)}, u32[]{:S(2)}) copy-start(f32[2,1024]{1,0:T(2,128)} %get-tuple-element.331.gain_ref) | copy-start | bytes 24580 | tf_op jit(solution)/shard_map/cond
  11.6 26.3 %copy-start.41 = (f32[1,1024]{1,0:T(1,128)S(1)}, f32[1,1024]{1,0:T(1,128)}, u32[]{:S(2)}) copy-start(f32[1,1024]{1,0:T(1,128)} %get-tuple-element.337.upb_ref) | copy-start | bytes 12292 | tf_op jit(solution)/shard_map/cond
  11.6 26.3 %copy-start.43 = (f32[1,512]{1,0:T(1,128)S(1)}, f32[1,512]{1,0:T(1,128)}, u32[]{:S(2)}) copy-start(f32[1,512]{1,0:T(1,128)} %get-tuple-element.335.downb_ref) | copy-start | bytes 6148 | tf_op jit(solution)/shard_map/cond
  53.4 20.9 %collective-permute-start = (bf16[288,1024]{1,0:T(8,128)(2,1)}, bf16[288,1024]{1,0:T(8,128)(2,1)}, u32[]{:S(2)}, u32[]{:S(2)}) collective-permute-start(bf16[288,1024]{1,0:T(8,128)(2,1)} %get-tuple-element.632), channel_id=1, source_target_pairs={{0,16},{1,17},{2,18},{3,19},{4,20},{5,21},{6,22},{7,23},{8,24},{9,... | collective-permute-start | bytes 1769480 | tf_op jit(solution)/shard_map/ppermute | solution.py:1276
  55.5 18.8 %copy-start.47 = (s32[1,2]{1,0:T(1,128)S(1)}, s32[1,2]{1,0:T(1,128)}, u32[]{:S(2)}) copy-start(s32[1,2]{1,0:T(1,128)} %param.42) | copy-start | bytes 28
  72.1 33.9 %collective-permute-start.2 = (bf16[288,1024]{1,0:T(8,128)(2,1)}, bf16[288,1024]{1,0:T(8,128)(2,1)}, u32[]{:S(2)}, u32[]{:S(2)}) collective-permute-start(bf16[288,1024]{1,0:T(8,128)(2,1)} %get-tuple-element.635), channel_id=1, source_target_pairs={{0,16},{1,17},{2,18},{3,19},{4,20},{5,21},{6,22},{7,23},{8,24},{9,... | collective-permute-start | bytes 1769480 | tf_op jit(solution)/shard_map/ppermute | solution.py:1276
  103.9 15.1 %collective-permute-start.1 = (bf16[288,1024]{1,0:T(8,128)(2,1)}, bf16[288,1024]{1,0:T(8,128)(2,1)}, u32[]{:S(2)}, u32[]{:S(2)}) collective-permute-start(bf16[288,1024]{1,0:T(8,128)(2,1)} %get-tuple-element.634), channel_id=1, source_target_pairs={{0,16},{1,17},{2,18},{3,19},{4,20},{5,21},{6,22},{7,23},{8,24},{9,... | collective-permute-start | bytes 1769480 | tf_op jit(solution)/shard_map/ppermute | solution.py:1276
  119.3 79.6 %collective-permute-start.3 = (bf16[288,1024]{1,0:T(8,128)(2,1)}, bf16[288,1024]{1,0:T(8,128)(2,1)}, u32[]{:S(2)}, u32[]{:S(2)}) collective-permute-start(bf16[288,1024]{1,0:T(8,128)(2,1)} %get-tuple-element.638), channel_id=1, source_target_pairs={{16,0},{17,1},{18,2},{19,3},{20,4},{21,5},{22,6},{23,7},{24,8},{25... | collective-permute-start | bytes 1769480 | tf_op jit(solution)/shard_map/ppermute | solution.py:1280
  120.6 94.2 %collective-permute-start.4 = (bf16[288,1024]{1,0:T(8,128)(2,1)}, bf16[288,1024]{1,0:T(8,128)(2,1)}, u32[]{:S(2)}, u32[]{:S(2)}) collective-permute-start(bf16[288,1024]{1,0:T(8,128)(2,1)} %get-tuple-element.659), channel_id=1, source_target_pairs={{16,0},{17,1},{18,2},{19,3},{20,4},{21,5},{22,6},{23,7},{24,8},{25... | collective-permute-start | bytes 1769480 | tf_op jit(solution)/shard_map/ppermute | solution.py:1280
  121.9 111.2 %collective-permute-start.5 = (bf16[192,1024]{1,0:T(8,128)(2,1)}, bf16[192,1024]{1,0:T(8,128)(2,1)}, u32[]{:S(2)}, u32[]{:S(2)}) collective-permute-start(bf16[192,1024]{1,0:T(8,128)(2,1)} %get-tuple-element.665), channel_id=1, source_target_pairs={{16,0},{17,1},{18,2},{19,3},{20,4},{21,5},{22,6},{23,7},{24,8},{25... | collective-permute-start | bytes 1179656 | tf_op jit(solution)/shard_map/ppermute | solution.py:1280
  123.3 109.9 %collective-permute-start.6 = (bf16[96,1024]{1,0:T(8,128)(2,1)}, bf16[96,1024]{1,0:T(8,128)(2,1)}, u32[]{:S(2)}, u32[]{:S(2)}) collective-permute-start(bf16[96,1024]{1,0:T(8,128)(2,1)} %get-tuple-element.666), channel_id=1, source_target_pairs={{16,0},{17,1},{18,2},{19,3},{20,4},{21,5},{22,6},{23,7},{24,8},{25... | collective-permute-start | bytes 589832 | tf_op jit(solution)/shard_map/ppermute | solution.py:1280
  214.9 18.3 %copy-start.32 = (bf16[288,512]{1,0:T(8,128)(2,1)S(1)}, bf16[288,512]{1,0:T(8,128)(2,1)}, u32[]{:S(2)}) copy-start(bf16[288,512]{1,0:T(8,128)(2,1)} %get-tuple-element.673) | copy-start | bytes 884740
  214.9 18.3 %copy-start.38 = (f32[288,128]{1,0:T(8,128)S(1)}, f32[288,128]{1,0:T(8,128)}, u32[]{:S(2)}) copy-start(f32[288,128]{1,0:T(8,128)} %get-tuple-element.668) | copy-start | bytes 442372
  233.2 21.6 %copy-start.11 = (bf16[864,1024]{1,0:T(8,128)(2,1)S(1)}, bf16[864,1024]{1,0:T(8,128)(2,1)}, u32[]{:S(2)}) copy-start(bf16[864,1024]{1,0:T(8,128)(2,1)} %get-tuple-element.630.o_ref) | copy-start | bytes 5308420
  233.2 21.6 %copy-start.49 = (f32[1,1024]{1,0:T(1,128)S(1)}, f32[1,1024]{1,0:T(1,128)}, u32[]{:S(2)}) copy-start(f32[1,1024]{1,0:T(1,128)} %get-tuple-element.691.long_upb) | copy-start | bytes 12292
  233.2 21.6 %copy-start.50 = (f32[1,1024]{1,0:T(1,128)S(1)}, f32[1,1024]{1,0:T(1,128)}, u32[]{:S(2)}) copy-start(f32[1,1024]{1,0:T(1,128)} %get-tuple-element.695.short_upb) | copy-start | bytes 12292
  233.2 21.6 %copy-start.51 = (f32[1,512]{1,0:T(1,128)S(1)}, f32[1,512]{1,0:T(1,128)}, u32[]{:S(2)}) copy-start(f32[1,512]{1,0:T(1,128)} %get-tuple-element.689.long_downb) | copy-start | bytes 6148
  233.2 21.6 %copy-start.52 = (f32[1,512]{1,0:T(1,128)S(1)}, f32[1,512]{1,0:T(1,128)}, u32[]{:S(2)}) copy-start(f32[1,512]{1,0:T(1,128)} %get-tuple-element.693.short_downb) | copy-start | bytes 6148
  233.3 16.0 %copy-start.16 = (bf16[288,1024]{1,0:T(8,128)(2,1)S(1)}, bf16[288,1024]{1,0:T(8,128)(2,1)}, u32[]{:S(2)}) copy-start(bf16[288,1024]{1,0:T(8,128)(2,1)} %get-tuple-element.516.refs_3_.refs_2_) | copy-start | bytes 1769476 | tf_op jit(solution)/shard_map/cond
  233.3 16.0 %copy-start.17 = (bf16[288,1024]{1,0:T(8,128)(2,1)S(1)}, bf16[288,1024]{1,0:T(8,128)(2,1)}, u32[]{:S(2)}) copy-start(bf16[288,1024]{1,0:T(8,128)(2,1)} %get-tuple-element.528.refs_0_) | copy-start | bytes 1769476 | tf_op jit(solution)/shard_map/cond
  233.3 16.0 %copy-start.19 = (bf16[288,1024]{1,0:T(8,128)(2,1)S(1)}, bf16[288,1024]{1,0:T(8,128)(2,1)}, u32[]{:S(2)}) copy-start(bf16[288,1024]{1,0:T(8,128)(2,1)} %get-tuple-element.529.refs_1_) | copy-start | bytes 1769476 | tf_op jit(solution)/shard_map/cond
  (18 other events, 211.7 us)

commit v2 on v1

--- a/solution.py
+++ b/solution.py
@@ -169,7 +169,7 @@
     return parts[0] if len(parts) == 1 else jnp.concatenate(parts, 0)
 
 
-def attend_pair(*refs, segs, prefix, causal, pieces, which):
+def attend_pair(*refs, segs, prefix, causal, pieces, which, checked):
     len_ref, q_ref = refs[:2]
     k_refs, v_refs = refs[2 : 2 + pieces], refs[2 + pieces : 2 + 2 * pieces]
     at = 2 + 2 * pieces
@@ -179,37 +179,82 @@
         at += 2
     o_ref, inv_ref = refs[at : at + 2]
     p_refs = refs[at + 2 :]
-    for seg, (q0, nq, k0, nk) in enumerate(segs):
-        keys = stacked(k_refs, pk_ref, k0, nk)
-        values = stacked(v_refs, pv_ref, k0, nk)
-        count = keys.shape[0]
-        row = lax.broadcasted_iota(jnp.int32, (count, 1), 0)
-        seen = row < jnp.minimum(len_ref[0, which + seg], nk)
-        if prefix:
-            seen = seen | ((row >= nk) & (row < nk + PRE))
-        queries = q_ref[q0 : q0 + nq] * bf(HD**-0.5)
-        out = inv = None
-        for head in range(2):
-            own, first, _ = head_lanes(head)
-            k_own = jnp.where(own, keys, jnp.where(first & ~seen, bf(big_negative), bf(0)))
-            q_own = jnp.where(own, queries, jnp.where(first, bf(1), bf(0)))
-            v_own = jnp.where(own, values, bf(1))
-            scores = nt(k_own, q_own)
-            if causal:
-                key_at = lax.broadcasted_iota(jnp.int32, scores.shape, 0)
-                query_at = lax.broadcasted_iota(jnp.int32, scores.shape, 1)
-                allowed = (key_at <= query_at) | (key_at >= nk)
-                scores = jnp.where(allowed, scores, big_negative)
-            peak = jnp.max(scores, axis=0, keepdims=True)
-            weights = jnp.exp(scores - peak).astype(BF)
-            p_refs[seg][head] = weights
-            mixed = tn(weights, v_own)
-            inverse = 1.0 / pltpu.roll(mixed, HD, 1)
-            mixed = mixed * inverse
-            out = mixed if out is None else jnp.where(own, mixed, out)
-            inv = inverse if inv is None else jnp.where(own, inverse, inv)
-        o_ref[q0 : q0 + nq] = out.astype(BF)
-        inv_ref[q0 : q0 + nq] = inv
+
+    def work(peaked):
+        for seg, (q0, nq, k0, nk) in enumerate(segs):
+            keys = stacked(k_refs, pk_ref, k0, nk)
+            values = stacked(v_refs, pv_ref, k0, nk)
+            count = keys.shape[0]
+            row = lax.broadcasted_iota(jnp.int32, (count, 1), 0)
+            seen = row < jnp.minimum(len_ref[0, which + seg], nk)
+            if prefix:
+                seen = seen | ((row >= nk) & (row < nk + PRE))
+            queries = q_ref[q0 : q0 + nq] * bf(HD**-0.5)
+            out = inv = None
+            across = nq >= 4 * LANES
+            outs, invs = [], []
+            if across:
+                turned = values.T
+                ones = jnp.ones((16, count), BF)
+            for head in range(2):
+                own, first, _ = head_lanes(head)
+                k_own = jnp.where(own, keys, jnp.where(first & ~seen, bf(big_negative), bf(0)))
+                q_own = jnp.where(own, queries, jnp.where(first, bf(1), bf(0)))
+                scores = nt(k_own, q_own)
+                if causal:
+                    key_at = lax.broadcasted_iota(jnp.int32, scores.shape, 0)
+                    query_at = lax.broadcasted_iota(jnp.int32, scores.shape, 1)
+                    allowed = (key_at <= query_at) | (key_at >= nk)
+                    scores = jnp.where(allowed, scores, big_negative)
+                if peaked:
+                    scores = scores - jnp.max(scores, axis=0, keepdims=True)
+                weights = jnp.exp(scores).astype(BF)
+                p_refs[seg][head] = weights
+                if across:
+                    rows = jnp.concatenate([turned[head * HD : (head + 1) * HD], ones], 0)
+                    mixed = nn(rows, weights)
+                    inverse = 1.0 / mixed[HD : HD + 1]
+                    outs.append(mixed[:HD] * inverse)
+                    invs.append(jnp.broadcast_to(inverse, (HD, nq)))
+                    continue
+                mixed = tn(weights, jnp.where(own, values, bf(1)))
+                inverse = 1.0 / pltpu.roll(mixed, HD, 1)
+                mixed = mixed * inverse
+                out = mixed if out is None else jnp.where(own, mixed, out)
+                inv = inverse if inv is None else jnp.where(own, inverse, inv)
+            if across:
+                out = jnp.concatenate(outs, 0).T
+                inv = jnp.concatenate(invs, 0).T
+            o_ref[q0 : q0 + nq] = out.astype(BF)
+            inv_ref[q0 : q0 + nq] = inv
+
+    if not checked:
+        work(True)
+        return
+
+    limit = 50.0**2
+    head_row = lax.broadcasted_iota(jnp.int32, (LANES, LANES), 0) // HD
+    head_col = lax.broadcasted_iota(jnp.int32, (LANES, LANES), 1) // HD
+    same_head = jnp.where(head_row == head_col, 1.0, 0.0).astype(BF)
+
+    def largest(array):
+        square = (array.astype(F32) * array.astype(F32)).astype(BF)
+        return jnp.max(nn(square, same_head), axis=0, keepdims=True)
+
+    key_peak = largest(k_refs[0][...])
+    for ref in k_refs[1:]:
+        key_peak = jnp.maximum(key_peak, largest(ref[...]))
+    if prefix:
+        key_peak = jnp.maximum(key_peak, largest(pk_ref[...]))
+    small = jnp.max(largest(q_ref[...]) * key_peak) * (1.0 / HD) <= limit
+
+    @pl.when(small)
+    def _():
+        work(False)
+
+    @pl.when(jnp.logical_not(small))
+    def _():
+        work(True)
 
 
 def lane_views(refs, group, j):
@@ -231,7 +276,7 @@
     return pl.BlockSpec((rows, group * LANES), lambda h: (row_block, h + offset // group))
 
 
-def attend(lengths, q, keys, values, prefixes, segs, causal, which=0, group=1):
+def attend(lengths, q, keys, values, prefixes, segs, causal, which=0, group=1, checked=False):
     pairs = 8
     q_rows = q[1]
     prefix = prefixes is not None
@@ -247,7 +292,8 @@
     weight_shapes = [(2 * pairs, nk + extra, nq) for _, nq, _, nk in segs]
     return pl.pallas_call(
         functools.partial(
-            attend_kernel, group=group, segs=segs, prefix=prefix, causal=causal, pieces=len(keys), which=which
+            attend_kernel, group=group, segs=segs, prefix=prefix, causal=causal, pieces=len(keys), which=which,
+            checked=checked,
         ),
         grid=(pairs // group,),
         in_specs=specs,
@@ -276,6 +322,10 @@
         grads_low = grads.astype(BF)
         dots = grads * o_ref[q0 : q0 + nq].astype(F32)
         dq = dk = dv = None
+        across = nq >= LANES and keys.shape[0] >= 4 * LANES
+        turned_grads = []
+        if across:
+            turned = keys.T
         for head in range(2):
             own, first, second = head_lanes(head)
             row_dot = -jnp.sum(jnp.where(own, dots, 0.0), axis=1, keepdims=True)
@@ -289,10 +339,15 @@
             score_grad = (weights.astype(F32) * nt(v_own, g_own)).astype(BF)
             dv_head = nn(weights, grads_low)
             dk_head = nn(score_grad, queries)
-            dq_head = tn(score_grad, keys)
-            dq = dq_head if dq is None else jnp.where(own, dq_head, dq)
+            dq_head = None if across else tn(score_grad, keys)
+            if across:
+                turned_grads.append(nn(turned[head * HD : (head + 1) * HD], score_grad))
+            if not across:
+                dq = dq_head if dq is None else jnp.where(own, dq_head, dq)
             dk = dk_head if dk is None else jnp.where(own, dk_head, dk)
             dv = dv_head if dv is None else jnp.where(own, dv_head, dv)
+        if across:
+            dq = jnp.concatenate(turned_grads, 0).T
         dk = dk * scale
         dq_ref[q0 : q0 + nq] = (dq * scale).astype(BF)
         at = k0 - segs[0][2]
@@ -365,6 +420,35 @@
     )(*args)
 
 
+class Weights:
+    def __init__(self, sources, targets, sems):
+        self.sources, self.targets, self.sems = sources, targets, sems
+
+    def copy(self, name, part=None):
+        source, target = self.sources[name], self.targets[name]
+        first = list(self.sources).index(name)
+        sem = self.sems.at[first, 0 if part is None else part]
+        if part is not None:
+            cut = pl.ds(pl.multiple_of(part * wide, wide), wide)
+            index = (slice(None), cut) if name == "in" else (cut, slice(None))
+            source, target = source.at[index], target.at[index]
+        return pltpu.make_async_copy(source, target, sem)
+
+    def wait(self, name, part=None):
+        self.copy(name, part).wait()
+
+    def part(self, name, part):
+        cut = pl.ds(pl.multiple_of(part * wide, wide), wide)
+        index = (slice(None), cut) if name == "in" else (cut, slice(None))
+        return self.targets[name].at[index]
+
+
+def weight_scratch(arrays, parts):
+    return [pltpu.VMEM(a.shape, BF) for a in arrays] + [
+        pltpu.SemaphoreType.DMA((len(arrays), parts))
+    ]
+
+
 def ffn_step(low_ref, acc_ref, in_ref, out_ref, slope_ref, act_ref, bias_ref, scale):
     for start, size in row_tiles(low_ref.shape[0]):
         rows = slice(start, start + size)
@@ -381,33 +465,45 @@
 
 
 def enc_ffn_kernel(
-    x_ref, att_ref, wo_ref, gain_ref, in_ref, out_ref, down_ref, downb_ref, up_ref, upb_ref,
-    mem_ref, slope_ref, pre_slope_ref, act_ref, low_ref, scales_ref, acc_ref,
+    x_ref, att_ref, gain_ref, downb_ref, upb_ref, wo_hbm, in_hbm, out_hbm, down_hbm, up_hbm,
+    mem_ref, slope_ref, pre_slope_ref, act_ref, low_ref, scales_ref,
+    acc_ref, wo_ref, in_ref, out_ref, down_ref, up_ref, sems,
 ):
-    step = pl.program_id(0)
-    last = pl.num_programs(0) - 1
-
-    @pl.when(step == 0)
-    def _():
-        first = x_ref[...].astype(F32) + nn(att_ref[...], wo_ref[...])
-        hat, scale = norm_rows(first)
-        normed = hat * gain_ref[0:1]
-        acc_ref[...] = normed
-        low_ref[...] = normed.astype(BF)
-        scales_ref[:, 0:1] = scale
-
-    @pl.when((step > 0) & (step < last))
-    def _():
-        ffn_step(low_ref, acc_ref, in_ref, out_ref, slope_ref, None, None, None)
-
-    @pl.when(step == last)
-    def _():
+    weights = Weights(
+        {"wo": wo_hbm, "in": in_hbm, "out": out_hbm, "down": down_hbm, "up": up_hbm},
+        {"wo": wo_ref, "in": in_ref, "out": out_ref, "down": down_ref, "up": up_ref},
+        sems,
+    )
+
+    weights.copy("wo").start()
+    for part in range(in_ref.shape[1] // wide):
+        weights.copy("in", part).start()
+        weights.copy("out", part).start()
+    weights.copy("down").start()
+    weights.copy("up").start()
+    weights.wait("wo")
+    first = x_ref[...].astype(F32) + nn(att_ref[...], wo_ref[...])
+    hat, scale = norm_rows(first)
+    normed = hat * gain_ref[0:1]
+    acc_ref[...] = normed
+    low_ref[...] = normed.astype(BF)
+    scales_ref[:, 0:1] = scale
+
+    for part in range(in_ref.shape[1] // wide):
+        weights.wait("in", part)
+        weights.wait("out", part)
+        cols = slice(part * wide, (part + 1) * wide)
         ffn_step(
-            low_ref, acc_ref, down_ref, up_ref, pre_slope_ref, act_ref, downb_ref, adapter_scale
-        )
-        hat, scale = norm_rows(acc_ref[...] + adapter_scale * upb_ref[...])
-        mem_ref[...] = (hat * gain_ref[1:2]).astype(BF)
-        scales_ref[:, 1:2] = scale
+            low_ref, acc_ref, in_ref.at[:, cols], out_ref.at[cols], slope_ref.at[:, cols],
+            None, None, None,
+        )
+
+    weights.wait("down")
+    weights.wait("up")
+    ffn_step(low_ref, acc_ref, down_ref, up_ref, pre_slope_ref, act_ref, downb_ref, adapter_scale)
+    hat, scale = norm_rows(acc_ref[...] + adapter_scale * upb_ref[...])
+    mem_ref[...] = (hat * gain_ref[1:2]).astype(BF)
+    scales_ref[:, 1:2] = scale
 
 
 def enc_ffn(x, att, w, part):
@@ -415,28 +511,21 @@
     rows = ENC_ROWS
     hidden = w["ffn_in"].shape[1]
     steps = hidden // wide
-
-    def at(i):
-        return jnp.clip(i - 1, 0, steps - 1)
-
+    weights = [w["out"], w["ffn_in"], w["ffn_out"], w["down"], w["up"]]
     return pl.pallas_call(
         enc_ffn_kernel,
-        grid=(steps + 2,),
+        grid=(1,),
         in_specs=[
             pl.BlockSpec((rows, width), lambda i: (part, 0)),
             pl.BlockSpec((rows, width), lambda i: (part, 0)),
-            whole((width, width)),
             whole((2, width)),
-            pl.BlockSpec((width, wide), lambda i: (0, at(i))),
-            pl.BlockSpec((wide, width), lambda i: (at(i), 0)),
-            whole((width, chunk)),
             whole((1, chunk)),
-            whole((chunk, width)),
             whole((1, width)),
-        ],
+        ]
+        + [pl.BlockSpec(memory_space=pl.ANY)] * len(weights),
         out_specs=[
             whole((rows, width)),
-            pl.BlockSpec((rows, wide), lambda i: (0, at(i))),
+            whole((rows, hidden)),
             whole((rows, chunk)),
             whole((rows, chunk)),
             whole((rows, width)),
@@ -450,13 +539,10 @@
             jax.ShapeDtypeStruct((rows, width), BF),
             jax.ShapeDtypeStruct((rows, LANES), F32),
         ],
-        scratch_shapes=[pltpu.VMEM((rows, width), F32)],
+        scratch_shapes=[pltpu.VMEM((rows, width), F32)] + weight_scratch(weights, steps),
         compiler_params=params(),
         name="enc_ffn",
-    )(
-        x, att, w["out"], w["gains"], w["ffn_in"], w["ffn_out"],
-        w["down"], w["down_bias"], w["up"], w["up_bias"],
-    )
+    )(x, att, w["gains"], w["down_bias"], w["up_bias"], *weights)
 
 
 def ffn_back_step(grad_ref, acc_ref, in_ref, out_ref, slope_ref):
@@ -483,42 +569,55 @@
     dupb_ref[...] = adapter_scale * jnp.sum(grad_ref[...].astype(F32), axis=0, keepdims=True)
 
 
-def enc_ffn_back_kernel(
-    *refs, pieces,
-):
+def enc_ffn_back_kernel(*refs, pieces):
     enc_ffn_back_body(refs[:pieces], *refs[pieces:])
 
 
 def enc_ffn_back_body(
     dmem_refs, mem_ref, low_ref, scales_ref, gain_ref, slope_ref, pre_slope_ref,
-    in_ref, out_ref, down_ref, up_ref, wo_ref,
+    up_hbm, down_hbm, in_hbm, out_hbm, wo_hbm,
     dfirst_ref, datt_ref, grad_ref, pre_ref,
-    acc_ref,
+    acc_ref, up_ref, down_ref, in_ref, out_ref, wo_ref, sems,
 ):
-    step = pl.program_id(0)
-    last = pl.num_programs(0) - 1
-
-    @pl.when(step == 0)
-    def _():
-        gain = gain_ref[1:2]
-        hat = mem_ref[...].astype(F32) / gain
-        grad = norm_rows_back(hat, scales_ref[:, 1:2], stacked(dmem_refs, None, 0, ENC_ROWS).astype(F32) * gain)
-        low = grad.astype(BF)
-        grad_ref[...] = low
-        back = adapter_scale * nt(low, up_ref[...])
-        pre = (back * pre_slope_ref[...].astype(F32)).astype(BF)
-        pre_ref[...] = pre
-        acc_ref[...] = grad + nt(pre, down_ref[...])
-
-    ffn_back_step(grad_ref, acc_ref, in_ref, out_ref, slope_ref)
-
-    @pl.when(step == last)
-    def _():
-        gain = gain_ref[0:1]
-        hat = low_ref[...].astype(F32) / gain
-        grad = norm_rows_back(hat, scales_ref[:, 0:1], acc_ref[...] * gain)
-        dfirst_ref[...] = grad
-        datt_ref[...] = nt(grad.astype(BF), wo_ref[...]).astype(BF)
+    weights = Weights(
+        {"up": up_hbm, "down": down_hbm, "in": in_hbm, "out": out_hbm, "wo": wo_hbm},
+        {"up": up_ref, "down": down_ref, "in": in_ref, "out": out_ref, "wo": wo_ref},
+        sems,
+    )
+
+    weights.copy("up").start()
+    weights.copy("down").start()
+    for part in range(in_ref.shape[1] // wide):
+        weights.copy("out", part).start()
+        weights.copy("in", part).start()
+    weights.copy("wo").start()
+    gain = gain_ref[1:2]
+    hat = mem_ref[...].astype(F32) / gain
+    dmem = stacked(dmem_refs, None, 0, ENC_ROWS).astype(F32)
+    grad = norm_rows_back(hat, scales_ref[:, 1:2], dmem * gain)
+    low = grad.astype(BF)
+    grad_ref[...] = low
+    weights.wait("up")
+    back = adapter_scale * nt(low, up_ref[...])
+    pre = (back * pre_slope_ref[...].astype(F32)).astype(BF)
+    pre_ref[...] = pre
+    weights.wait("down")
+    acc_ref[...] = grad + nt(pre, down_ref[...])
+
+    for part in range(in_ref.shape[1] // wide):
+        weights.wait("out", part)
+        weights.wait("in", part)
+        cols = slice(part * wide, (part + 1) * wide)
+        ffn_back_step(
+            grad_ref, acc_ref, in_ref.at[:, cols], out_ref.at[cols], slope_ref.at[:, cols]
+        )
+
+    gain = gain_ref[0:1]
+    hat = low_ref[...].astype(F32) / gain
+    grad = norm_rows_back(hat, scales_ref[:, 0:1], acc_ref[...] * gain)
+    dfirst_ref[...] = grad
+    weights.wait("wo")
+    datt_ref[...] = nt(grad.astype(BF), wo_ref[...]).astype(BF)
 
 
 def enc_ffn_back(dmems, saved, w):
@@ -526,23 +625,20 @@
     rows, width = mem.shape
     hidden = w["ffn_in"].shape[1]
     steps = hidden // wide
+    weights = [w["up"], w["down"], w["ffn_in"], w["ffn_out"], w["out"]]
     return pl.pallas_call(
         functools.partial(enc_ffn_back_kernel, pieces=len(dmems)),
-        grid=(steps,),
+        grid=(1,),
         in_specs=[whole(d.shape) for d in dmems]
         + [
             whole((rows, width)),
             whole((rows, width)),
             whole((rows, LANES)),
             whole((2, width)),
-            pl.BlockSpec((rows, wide), lambda i: (0, i)),
+            whole((rows, hidden)),
             whole((rows, chunk)),
-            pl.BlockSpec((width, wide), lambda i: (0, i)),
-            pl.BlockSpec((wide, width), lambda i: (i, 0)),
-            whole((width, chunk)),
-            whole((chunk, width)),
-            whole((width, width)),
-        ],
+        ]
+        + [pl.BlockSpec(memory_space=pl.ANY)] * len(weights),
         out_specs=[
             whole((rows, width)),
             whole((rows, width)),
@@ -555,13 +651,10 @@
             jax.ShapeDtypeStruct((rows, width), BF),
             jax.ShapeDtypeStruct((rows, chunk), BF),
         ],
-        scratch_shapes=[pltpu.VMEM((rows, width), F32)],
+        scratch_shapes=[pltpu.VMEM((rows, width), F32)] + weight_scratch(weights, steps),
         compiler_params=params(),
         name="enc_ffn_back",
-    )(
-        *dmems, mem, low, scales, w["gains"], slope, pre_slope,
-        w["ffn_in"], w["ffn_out"], w["down"], w["up"], w["out"],
-    )
+    )(*dmems, mem, low, scales, w["gains"], slope, pre_slope, *weights)
 
 
 def adapter_grads_kernel(*refs, parts):
@@ -615,92 +708,102 @@
 
 
 def dec_ffn_kernel(
-    len_ref, n_ref, catt_ref, cot_ref, wco_ref, cgain_ref, gain_ref,
-    in_ref, out_ref, down_ref, downb_ref, up_ref, upb_ref,
+    len_ref, n_ref, catt_ref, cot_ref, cgain_ref, gain_ref, downb_ref, upb_ref,
+    wco_hbm, in_hbm, out_hbm, down_hbm, up_hbm,
     y_ref, dsecond_ref, dcatt_ref, ddown_ref, ddownb_ref, dup_ref, dupb_ref,
     acc_ref, low_ref, grad_ref, slope_ref, pre_slope_ref, act_ref, pre_ref, scale_ref,
+    wco_ref, in_ref, out_ref, down_ref, up_ref, sems,
     *, steps, which,
 ):
     step = pl.program_id(0)
-    tiles = row_tiles(n_ref.shape[0], TGT)
+    weights = Weights(
+        {"wco": wco_hbm, "in": in_hbm, "out": out_hbm, "down": down_hbm, "up": up_hbm},
+        {"wco": wco_ref, "in": in_ref, "out": out_ref, "down": down_ref, "up": up_ref},
+        sems,
+    )
 
     @pl.when(step == 0)
     def _():
-        for start, size in tiles:
-            rows = slice(start, start + size)
-            second = n_ref[rows] + nn(catt_ref[rows], wco_ref[...])
-            hat, scale = norm_rows(second)
-            middle = hat * cgain_ref[...]
-            acc_ref[rows] = middle
-            low_ref[rows] = middle.astype(BF)
-            scale_ref[rows, 0:1] = scale
-
-    @pl.when((step > 0) & (step <= steps))
+        weights.copy("wco").start()
+        for part in range(steps):
+            weights.copy("in", part).start()
+            weights.copy("out", part).start()
+        weights.copy("down").start()
+        weights.copy("up").start()
+        weights.wait("wco")
+        second = n_ref[...] + nn(catt_ref[...], wco_ref[...])
+        hat, scale = norm_rows(second)
+        middle = hat * cgain_ref[...]
+        acc_ref[...] = middle
+        low_ref[...] = middle.astype(BF)
+        scale_ref[:, 0:1] = scale
+
+    @pl.when(step < steps)
     def _():
-        ffn_step(low_ref, acc_ref, in_ref, out_ref, slope_ref.at[step - 1], None, None, None)
-
-    @pl.when(step == steps + 1)
+        weights.wait("in", step)
+        weights.wait("out", step)
+        ffn_step(
+            low_ref, acc_ref, weights.part("in", step), weights.part("out", step),
+            slope_ref.at[step], None, None, None,
+        )
+
+    @pl.when(step == steps)
     def _():
+        weights.wait("down")
+        weights.wait("up")
         ffn_step(
-            low_ref, acc_ref, down_ref, up_ref, pre_slope_ref, act_ref, downb_ref,
-            adapter_scale,
-        )
-        for start, size in tiles:
-            rows = slice(start, start + size)
-            gain = gain_ref[1:2]
-            hat, scale = norm_rows(acc_ref[rows] + adapter_scale * upb_ref[...])
-            valid = lax.broadcasted_iota(jnp.int32, (size, 1), 0) < len_ref[0, which]
-            y_ref[rows] = jnp.where(valid, hat * gain, 0.0).astype(BF)
-            cot = jnp.where(valid, cot_ref[rows].astype(F32), 0.0)
-            grad = norm_rows_back(hat, scale, cot * gain)
-            acc_ref[rows] = grad
-            grad_ref[rows] = grad.astype(BF)
+            low_ref, acc_ref, down_ref, up_ref, pre_slope_ref, act_ref, downb_ref, adapter_scale
+        )
+        gain = gain_ref[1:2]
+        hat, scale = norm_rows(acc_ref[...] + adapter_scale * upb_ref[...])
+        row = lax.broadcasted_iota(jnp.int32, (low_ref.shape[0], 1), 0)
+        valid = row < len_ref[0, which]
+        y_ref[...] = jnp.where(valid, hat * gain, 0.0).astype(BF)
+        cot = jnp.where(valid, cot_ref[...].astype(F32), 0.0)
+        grad = norm_rows_back(hat, scale, cot * gain)
+        acc_ref[...] = grad
+        grad_ref[...] = grad.astype(BF)
         adapter_back(
             grad_ref, acc_ref, low_ref, act_ref, pre_slope_ref, down_ref, up_ref,
             (ddown_ref, ddownb_ref, dup_ref, dupb_ref), pre_ref,
         )
 
-    @pl.when(step > steps + 1)
+    @pl.when(step > steps)
     def _():
-        ffn_back_step(grad_ref, acc_ref, in_ref, out_ref, slope_ref.at[2 * steps + 1 - step])
-
-    @pl.when(step == 2 * steps + 1)
+        part = step - steps - 1
+        ffn_back_step(
+            grad_ref, acc_ref, weights.part("in", part), weights.part("out", part),
+            slope_ref.at[part],
+        )
+
+    @pl.when(step == 2 * steps)
     def _():
-        for start, size in tiles:
-            rows = slice(start, start + size)
-            gain = cgain_ref[...]
-            hat = low_ref[rows].astype(F32) / gain
-            grad = norm_rows_back(hat, scale_ref[rows, 0:1], acc_ref[rows] * gain)
-            dsecond_ref[rows] = grad
-            dcatt_ref[rows] = nt(grad.astype(BF), wco_ref[...]).astype(BF)
+        gain = cgain_ref[...]
+        hat = low_ref[...].astype(F32) / gain
+        grad = norm_rows_back(hat, scale_ref[:, 0:1], acc_ref[...] * gain)
+        dsecond_ref[...] = grad
+        dcatt_ref[...] = nt(grad.astype(BF), wco_ref[...]).astype(BF)
 
 
 def dec_ffn(lengths, n, catt, cot, w, cross, which):
     rows, width = catt.shape
     hidden = w["ffn_in"].shape[1]
     steps = hidden // wide
-
-    def at(i):
-        return jnp.where(i <= steps, jnp.clip(i - 1, 0, steps - 1), jnp.clip(2 * steps + 1 - i, 0, steps - 1))
-
+    weights = [cross["out"], w["ffn_in"], w["ffn_out"], w["down"], w["up"]]
     return pl.pallas_call(
         functools.partial(dec_ffn_kernel, steps=steps, which=which),
-        grid=(2 * steps + 2,),
+        grid=(2 * steps + 1,),
         in_specs=[
             pl.BlockSpec(memory_space=pltpu.SMEM),
             pl.BlockSpec((rows, width), lambda i: (which, 0)),
             whole((rows, width)),
             pl.BlockSpec((rows, width), lambda i: (which, 0)),
-            whole((width, width)),
             whole((1, width)),
             whole((2, width)),
-            pl.BlockSpec((width, wide), lambda i: (0, at(i))),
-            pl.BlockSpec((wide, width), lambda i: (at(i), 0)),
-            whole((width, chunk)),
             whole((1, chunk)),
-            whole((chunk, width)),
             whole((1, width)),
-        ],
+        ]
+        + [pl.BlockSpec(memory_space=pl.ANY)] * len(weights),
         out_specs=[
             whole((rows, width)),
             whole((rows, width)),
@@ -728,12 +831,12 @@
             pltpu.VMEM((rows, chunk), BF),
             pltpu.VMEM((rows, chunk), BF),
             pltpu.VMEM((rows, LANES), F32),
-        ],
+        ]
+        + weight_scratch(weights, steps),
         compiler_params=params(),
         name="dec_ffn",
     )(
-        lengths, n, catt, cot, cross["out"], cross["gain"], w["gains"],
-        w["ffn_in"], w["ffn_out"], w["down"], w["down_bias"], w["up"], w["up_bias"],
+        lengths, n, catt, cot, cross["gain"], w["gains"], w["down_bias"], w["up_bias"], *weights
     )
 
 
@@ -822,7 +925,7 @@
     enc_down, enc_downb, enc_up, enc_upb, long_down, long_downb, long_up, long_upb,
     short_down, short_downb, short_up, short_upb, dpk_ref, dpv_ref,
     y0_ref, y1_ref, dt_ref,
-    source_ref, y_ref, target_ref, o_up_ref, o_down_ref, o_small_ref,
+    source_ref, y_ref, target_ref, o_up_ref, o_down_ref, o_prefix_ref, o_upb_ref, o_downb_ref,
     dq, dk, dv, small, ups, downs, mine, theirs, half_sum, across_y, y_sum, landed, total, result,
     small_landed, small_total, small_result, dx_low, dx_high, dx_landed, lows, lows_landed,
     load_sems, pair_sems, y_sems, z_sems, gather_sems, share_y_sems, back_sems,
@@ -1124,7 +1227,10 @@
         o_down_ref[chunk:width] = result[chunk:width, chunk:width]
         for s in range(1, devices):
             small_share(s).wait()
-        o_small_ref[...] = small_result[...]
+        o_prefix_ref[0] = small_result[0:PRE]
+        o_prefix_ref[1] = small_result[PRE_PAD : PRE_PAD + PRE]
+        o_upb_ref[...] = small_result[PRE : PRE + 1]
+        o_downb_ref[...] = small_result[PRE + 1 : PRE + 2, 0:chunk]
 
         @pl.when(is_encoder)
         def _():
@@ -1202,7 +1308,7 @@
         out_specs=[
             once((rows, half)), once((targets, half)), once((targets, half)),
             once((chunk, width)), once((width, chunk)),
-            once((2 * PRE_PAD, width)),
+            once((2, PRE, width)), once((1, width)), once((1, chunk)),
         ],
         out_shape=[
             jax.ShapeDtypeStruct((rows, half), BF),
@@ -1210,7 +1316,9 @@
             jax.ShapeDtypeStruct((targets, half), BF),
             jax.ShapeDtypeStruct((chunk, width), BF),
             jax.ShapeDtypeStruct((width, chunk), BF),
-            jax.ShapeDtypeStruct((2 * PRE_PAD, width), F32),
+            jax.ShapeDtypeStruct((2, PRE, width), F32),
+            jax.ShapeDtypeStruct((1, width), F32),
+            jax.ShapeDtypeStruct((1, chunk), F32),
         ],
         scratch_shapes=[
             vmem((rows, width), BF), vmem((rows, width), BF), vmem((rows, width), BF),
@@ -1310,7 +1418,7 @@
     def encoder_start():
         qkv = product(sources, w["qkv"])
         att, inv, *weights = attend(
-            source_lengths, *self_columns(qkv), w["prefix"], enc_segs, False
+            source_lengths, *self_columns(qkv), w["prefix"], enc_segs, False, checked=True
         )
         return (qkv, att, inv, weights), enc_ffn(sources, att, w, 2)
 
@@ -1379,7 +1487,7 @@
         encoder_end, dmem2, dmem_short, part0, part1, part2, back0, back1
     )
     backs = (back0, back1, back2)
-    source_grad, y, target_grad, up, down, small = finish(
+    source_grad, y, target_grad, up, down, prefix_grad, up_bias, down_bias = finish(
         saved, [b[1] for b in backs], [b[0] for b in backs], w,
         [enc_adapter, long_adapter, short_adapter], dec_prefix, [long_y, short_y], dt,
     )
@@ -1387,11 +1495,11 @@
         y,
         source_grad,
         target_grad,
-        jnp.stack([small[:PRE], small[PRE_PAD : PRE_PAD + PRE]])[None],
+        prefix_grad[None],
         down.astype(F32)[None],
-        small[PRE + 1 : PRE + 2, :chunk],
+        down_bias,
         up.astype(F32)[None],
-        small[PRE : PRE + 1],
+        up_bias,
     )
 
 

time: 332 us -> 331 us (level)
  the two profiles are of different devices: /device:TPU:0 before, /device:TPU:27 now
where the time goes in v2:
time: 331 us; the launch traced here: 326 us
  Pallas kernels  236 us (71%)
  loops' own time  41.2 us (12%)
  waiting for transfers between devices  22.8 us (7%)
  starting transfers between devices  12.1 us (4%)
  local copies, waits for them, and re-layouts  8.78 us (3%)
  other arithmetic  4.4 us (1%)
    pallas_call x1, Pallas kernels, finish(): pl.pallas_call(functools.partial(finish_kernel, devices=devices), grid=(p...  75.1 us
    pallas_call x2, Pallas kernels, dec_ffn(): pl.pallas_call(functools.partial(dec_ffn_kernel, steps=steps, which=which...  49.5 us
    another operation x10, loops' own time, on_section(): return lax.cond(is_encoder, encoder_branch, decoder_branch, *operands)  41.2 us
    pallas_call x3, Pallas kernels, attend(): pl.pallas_call(functools.partial(attend_kernel, group=group, segs=segs, p...  31.2 us
    pallas_call x3, Pallas kernels, attend_back(): pl.pallas_call(functools.partial(attend_back_kernel, group=group, segs=se...  31 us
    ppermute x3, waiting for transfers between devices, to_decoder(): return lax.ppermute(block, 'section', [(0, 1)])  22.8 us
    pallas_call x4, Pallas kernels, product(): pl.pallas_call(product_kernel, grid=(width // tile,), in_specs=[whole((ro...  18 us
    pallas_call x3, Pallas kernels, back_product(): pl.pallas_call(functools.partial(back_product_kernel, parts=parts, residu...  16.5 us
  transfers between devices with their start and end apart: 7, of which 2 were waited for; matrix products, arithmetic and copies ran while one was open for 0% of the time, Pallas kernels for 23%

profile of v2, /device:TPU:27, one launch (start us, length us, event | category | flops | bytes accessed | tf_op | source)
XLA Modules:
  0.0 326.1 jit_solution(3291171087351245551)
XLA Ops:
  1.6 34.1 %conditional.10 = (bf16[864,3072]{1,0:T(8,128)(2,1)}, bf16[864,1024]{1,0:T(8,128)(2,1)}, f32[864,1024]{1,0:T(8,128)}, bf16[16,800,768]{2,1,0:T(8,128)(2,1)}, bf1...) conditional(s32[]{:T(128)} %convert_element_type.4, ...), branch_computations={%region_0.1_spmd, %region_1.2_spmd} | conditional | bytes 16834880 | solution.py:1380
  1.6 6.1 %product.5.refs_0_.refs_1_.refs_2_ = bf16[512,3072]{1,0:T(8,128)(2,1)S(1)} custom-call(bf16[512,1024]{1,0:T(8,128)(2,1)} %get-tuple-element.712.x_ref, bf16[1024,3072]{1,0:T(8,128)(2,1)} %get-tuple-element.308.w_ref), custom_call_target="tpu_custom_call" | custom-call | tf_op jit(solution)/shard_map/cond/branch_0_fun/product/pallas_call | solution.py:92
  7.8 14.6 %attend.4 = (bf16[512,1024]{1,0:T(8,128)(2,1)}, f32[512,1024]{1,0:T(8,128)}, bf16[16,288,256]{2,1,0:T(8,128)(2,1)}, bf16[16,288,256]{2,1,0:T(8,128)(2,1)}) custom-call(s32[1,2]{1,0:T(1,128)S(1)} %copy-done.44, bf16[512,3072]{1,0:T(8,128)(2,1)S(1)} %product.5.refs_0_.refs_1_.refs_2_, bf16[512,3072]{1,0:T(8,128)(2,1)S(1)} %product.5.refs_0_.refs_1_.refs_2_, ...), custom_call_target="tpu_custom_call" | custom-call | tf_op jit(solution)/shard_map/cond/branch_0_fun/attend/pallas_call | solution.py:293
  22.4 6.1 %dec_mid.1 = (f32[512,1024]{1,0:T(8,128)}, f32[512,128]{1,0:T(8,128)S(1)}, bf16[512,1024]{1,0:T(8,128)(2,1)}) custom-call(bf16[512,1024]{1,0:T(8,128)(2,1)} %get-tuple-element.712.x_ref, bf16[512,1024]{1,0:T(8,128)(2,1)} %get-tuple-element.736.att_ref, bf16[1024,1024]{1,0:T(8,128)(2,1)S(1)} %copy-done, f32[2,1024]{1,0:T(2,128)S(1)} %copy-done.24, ...), custom_call_target="tpu_custom_call" | custom-call | tf_op jit(solution)/shard_map/cond/branch_0_fun/dec_mid/pallas_call | solution.py:698
  38.4 17.4 %collective-permute-done = bf16[288,1024]{1,0:T(8,128)(2,1)} collective-permute-done((bf16[288,1024]{1,0:T(8,128)(2,1)}, bf16[288,1024]{1,0:T(8,128)(2,1)}, u32[]{:S(2)}, u32[]{:S(2)}) %collective-permute-start) | collective-permute-done | bytes 589856 | tf_op jit(solution)/shard_map/ppermute | solution.py:1384
  55.7 24.1 %conditional.11 = (bf16[288,1024]{1,0:T(8,128)(2,1)}, bf16[288,4096]{1,0:T(8,128)(2,1)}, bf16[288,512]{1,0:T(8,128)(2,1)}, bf16[288,512]{1,0:T(8,128)(2,1)}, bf1...) conditional(s32[]{:T(128)} %convert_element_type.4, ...), branch_computations={%region_2.3_spmd, %region_3.4_spmd} | conditional | bytes 8913032 | solution.py:1380
  60.2 4.9 %attend.6 = (bf16[256,1024]{1,0:T(8,128)(2,1)}, f32[256,1024]{1,0:T(8,128)}, bf16[16,96,256]{2,1,0:T(8,128)(2,1)}) custom-call(s32[1,2]{1,0:T(1,128)S(1)} %get-tuple-element.360.len_ref, bf16[512,1024]{1,0:T(8,128)(2,1)S(1)} %copy-done.12, bf16[288,2048]{1,0:T(8,128)(2,1)S(1)} %product.7.refs_1_.refs_2_, bf16[288,2048]{1,0:T(8,128)(2,1)S(1)} %product.7.refs_1_.refs_2_), custom_call_target="tpu_custom_call" | custom-call | tf_op jit(solution)/shard_map/cond/branch_0_fun/attend/pallas_call | solution.py:293
  81.2 4.2 %conditional.13 = (bf16[288,2048]{1,0:T(8,128)(2,1)}) conditional(s32[]{:T(128)} %convert_element_type.4, (bf16[288,1024]{1,0:T(8,128)(2,1)}, bf16[1024,2048]{1,0:T(8,128)(2,1)}) %tuple.84, () %tuple.85), branch_computations={%region_6.7_spmd, %region_7.8_spmd} | conditional | bytes 8 | solution.py:1380
  85.4 5.4 %collective-permute-done.1 = bf16[288,1024]{1,0:T(8,128)(2,1)} collective-permute-done((bf16[288,1024]{1,0:T(8,128)(2,1)}, bf16[288,1024]{1,0:T(8,128)(2,1)}, u32[]{:S(2)}, u32[]{:S(2)}) %collective-permute-start.1) | collective-permute-done | bytes 589856 | tf_op jit(solution)/shard_map/ppermute | solution.py:1384
  90.8 58.6 %conditional.14 = ((bf16[288,1024]{1,0:T(8,128)(2,1)}, bf16[288,1024]{1,0:T(8,128)(2,1)}, bf16[192,1024]{1,0:T(8,128)(2,1)}, bf16[256,1024]{1,0:T(8,128)(2,1)}, ...) conditional(s32[]{:T(128)} %convert_element_type.4, ...), branch_computations={%region_8.9_spmd, %region_9.10_spmd} | conditional | bytes 34619768 | solution.py:1380
  90.9 4.3 %product.9.refs_1_.refs_4_.refs_7_ = bf16[288,2048]{1,0:T(8,128)(2,1)} custom-call(bf16[288,1024]{1,0:T(8,128)(2,1)} %get-tuple-element.399.x_ref, bf16[1024,2048]{1,0:T(8,128)(2,1)} %get-tuple-element.400.w_ref.refs_2_), custom_call_target="tpu_custom_call" | custom-call | tf_op jit(solution)/shard_map/cond/branch_0_fun/product/pallas_call | solution.py:92
  95.3 11.7 %attend.7 = (bf16[256,1024]{1,0:T(8,128)(2,1)}, f32[256,1024]{1,0:T(8,128)}, bf16[16,768,256]{2,1,0:T(8,128)(2,1)}) custom-call(s32[1,2]{1,0:T(1,128)S(1)} %copy-done.47, bf16[512,1024]{1,0:T(8,128)(2,1)} %get-tuple-element.397.refs_0_, bf16[288,2048]{1,0:T(8,128)(2,1)} %product.9.refs_1_.refs_4_.refs_7_, bf16[288,2048]{1,0:T(8,128)(2,1)S(1)} %copy-done.10, ...), custom_call_target="tpu_custom_call" | custom-call | tf_op jit(solution)/shard_map/cond/branch_0_fun/attend/pallas_call | solution.py:293
  107.0 24.7 %dec_ffn.2 = (bf16[256,1024]{1,0:T(8,128)(2,1)}, f32[256,1024]{1,0:T(8,128)}, bf16[256,1024]{1,0:T(8,128)(2,1)}, f32[1024,512]{1,0:T(8,128)}, f32[1,512]{1,0:T(1...) custom-call(s32[1,2]{1,0:T(1,128)S(1)} %copy-done.45, f32[512,1024]{1,0:T(8,128)} %get-tuple-element.406.n_ref, ...), custom_call_target="tpu_custom_call" | custom-call | tf_op jit(solution)/shard_map/cond/branch_0_fun/dec_ffn/pallas_call | solution.py:793
  131.7 11.0 %attend_back.3 = (bf16[256,1024]{1,0:T(8,128)(2,1)}, bf16[768,1024]{1,0:T(8,128)(2,1)}, bf16[768,1024]{1,0:T(8,128)(2,1)}) custom-call(bf16[512,1024]{1,0:T(8,128)(2,1)} %get-tuple-element.397.refs_0_, bf16[256,1024]{1,0:T(8,128)(2,1)} %get-tuple-element.403.catt_ref.refs_1_, f32[256,1024]{1,0:T(8,128)} %get-tuple-element.404.refs_2_, ...), custom_call_target="tpu_custom_call" | custom-call | tf_op jit(solution)/shard_map/cond/branch_0_fun/attend_back/pallas_call | solution.py:410
  142.7 6.4 %back_product.3 = (bf16[288,1024]{1,0:T(8,128)(2,1)}, bf16[288,1024]{1,0:T(8,128)(2,1)}, bf16[192,1024]{1,0:T(8,128)(2,1)}) custom-call(bf16[768,1024]{1,0:T(8,128)(2,1)} %get-tuple-element.419.refs_0_, bf16[768,1024]{1,0:T(8,128)(2,1)} %get-tuple-element.420.refs_1_, bf16[1024,2048]{1,0:T(8,128)(2,1)S(1)} %copy-done.2), custom_call_target="tpu_custom_call" | custom-call | tf_op jit(solution)/shard_map/cond/branch_0_fun/back_product/pallas_call | solution.py:130
  155.7 34.3 %conditional.15 = ((bf16[96,1024]{1,0:T(8,128)(2,1)}, bf16[256,1024]{1,0:T(8,128)(2,1)}, f32[256,1024]{1,0:T(8,128)}, bf16[256,1024]{1,0:T(8,128)(2,1)}, f32[102...) conditional(s32[]{:T(128)} %convert_element_type.4, (s32[1,2]{1,0:T(1,128)}, ...), branch_computations={%region_10.11_spmd, %region_11.12_spmd} | conditional | bytes 18874496 | solution.py:1380
  155.7 24.8 %dec_ffn.3 = (bf16[256,1024]{1,0:T(8,128)(2,1)}, f32[256,1024]{1,0:T(8,128)}, bf16[256,1024]{1,0:T(8,128)(2,1)}, f32[1024,512]{1,0:T(8,128)}, f32[1,512]{1,0:T(1...) custom-call(s32[1,2]{1,0:T(1,128)} %get-tuple-element.434.len_ref, f32[512,1024]{1,0:T(8,128)} %get-tuple-element.435.n_ref, ...), custom_call_target="tpu_custom_call" | custom-call | tf_op jit(solution)/shard_map/cond/branch_0_fun/dec_ffn/pallas_call | solution.py:793
  180.5 6.3 %attend_back.4 = (bf16[256,1024]{1,0:T(8,128)(2,1)}, bf16[96,1024]{1,0:T(8,128)(2,1)}, bf16[96,1024]{1,0:T(8,128)(2,1)}) custom-call(bf16[512,1024]{1,0:T(8,128)(2,1)} %get-tuple-element.431.refs_0_, bf16[256,1024]{1,0:T(8,128)(2,1)S(1)} %copy-done.20, f32[256,1024]{1,0:T(8,128)} %get-tuple-element.433.refs_2_, ...), custom_call_target="tpu_custom_call" | custom-call | tf_op jit(solution)/shard_map/cond/branch_0_fun/attend_back/pallas_call | solution.py:410
  192.0 29.1 %conditional.16 = ((bf16[512,1024]{1,0:T(8,128)(2,1)S(1)}, f32[32,1024]{1,0:T(8,128)}, f32[32,1024]{1,0:T(8,128)})) conditional(s32[]{:T(128)} %convert_element_type.4, (f32[256,1024]{1,0:T(8,128)}, f32[256,1024]{1,0:T(8,128)}, bf16[256,1024]{1,0:T(8,128)(2,1)}, bf16[256,1024]{1,0:T(8,128)(2,1)}, bf16[1024,1024]{1,0:T(8,128)(2,1)}, ...), branch_computations={%region_12.13_spmd, %region_13.14_spmd} | conditional | bytes 13631576 | solution.py:1380
  192.2 8.2 %dec_mid_back.1 = (f32[512,1024]{1,0:T(8,128)}, bf16[512,1024]{1,0:T(8,128)(2,1)}) custom-call(f32[256,1024]{1,0:T(8,128)} %get-tuple-element.462.dsecond0_ref, f32[256,1024]{1,0:T(8,128)} %get-tuple-element.463.dsecond1_ref, bf16[256,1024]{1,0:T(8,128)(2,1)} %get-tuple-element.464.dcq0_ref, bf16[256,1024]{1,0:T(8,128)(2,1)} %get-tuple-element.465.dcq1_ref, ...), custom_call_target="tpu_custom_call" | custom-call | tf_op jit(solution)/shard_map/cond/branch_0_fun/dec_mid_back/pallas_call | solution.py:860
  200.4 13.8 %attend_back.5 = (bf16[512,1024]{1,0:T(8,128)(2,1)}, bf16[512,1024]{1,0:T(8,128)(2,1)}, bf16[512,1024]{1,0:T(8,128)(2,1)}, f32[32,1024]{1,0:T(8,128)}, f32[32,1024]{1,0:T(8,128)}) custom-call(bf16[512,3072]{1,0:T(8,128)(2,1)S(1)} %get-tuple-element.459.refs_0_.refs_4_.refs_5_, bf16[512,1024]{1,0:T(8,128)(2,1)S(1)} %copy-done.14, ...), custom_call_target="tpu_custom_call" | custom-call | tf_op jit(solution)/shard_map/cond/branch_0_fun/attend_back/pallas_call | solution.py:410
  214.2 6.9 %back_product.5 = bf16[512,1024]{1,0:T(8,128)(2,1)S(1)} custom-call(bf16[512,1024]{1,0:T(8,128)(2,1)} %get-tuple-element.476.refs_0_, bf16[512,1024]{1,0:T(8,128)(2,1)} %get-tuple-element.477.refs_1_, bf16[512,1024]{1,0:T(8,128)(2,1)} %get-tuple-element.478.refs_2_, bf16[1024,3072]{1,0:T(8,128)(2,1)} %get-tuple-element.479.refs_3_, ...), custom_call_target="tpu_custom_call" | custom-call | tf_op jit(solution)/shard_map/cond/branch_0_fun/back_product/pallas_call | solution.py:130
  226.7 13.9 %conditional.19 = (f32[288,1024]{1,0:T(8,128)}, bf16[288,1024]{1,0:T(8,128)(2,1)}, f32[1024,512]{1,0:T(8,128)}, f32[1,512]{1,0:T(1,128)S(1)}, f32[512,1024]{1,0:T(8,128)}, /*index=5*/f32[1,1024]{1,0:T(1,128)S(1)}) conditional(s32[]{:T(128)} %convert_element_type.4, () %tuple.96, (bf16[192,1024]{1,0:T(8,128)(2,1)}, bf16[96,1024]{1,0:T(8,128)(2,1)}, ...), branch_computations={%region_18.19_spmd, %region_19.20_spmd} | conditional | bytes 16515372 | solution.py:1380
  240.7 75.1 %finish.1 = (bf16[864,512]{1,0:T(8,128)(2,1)}, bf16[512,512]{1,0:T(8,128)(2,1)}, bf16[512,512]{1,0:T(8,128)(2,1)}, bf16[512,1024]{1,0:T(8,128)(2,1)}, bf16[1024,...) custom-call(bf16[864,3072]{1,0:T(8,128)(2,1)} %get-tuple-element.631.q_ref.k_ref.v_ref, ...), custom_call_target="tpu_custom_call" | custom-call | tf_op jit(solution)/shard_map/finish/pallas_call | solution.py:1289
  (112 shorter events, 40.5 us)
Async XLA Ops:
  7.7 14.7 %copy-start = (bf16[1024,1024]{1,0:T(8,128)(2,1)S(1)}, bf16[1024,1024]{1,0:T(8,128)(2,1)}, u32[]{:S(2)}) copy-start(bf16[1024,1024]{1,0:T(8,128)(2,1)} %get-tuple-element.312.wo_ref) | copy-start | bytes 6291460 | tf_op jit(solution)/shard_map/cond
  7.8 14.7 %copy-start.13 = (bf16[1024,1024]{1,0:T(8,128)(2,1)S(1)}, bf16[1024,1024]{1,0:T(8,128)(2,1)}, u32[]{:S(2)}) copy-start(bf16[1024,1024]{1,0:T(8,128)(2,1)} %get-tuple-element.314.wq_ref) | copy-start | bytes 6291460 | tf_op jit(solution)/shard_map/cond
  7.8 14.7 %copy-start.24 = (f32[2,1024]{1,0:T(2,128)S(1)}, f32[2,1024]{1,0:T(2,128)}, u32[]{:S(2)}) copy-start(f32[2,1024]{1,0:T(2,128)} %get-tuple-element.313.gain_ref) | copy-start | bytes 24580 | tf_op jit(solution)/shard_map/cond
  35.7 20.0 %collective-permute-start = (bf16[288,1024]{1,0:T(8,128)(2,1)}, bf16[288,1024]{1,0:T(8,128)(2,1)}, u32[]{:S(2)}, u32[]{:S(2)}) collective-permute-start(bf16[288,1024]{1,0:T(8,128)(2,1)} %get-tuple-element.634), channel_id=1, source_target_pairs={{0,16},{1,17},{2,18},{3,19},{4,20},{5,21},{6,22},{7,23},{8,24},{9,... | collective-permute-start | bytes 1769480 | tf_op jit(solution)/shard_map/ppermute | solution.py:1384
  37.0 18.7 %copy-start.46 = (s32[1,2]{1,0:T(1,128)S(1)}, s32[1,2]{1,0:T(1,128)}, u32[]{:S(2)}) copy-start(s32[1,2]{1,0:T(1,128)} %param.42) | copy-start | bytes 28
  37.1 44.1 %collective-permute-start.2 = (bf16[288,1024]{1,0:T(8,128)(2,1)}, bf16[288,1024]{1,0:T(8,128)(2,1)}, u32[]{:S(2)}, u32[]{:S(2)}) collective-permute-start(bf16[288,1024]{1,0:T(8,128)(2,1)} %get-tuple-element.637), channel_id=1, source_target_pairs={{0,16},{1,17},{2,18},{3,19},{4,20},{5,21},{6,22},{7,23},{8,24},{9,... | collective-permute-start | bytes 1769480 | tf_op jit(solution)/shard_map/ppermute | solution.py:1384
  79.9 10.9 %collective-permute-start.1 = (bf16[288,1024]{1,0:T(8,128)(2,1)}, bf16[288,1024]{1,0:T(8,128)(2,1)}, u32[]{:S(2)}, u32[]{:S(2)}) collective-permute-start(bf16[288,1024]{1,0:T(8,128)(2,1)} %get-tuple-element.636), channel_id=1, source_target_pairs={{0,16},{1,17},{2,18},{3,19},{4,20},{5,21},{6,22},{7,23},{8,24},{9,... | collective-permute-start | bytes 1769480 | tf_op jit(solution)/shard_map/ppermute | solution.py:1384
  81.2 9.6 %copy-start.23 = (f32[1,2,1024]{2,1,0:T(2,128)S(1)}, f32[1,2,1024]{2,1,0:T(2,128)}, u32[]{:S(2)}) copy-start(f32[1,2,1024]{2,1,0:T(2,128)} %param.48) | copy-start | bytes 24580
  81.2 9.6 %copy-start.39 = (f32[1,1024]{1,0:T(1,128)S(1)}, f32[1,1024]{1,0:T(1,128)}, u32[]{:S(2)}) copy-start(f32[1,1024]{1,0:T(1,128)} %param.53) | copy-start | bytes 12292
  95.2 11.8 %copy-start.7 = (bf16[1024,512]{1,0:T(8,128)(2,1)S(1)}, bf16[1024,512]{1,0:T(8,128)(2,1)}, u32[]{:S(2)}) copy-start(bf16[1024,512]{1,0:T(8,128)(2,1)} %get-tuple-element.415.down_hbm) | copy-start | bytes 3145732 | tf_op jit(solution)/shard_map/cond
  95.2 11.8 %copy-start.9 = (bf16[512,1024]{1,0:T(8,128)(2,1)S(1)}, bf16[512,1024]{1,0:T(8,128)(2,1)}, u32[]{:S(2)}) copy-start(bf16[512,1024]{1,0:T(8,128)(2,1)} %get-tuple-element.416.up_hbm) | copy-start | bytes 3145732 | tf_op jit(solution)/shard_map/cond
  95.2 11.8 %copy-start.43 = (f32[1,1024]{1,0:T(1,128)S(1)}, f32[1,1024]{1,0:T(1,128)}, u32[]{:S(2)}) copy-start(f32[1,1024]{1,0:T(1,128)} %get-tuple-element.408.cgain_ref) | copy-start | bytes 12292 | tf_op jit(solution)/shard_map/cond
  95.3 11.7 %copy-start.45 = (s32[1,2]{1,0:T(1,128)S(1)}, s32[1,2]{1,0:T(1,128)}, u32[]{:S(2)}) copy-start(s32[1,2]{1,0:T(1,128)} %get-tuple-element.405.len_ref) | copy-start | bytes 28 | tf_op jit(solution)/shard_map/cond
  131.7 11.0 %copy-start.2 = (bf16[1024,2048]{1,0:T(8,128)(2,1)S(1)}, bf16[1024,2048]{1,0:T(8,128)(2,1)}, u32[]{:S(2)}) copy-start(bf16[1024,2048]{1,0:T(8,128)(2,1)} %get-tuple-element.400.w_ref.refs_2_) | copy-start | bytes 12582916 | tf_op jit(solution)/shard_map/cond
  149.5 71.7 %collective-permute-start.3 = (bf16[288,1024]{1,0:T(8,128)(2,1)}, bf16[288,1024]{1,0:T(8,128)(2,1)}, u32[]{:S(2)}, u32[]{:S(2)}) collective-permute-start(bf16[288,1024]{1,0:T(8,128)(2,1)} %get-tuple-element.640), channel_id=1, source_target_pairs={{16,0},{17,1},{18,2},{19,3},{20,4},{21,5},{22,6},{23,7},{24,8},{25... | collective-permute-start | bytes 1769480 | tf_op jit(solution)/shard_map/ppermute | solution.py:1388
  151.6 69.8 %collective-permute-start.4 = (bf16[288,1024]{1,0:T(8,128)(2,1)}, bf16[288,1024]{1,0:T(8,128)(2,1)}, u32[]{:S(2)}, u32[]{:S(2)}) collective-permute-start(bf16[288,1024]{1,0:T(8,128)(2,1)} %get-tuple-element.661), channel_id=1, source_target_pairs={{16,0},{17,1},{18,2},{19,3},{20,4},{21,5},{22,6},{23,7},{24,8},{25... | collective-permute-start | bytes 1769480 | tf_op jit(solution)/shard_map/ppermute | solution.py:1388
  153.7 72.9 %collective-permute-start.5 = (bf16[192,1024]{1,0:T(8,128)(2,1)}, bf16[192,1024]{1,0:T(8,128)(2,1)}, u32[]{:S(2)}, u32[]{:S(2)}) collective-permute-start(bf16[192,1024]{1,0:T(8,128)(2,1)} %get-tuple-element.667), channel_id=1, source_target_pairs={{16,0},{17,1},{18,2},{19,3},{20,4},{21,5},{22,6},{23,7},{24,8},{25... | collective-permute-start | bytes 1179656 | tf_op jit(solution)/shard_map/ppermute | solution.py:1388
  155.7 24.8 %copy-start.20 = (bf16[256,1024]{1,0:T(8,128)(2,1)S(1)}, bf16[256,1024]{1,0:T(8,128)(2,1)}, u32[]{:S(2)}) copy-start(bf16[256,1024]{1,0:T(8,128)(2,1)} %get-tuple-element.432.catt_ref.refs_1_) | copy-start | bytes 1572868 | tf_op jit(solution)/shard_map/cond
  190.1 36.6 %collective-permute-start.6 = (bf16[96,1024]{1,0:T(8,128)(2,1)}, bf16[96,1024]{1,0:T(8,128)(2,1)}, u32[]{:S(2)}, u32[]{:S(2)}) collective-permute-start(bf16[96,1024]{1,0:T(8,128)(2,1)} %get-tuple-element.668), channel_id=1, source_target_pairs={{16,0},{17,1},{18,2},{19,3},{20,4},{21,5},{22,6},{23,7},{24,8},{25... | collective-permute-start | bytes 589832 | tf_op jit(solution)/shard_map/ppermute | solution.py:1388
  226.7 14.0 %copy-start.11 = (bf16[864,1024]{1,0:T(8,128)(2,1)S(1)}, bf16[864,1024]{1,0:T(8,128)(2,1)}, u32[]{:S(2)}) copy-start(bf16[864,1024]{1,0:T(8,128)(2,1)} %get-tuple-element.632.o_ref) | copy-start | bytes 5308420
  226.7 14.0 %copy-start.48 = (f32[1,1024]{1,0:T(1,128)S(1)}, f32[1,1024]{1,0:T(1,128)}, u32[]{:S(2)}) copy-start(f32[1,1024]{1,0:T(1,128)} %get-tuple-element.693.long_upb) | copy-start | bytes 12292
  226.7 14.0 %copy-start.49 = (f32[1,1024]{1,0:T(1,128)S(1)}, f32[1,1024]{1,0:T(1,128)}, u32[]{:S(2)}) copy-start(f32[1,1024]{1,0:T(1,128)} %get-tuple-element.697.short_upb) | copy-start | bytes 12292
  226.7 14.0 %copy-start.51 = (f32[1,512]{1,0:T(1,128)S(1)}, f32[1,512]{1,0:T(1,128)}, u32[]{:S(2)}) copy-start(f32[1,512]{1,0:T(1,128)} %get-tuple-element.691.long_downb) | copy-start | bytes 6148
  226.7 14.0 %copy-start.52 = (f32[1,512]{1,0:T(1,128)S(1)}, f32[1,512]{1,0:T(1,128)}, u32[]{:S(2)}) copy-start(f32[1,512]{1,0:T(1,128)} %get-tuple-element.695.short_downb) | copy-start | bytes 6148
  (22 other events, 86.3 us)

commit v3 on v2

--- a/solution.py
+++ b/solution.py
@@ -489,14 +489,17 @@
     low_ref[...] = normed.astype(BF)
     scales_ref[:, 0:1] = scale
 
-    for part in range(in_ref.shape[1] // wide):
+    def one_part(part, carry):
         weights.wait("in", part)
         weights.wait("out", part)
-        cols = slice(part * wide, (part + 1) * wide)
+        cols = pl.ds(pl.multiple_of(part * wide, wide), wide)
         ffn_step(
             low_ref, acc_ref, in_ref.at[:, cols], out_ref.at[cols], slope_ref.at[:, cols],
             None, None, None,
         )
+        return carry
+
+    lax.fori_loop(0, in_ref.shape[1] // wide, one_part, 0)
 
     weights.wait("down")
     weights.wait("up")
@@ -604,13 +607,16 @@
     weights.wait("down")
     acc_ref[...] = grad + nt(pre, down_ref[...])
 
-    for part in range(in_ref.shape[1] // wide):
+    def one_part(part, carry):
         weights.wait("out", part)
         weights.wait("in", part)
-        cols = slice(part * wide, (part + 1) * wide)
+        cols = pl.ds(pl.multiple_of(part * wide, wide), wide)
         ffn_back_step(
             grad_ref, acc_ref, in_ref.at[:, cols], out_ref.at[cols], slope_ref.at[:, cols]
         )
+        return carry
+
+    lax.fori_loop(0, in_ref.shape[1] // wide, one_part, 0)
 
     gain = gain_ref[0:1]
     hat = low_ref[...].astype(F32) / gain
@@ -927,7 +933,7 @@
     y0_ref, y1_ref, dt_ref,
     source_ref, y_ref, target_ref, o_up_ref, o_down_ref, o_prefix_ref, o_upb_ref, o_downb_ref,
     dq, dk, dv, small, ups, downs, mine, theirs, half_sum, across_y, y_sum, landed, total, result,
-    small_landed, small_total, small_result, dx_low, dx_high, dx_landed, lows, lows_landed,
+    small_landed, small_total, small_result, dx, dx_landed, lows, lows_landed,
     load_sems, pair_sems, y_sems, z_sems, gather_sems, share_y_sems, back_sems,
     small_sems, share_sems, cross_sems,
     *, devices,
@@ -1044,7 +1050,7 @@
 
     def send_high(i):
         return remote(
-            dx_high.at[i], dx_landed.at[i], cross_sems.at[0, 1 + i], cross_sems.at[1, 1 + i], across
+            dx.at[i], dx_landed.at[i], cross_sems.at[0, 1 + i], cross_sems.at[1, 1 + i], across
         )
 
     def greet(barrier, other):
@@ -1192,18 +1198,18 @@
     def _():
         pl.semaphore_wait(pltpu.get_barrier_semaphore(), 1)
 
-    for i in range(4):
+    @pl.when(is_encoder & (step >= pairs))
+    def _():
+        acc = jnp.concatenate([dfirst0_ref[...], dfirst1_ref[...], dfirst2_ref[...]], 0)
+        for n, grad in enumerate((dq, dk, dv)):
+            acc = acc + nt(grad[...], wqkv_ref[:, n * width : (n + 1) * width])
+        dx[step - pairs] = acc.astype(BF)
+
+    for i in range(2):
 
         @pl.when(is_encoder & (step == pairs + i))
         def _(i=i):
-            acc = jnp.concatenate([dfirst0_ref[...], dfirst1_ref[...], dfirst2_ref[...]], 0)
-            for n, grad in enumerate((dq, dk, dv)):
-                acc = acc + nt(grad[...], wqkv_ref[:, n * width : (n + 1) * width])
-            if i < 2:
-                dx_high[i] = acc.astype(BF)
-                send_high(i).start()
-            else:
-                dx_low[:, (i - 2) * tile : (i - 1) * tile] = acc.astype(BF)
+            send_high(i).start()
 
     @pl.when(step == pairs + 1)
     def _():
@@ -1234,7 +1240,8 @@
 
         @pl.when(is_encoder)
         def _():
-            source_ref[...] = dx_low[...]
+            for i in range(2):
+                source_ref[:, i * tile : (i + 1) * tile] = dx[2 + i]
             send_low().wait_recv()
             y_ref[...] = lows_landed[0]
             target_ref[...] = lows_landed[1]
@@ -1330,7 +1337,7 @@
             vmem((width, width), BF),
             vmem((devices - 1, small_rows, small_cols), F32), vmem((small_rows, small_cols), F32),
             vmem((2 * PRE_PAD, width), F32),
-            vmem((rows, half), BF), vmem((2, rows, tile), BF), vmem((2, rows, tile), BF),
+            vmem((4, rows, tile), BF), vmem((2, rows, tile), BF),
             vmem((2, targets, half), BF), vmem((2, targets, half), BF),
             dma((4,)), dma((2,)), dma((2, slices)), dma((2, slices, line - 1)),
             dma((2, slices, line - 1)), dma((2, slices)), dma((2, slices, 2)),
@@ -1429,12 +1436,16 @@
     part1 = at_encoder(lambda saved: enc_ffn(sources, saved[1], w, 1), saved)
     mem1 = to_decoder(part1[0])
 
-    def decoder_short(saved, mem2, cq):
+    def decoder_short(saved, mem2, cq, kept):
         kv2 = product(mem2, cross["pairs"])
-        return kv2, cross_forward(source_lengths, cq, [kv2], 1)
-
-    part0, (kv2, short) = at_both(
-        lambda saved, mem2, cq: enc_ffn(sources, saved[1], w, 0), decoder_short, saved, mem2, cq
+        forward = cross_forward(source_lengths, cq, [kv2], 1)
+        return kv2, forward, dec_ffn(
+            target_lengths, kept[4], forward[0], cotangent, w, cross, 1
+        )
+
+    part0, (kv2, short, short_ffn) = at_both(
+        lambda saved, *a: enc_ffn(sources, saved[1], w, 0),
+        decoder_short, saved, mem2, cq, kept,
     )
     mem0 = to_decoder(part0[0])
     kv1 = at_decoder(lambda mem1: product(mem1, cross["pairs"]), mem1)
@@ -1452,21 +1463,18 @@
     dmems, *long = at_decoder(decoder_long, mem0, kv1, kv2, cq, kept)
     dmem0, dmem1, dmem2 = [to_encoder(block) for block in dmems]
 
-    def decoder_short_back(kv2, cq, kept, short):
-        y, dsecond, dcatt, *adapter = dec_ffn(
-            target_lengths, kept[4], short[0], cotangent, w, cross, 1
-        )
+    def decoder_short_back(kv2, cq, short, dcatt):
         dcq, dck, dcv = cross_backward(cq, [kv2], short, dcatt, 1)
-        return back_product([dck, dcv], cross["pairs"])[0], y, dsecond, dcq, adapter
-
-    dmem_short, *short = at_decoder(decoder_short_back, kv2, cq, kept, short)
+        return back_product([dck, dcv], cross["pairs"])[0], dcq
+
+    short_y, short_second, short_dcatt, *short_adapter = short_ffn
+    dmem_short, short_cq = at_decoder(decoder_short_back, kv2, cq, short, short_dcatt)
     dmem_short = to_encoder(dmem_short)
 
     def decoder_end(kept, *grads):
         return decoder_self_back(kept, grads[:2], grads[2:], w, cross)
 
     (long_y, long_second, long_cq, long_adapter) = long
-    (short_y, short_second, short_cq, short_adapter) = short
     dt, dec_prefix = at_decoder(
         decoder_end, kept, long_second, short_second, long_cq, short_cq
     )

time: 331 us -> 319 us (0.964)
  the two profiles are of different devices: /device:TPU:27 before, /device:TPU:0 now
where the time goes in v3:
time: 319 us; the launch traced here: 315 us
  Pallas kernels  188 us (59%)
  waiting for transfers between devices  83.1 us (26%)
  starting transfers between devices  29.2 us (9%)
  local copies, waits for them, and re-layouts  6.69 us (2%)
  other arithmetic  4.4 us (1%)
    ppermute x4, waiting for transfers between devices, to_encoder(): return lax.ppermute(block, 'section', [(1, 0)])  71.1 us
    pallas_call x1, Pallas kernels, finish(): pl.pallas_call(functools.partial(finish_kernel, devices=devices), grid=(p...  61.8 us
    pallas_call x3, Pallas kernels, enc_ffn(): pl.pallas_call(enc_ffn_kernel, grid=(1,), in_specs=[pl.BlockSpec((rows, w...  43.4 us
    pallas_call x3, Pallas kernels, enc_ffn_back(): pl.pallas_call(functools.partial(enc_ffn_back_kernel, pieces=len(dmems)),...  40.7 us
    pallas_call x1, Pallas kernels, attend(): pl.pallas_call(functools.partial(attend_kernel, group=group, segs=segs, p...  27.5 us
    ppermute x3, starting transfers between devices, to_decoder(): return lax.ppermute(block, 'section', [(0, 1)])  24.1 us
    ppermute x3, waiting for transfers between devices, to_decoder(): return lax.ppermute(block, 'section', [(0, 1)])  12.1 us
    pallas_call x1, Pallas kernels, product(): pl.pallas_call(product_kernel, grid=(width // tile,), in_specs=[whole((ro...  9.64 us
  transfers between devices with their start and end apart: 7, of which 2 were waited for; matrix products, arithmetic and copies ran while one was open for 0% of the time, Pallas kernels for 18%

profile of v3, /device:TPU:0, one launch (start us, length us, event | category | flops | bytes accessed | tf_op | source)
XLA Modules:
  0.0 314.8 jit_solution(2741907710968627666)
XLA Ops:
  1.6 51.9 %conditional.10 = (bf16[864,3072]{1,0:T(8,128)(2,1)}, bf16[864,1024]{1,0:T(8,128)(2,1)}, f32[864,1024]{1,0:T(8,128)}, bf16[16,800,768]{2,1,0:T(8,128)(2,1)}, bf1...) conditional(s32[]{:T(128)} %convert_element_type.4, ...), branch_computations={%region_0.1_spmd, %region_1.2_spmd} | conditional | bytes 16834940 | solution.py:1387
  1.8 9.6 %product.6.refs_0_.refs_1_.refs_2_ = bf16[864,3072]{1,0:T(8,128)(2,1)} custom-call(bf16[864,1024]{1,0:T(8,128)(2,1)} %get-tuple-element.323.x_ref, bf16[1024,3072]{1,0:T(8,128)(2,1)} %get-tuple-element.324.w_ref), custom_call_target="tpu_custom_call" | custom-call | tf_op jit(solution)/shard_map/cond/branch_1_fun/product/pallas_call | solution.py:92
  11.5 27.5 %attend.5 = (bf16[864,1024]{1,0:T(8,128)(2,1)}, f32[864,1024]{1,0:T(8,128)}, bf16[16,800,768]{2,1,0:T(8,128)(2,1)}, bf16[16,128,96]{2,1,0:T(8,128)(2,1)}) custom-call(s32[1,2]{1,0:T(1,128)S(1)} %copy-done.51, bf16[864,3072]{1,0:T(8,128)(2,1)} %product.6.refs_0_.refs_1_.refs_2_, bf16[864,3072]{1,0:T(8,128)(2,1)} %product.6.refs_0_.refs_1_.refs_2_, ...), custom_call_target="tpu_custom_call" | custom-call | tf_op jit(solution)/shard_map/cond/branch_1_fun/attend/pallas_call | solution.py:293
  39.1 14.4 %enc_ffn.3 = (bf16[288,1024]{1,0:T(8,128)(2,1)}, bf16[288,4096]{1,0:T(8,128)(2,1)}, bf16[288,512]{1,0:T(8,128)(2,1)}, bf16[288,512]{1,0:T(8,128)(2,1)}, bf16[288,1024]{1,0:T(8,128)(2,1)}, /*index=5*/f32[288,128]{1,0:T(8,128)}) custom-call(bf16[864,1024]{1,0:T(8,128)(2,1)} %get-tuple-element.323.x_ref, bf16[864,1024]{1,0:T(8,128)(2,1)} %get-tuple-element.755.att_ref, ...), custom_call_target="tpu_custom_call" | custom-call | tf_op jit(solution)/shard_map/cond/branch_1_fun/enc_ffn/pallas_call | solution.py:518
  53.5 2.2 collective-permute-start
  55.7 14.8 %conditional.12 = ((bf16[288,1024]{1,0:T(8,128)(2,1)}, bf16[288,4096]{1,0:T(8,128)(2,1)}, bf16[288,512]{1,0:T(8,128)(2,1)}, bf16[288,512]{1,0:T(8,128)(2,1)}, bf...) conditional(s32[]{:T(128)} %convert_element_type.4, () %tuple.83, (bf16[864,1024]{1,0:T(8,128)(2,1)}, ...), branch_computations={%region_4.5_spmd, %region_5.6_spmd} | conditional | bytes 8 | solution.py:1387
  56.1 14.4 %enc_ffn.5 = (bf16[288,1024]{1,0:T(8,128)(2,1)}, bf16[288,4096]{1,0:T(8,128)(2,1)}, bf16[288,512]{1,0:T(8,128)(2,1)}, bf16[288,512]{1,0:T(8,128)(2,1)}, bf16[288,1024]{1,0:T(8,128)(2,1)}, /*index=5*/f32[288,128]{1,0:T(8,128)}) custom-call(bf16[864,1024]{1,0:T(8,128)(2,1)} %get-tuple-element.413.x_ref, bf16[864,1024]{1,0:T(8,128)(2,1)} %get-tuple-element.414.att_ref, ...), custom_call_target="tpu_custom_call" | custom-call | tf_op jit(solution)/shard_map/cond/branch_1_fun/enc_ffn/pallas_call | solution.py:518
  70.5 2.1 collective-permute-start.2
  72.7 14.7 %conditional.11 = (bf16[288,1024]{1,0:T(8,128)(2,1)}, bf16[288,4096]{1,0:T(8,128)(2,1)}, bf16[288,512]{1,0:T(8,128)(2,1)}, bf16[288,512]{1,0:T(8,128)(2,1)}, bf1...) conditional(s32[]{:T(128)} %convert_element_type.4, ...), branch_computations={%region_2.3_spmd, %region_3.4_spmd} | conditional | bytes 19456360 | solution.py:1387
  72.9 14.5 %enc_ffn.4 = (bf16[288,1024]{1,0:T(8,128)(2,1)}, bf16[288,4096]{1,0:T(8,128)(2,1)}, bf16[288,512]{1,0:T(8,128)(2,1)}, bf16[288,512]{1,0:T(8,128)(2,1)}, bf16[288,1024]{1,0:T(8,128)(2,1)}, /*index=5*/f32[288,128]{1,0:T(8,128)}) custom-call(bf16[864,1024]{1,0:T(8,128)(2,1)} %get-tuple-element.386.x_ref, bf16[864,1024]{1,0:T(8,128)(2,1)} %get-tuple-element.387.att_ref, ...), custom_call_target="tpu_custom_call" | custom-call | tf_op jit(solution)/shard_map/cond/branch_1_fun/enc_ffn/pallas_call | solution.py:518
  87.3 19.8 %collective-permute-start.1 = (bf16[288,1024]{1,0:T(8,128)(2,1)}, bf16[288,1024]{1,0:T(8,128)(2,1)}, u32[]{:S(2)}, u32[]{:S(2)}) collective-permute-start(bf16[288,1024]{1,0:T(8,128)(2,1)} %get-tuple-element.648), channel_id=1, source_target_pairs={{0,16},{1,17},{2,18},{3,19},{4,20},{5,21},{6,22},{7,23},{8,24},{9,... | collective-permute-start | bytes 1769480 | tf_op jit(solution)/shard_map/ppermute | solution.py:1391
  107.2 12.1 %collective-permute-done.1 = bf16[288,1024]{1,0:T(8,128)(2,1)} collective-permute-done((bf16[288,1024]{1,0:T(8,128)(2,1)}, bf16[288,1024]{1,0:T(8,128)(2,1)}, u32[]{:S(2)}, u32[]{:S(2)}) %collective-permute-start.1) | collective-permute-done | bytes 589856 | tf_op jit(solution)/shard_map/ppermute | solution.py:1391
  124.9 71.1 %collective-permute-done.3 = bf16[288,1024]{1,0:T(8,128)(2,1)} collective-permute-done((bf16[288,1024]{1,0:T(8,128)(2,1)}, bf16[288,1024]{1,0:T(8,128)(2,1)}, u32[]{:S(2)}, u32[]{:S(2)}) %collective-permute-start.3) | collective-permute-done | bytes 589856 | tf_op jit(solution)/shard_map/ppermute | solution.py:1395
  196.0 13.5 %conditional.17 = ((f32[288,1024]{1,0:T(8,128)}, bf16[288,1024]{1,0:T(8,128)(2,1)}, bf16[288,1024]{1,0:T(8,128)(2,1)}, bf16[288,512]{1,0:T(8,128)(2,1)})) conditional(s32[]{:T(128)} %convert_element_type.4, () %tuple.80, (bf16[288,1024]{1,0:T(8,128)(2,1)}, bf16[288,1024]{1,0:T(8,128)(2,1)}, bf16[288,1024]{1,0:T(8,128)(2,1)}, ...), branch_computations={%region_14.15_spmd, %region_15.16_spmd} | conditional | bytes 8 | solution.py:1387
  196.0 13.5 %enc_ffn_back.3 = (f32[288,1024]{1,0:T(8,128)}, bf16[288,1024]{1,0:T(8,128)(2,1)}, bf16[288,1024]{1,0:T(8,128)(2,1)}, bf16[288,512]{1,0:T(8,128)(2,1)}) custom-call(bf16[288,1024]{1,0:T(8,128)(2,1)} %get-tuple-element.493.refs_0_, bf16[288,1024]{1,0:T(8,128)(2,1)} %get-tuple-element.494.refs_1_, bf16[288,1024]{1,0:T(8,128)(2,1)} %get-tuple-element.495.refs_2_, ...), custom_call_target="tpu_custom_call" | custom-call | tf_op jit(solution)/shard_map/cond/branch_1_fun/enc_ffn_back/pallas_call | solution.py:635
  209.6 13.2 %conditional.18 = ((f32[288,1024]{1,0:T(8,128)}, bf16[288,1024]{1,0:T(8,128)(2,1)}, bf16[288,1024]{1,0:T(8,128)(2,1)}, bf16[288,512]{1,0:T(8,128)(2,1)})) conditional(s32[]{:T(128)} %convert_element_type.4, () %tuple.94, (bf16[288,1024]{1,0:T(8,128)(2,1)}, bf16[288,1024]{1,0:T(8,128)(2,1)S(1)}, bf16[288,1024]{1,0:T(8,128)(2,1)S(1)}, ...), branch_computations={%region_16.17_spmd, %region_17.18_spmd} | conditional | bytes 8 | solution.py:1387
  209.8 13.0 %enc_ffn_back.4 = (f32[288,1024]{1,0:T(8,128)}, bf16[288,1024]{1,0:T(8,128)(2,1)}, bf16[288,1024]{1,0:T(8,128)(2,1)}, bf16[288,512]{1,0:T(8,128)(2,1)}) custom-call(bf16[288,1024]{1,0:T(8,128)(2,1)} %get-tuple-element.505.refs_0_, bf16[288,1024]{1,0:T(8,128)(2,1)S(1)} %get-tuple-element.506.refs_1_, bf16[288,1024]{1,0:T(8,128)(2,1)S(1)} %get-tuple-element.507.refs_2_, ...), custom_call_target="tpu_custom_call" | custom-call | tf_op jit(solution)/shard_map/cond/branch_1_fun/enc_ffn_back/pallas_call | solution.py:635
  222.9 19.8 %conditional.19 = (f32[288,1024]{1,0:T(8,128)}, bf16[288,1024]{1,0:T(8,128)(2,1)}, f32[1024,512]{1,0:T(8,128)}, f32[1,512]{1,0:T(1,128)S(1)}, f32[512,1024]{1,0:T(8,128)}, /*index=5*/f32[1,1024]{1,0:T(1,128)S(1)}) conditional(s32[]{:T(128)} %convert_element_type.4, () %tuple.96, (bf16[192,1024]{1,0:T(8,128)(2,1)}, bf16[96,1024]{1,0:T(8,128)(2,1)S(1)}, ...), branch_computations={%region_18.19_spmd, %region_19.20_spmd} | conditional | bytes 16515372 | solution.py:1387
  223.0 14.2 %enc_ffn_back.5 = (f32[288,1024]{1,0:T(8,128)}, bf16[288,1024]{1,0:T(8,128)(2,1)}, bf16[288,1024]{1,0:T(8,128)(2,1)}, bf16[288,512]{1,0:T(8,128)(2,1)}) custom-call(bf16[192,1024]{1,0:T(8,128)(2,1)} %get-tuple-element.523.refs_0_, bf16[96,1024]{1,0:T(8,128)(2,1)S(1)} %get-tuple-element.524.refs_1_, bf16[288,1024]{1,0:T(8,128)(2,1)} %get-tuple-element.525.refs_2_, ...), custom_call_target="tpu_custom_call" | custom-call | tf_op jit(solution)/shard_map/cond/branch_1_fun/enc_ffn_back/pallas_call | solution.py:635
  237.3 5.2 %adapter_grads.1 = (f32[1024,512]{1,0:T(8,128)}, f32[1,512]{1,0:T(1,128)S(1)}, f32[512,1024]{1,0:T(8,128)}, f32[1,1024]{1,0:T(1,128)S(1)}) custom-call(bf16[288,1024]{1,0:T(8,128)(2,1)S(1)} %copy-done.19, bf16[288,1024]{1,0:T(8,128)(2,1)S(1)} %copy-done.21, bf16[288,1024]{1,0:T(8,128)(2,1)S(1)} %copy-done.18, bf16[288,512]{1,0:T(8,128)(2,1)S(1)} %copy-done.35, ...), custom_call_target="tpu_custom_call" | custom-call | tf_op jit(solution)/shard_map/cond/branch_1_fun/adapter_grads/pallas_call | solution.py:678
  242.7 61.8 %finish.1 = (bf16[864,512]{1,0:T(8,128)(2,1)}, bf16[512,512]{1,0:T(8,128)(2,1)}, bf16[512,512]{1,0:T(8,128)(2,1)}, bf16[512,1024]{1,0:T(8,128)(2,1)}, bf16[1024,...) custom-call(bf16[864,3072]{1,0:T(8,128)(2,1)} %get-tuple-element.642.q_ref.k_ref.v_ref, ...), custom_call_target="tpu_custom_call" | custom-call | tf_op jit(solution)/shard_map/finish/pallas_call | solution.py:1296
  304.6 1.9 copy.29
  306.5 2.8 bitcast_convert_fusion.1
  309.3 1.6 bitcast_convert_fusion
  (98 shorter events, 10.4 us)
Async XLA Ops:
  11.4 27.6 %copy-start.1 = (bf16[1024,1024]{1,0:T(8,128)(2,1)S(1)}, bf16[1024,1024]{1,0:T(8,128)(2,1)}, u32[]{:S(2)}) copy-start(bf16[1024,1024]{1,0:T(8,128)(2,1)} %get-tuple-element.335.wo_hbm) | copy-start | bytes 6291460 | tf_op jit(solution)/shard_map/cond
  11.4 27.6 %copy-start.6 = (bf16[1024,512]{1,0:T(8,128)(2,1)S(1)}, bf16[1024,512]{1,0:T(8,128)(2,1)}, u32[]{:S(2)}) copy-start(bf16[1024,512]{1,0:T(8,128)(2,1)} %get-tuple-element.338.down_hbm) | copy-start | bytes 3145732 | tf_op jit(solution)/shard_map/cond
  11.5 27.6 %copy-start.9 = (bf16[512,1024]{1,0:T(8,128)(2,1)S(1)}, bf16[512,1024]{1,0:T(8,128)(2,1)}, u32[]{:S(2)}) copy-start(bf16[512,1024]{1,0:T(8,128)(2,1)} %get-tuple-element.339.up_hbm) | copy-start | bytes 3145732 | tf_op jit(solution)/shard_map/cond
  11.5 27.6 %copy-start.27 = (f32[2,1024]{1,0:T(2,128)S(1)}, f32[2,1024]{1,0:T(2,128)}, u32[]{:S(2)}) copy-start(f32[2,1024]{1,0:T(2,128)} %get-tuple-element.332.gain_ref) | copy-start | bytes 24580 | tf_op jit(solution)/shard_map/cond
  11.5 27.6 %copy-start.42 = (f32[1,1024]{1,0:T(1,128)S(1)}, f32[1,1024]{1,0:T(1,128)}, u32[]{:S(2)}) copy-start(f32[1,1024]{1,0:T(1,128)} %get-tuple-element.334.upb_ref) | copy-start | bytes 12292 | tf_op jit(solution)/shard_map/cond
  11.5 27.6 %copy-start.45 = (f32[1,512]{1,0:T(1,128)S(1)}, f32[1,512]{1,0:T(1,128)}, u32[]{:S(2)}) copy-start(f32[1,512]{1,0:T(1,128)} %get-tuple-element.333.downb_ref) | copy-start | bytes 6148 | tf_op jit(solution)/shard_map/cond
  53.5 19.1 %collective-permute-start = (bf16[288,1024]{1,0:T(8,128)(2,1)}, bf16[288,1024]{1,0:T(8,128)(2,1)}, u32[]{:S(2)}, u32[]{:S(2)}) collective-permute-start(bf16[288,1024]{1,0:T(8,128)(2,1)} %get-tuple-element.645), channel_id=1, source_target_pairs={{0,16},{1,17},{2,18},{3,19},{4,20},{5,21},{6,22},{7,23},{8,24},{9,... | collective-permute-start | bytes 1769480 | tf_op jit(solution)/shard_map/ppermute | solution.py:1391
  55.7 17.0 %copy-start.47 = (f32[1024]{0:T(1024)S(1)}, f32[1024]{0:T(1024)}, u32[]{:S(2)}) copy-start(f32[1024]{0:T(1024)} %param.57) | copy-start | bytes 12292
  55.7 17.0 %copy-start.48 = (s32[1,2]{1,0:T(1,128)S(1)}, s32[1,2]{1,0:T(1,128)}, u32[]{:S(2)}) copy-start(s32[1,2]{1,0:T(1,128)} %param.43) | copy-start | bytes 28
  55.7 17.0 %copy-start.50 = (s32[1,2]{1,0:T(1,128)S(1)}, s32[1,2]{1,0:T(1,128)}, u32[]{:S(2)}) copy-start(s32[1,2]{1,0:T(1,128)} %param.42) | copy-start | bytes 28
  70.5 36.6 %collective-permute-start.2 = (bf16[288,1024]{1,0:T(8,128)(2,1)}, bf16[288,1024]{1,0:T(8,128)(2,1)}, u32[]{:S(2)}, u32[]{:S(2)}) collective-permute-start(bf16[288,1024]{1,0:T(8,128)(2,1)} %get-tuple-element.649), channel_id=1, source_target_pairs={{0,16},{1,17},{2,18},{3,19},{4,20},{5,21},{6,22},{7,23},{8,24},{9,... | collective-permute-start | bytes 1769480 | tf_op jit(solution)/shard_map/ppermute | solution.py:1391
  87.3 31.9 %collective-permute-start.1 = (bf16[288,1024]{1,0:T(8,128)(2,1)}, bf16[288,1024]{1,0:T(8,128)(2,1)}, u32[]{:S(2)}, u32[]{:S(2)}) collective-permute-start(bf16[288,1024]{1,0:T(8,128)(2,1)} %get-tuple-element.648), channel_id=1, source_target_pairs={{0,16},{1,17},{2,18},{3,19},{4,20},{5,21},{6,22},{7,23},{8,24},{9,... | collective-permute-start | bytes 1769480 | tf_op jit(solution)/shard_map/ppermute | solution.py:1391
  119.7 76.3 %collective-permute-start.3 = (bf16[288,1024]{1,0:T(8,128)(2,1)}, bf16[288,1024]{1,0:T(8,128)(2,1)}, u32[]{:S(2)}, u32[]{:S(2)}) collective-permute-start(bf16[288,1024]{1,0:T(8,128)(2,1)} %get-tuple-element.651), channel_id=1, source_target_pairs={{16,0},{17,1},{18,2},{19,3},{20,4},{21,5},{22,6},{23,7},{24,8},{25... | collective-permute-start | bytes 1769480 | tf_op jit(solution)/shard_map/ppermute | solution.py:1395
  121.0 88.6 %collective-permute-start.4 = (bf16[288,1024]{1,0:T(8,128)(2,1)}, bf16[288,1024]{1,0:T(8,128)(2,1)}, u32[]{:S(2)}, u32[]{:S(2)}) collective-permute-start(bf16[288,1024]{1,0:T(8,128)(2,1)} %get-tuple-element.673), channel_id=1, source_target_pairs={{16,0},{17,1},{18,2},{19,3},{20,4},{21,5},{22,6},{23,7},{24,8},{25... | collective-permute-start | bytes 1769480 | tf_op jit(solution)/shard_map/ppermute | solution.py:1395
  122.3 100.6 %collective-permute-start.5 = (bf16[192,1024]{1,0:T(8,128)(2,1)}, bf16[192,1024]{1,0:T(8,128)(2,1)}, u32[]{:S(2)}, u32[]{:S(2)}) collective-permute-start(bf16[192,1024]{1,0:T(8,128)(2,1)} %get-tuple-element.679), channel_id=1, source_target_pairs={{16,0},{17,1},{18,2},{19,3},{20,4},{21,5},{22,6},{23,7},{24,8},{25... | collective-permute-start | bytes 1179656 | tf_op jit(solution)/shard_map/ppermute | solution.py:1395
  123.6 99.2 %collective-permute-start.6 = (bf16[96,1024]{1,0:T(8,128)(2,1)}, bf16[96,1024]{1,0:T(8,128)(2,1)S(1)}, u32[]{:S(2)}, u32[]{:S(2)}) collective-permute-start(bf16[96,1024]{1,0:T(8,128)(2,1)} %get-tuple-element.680), channel_id=1, source_target_pairs={{16,0},{17,1},{18,2},{19,3},{20,4},{21,5},{22,6},{23,7},{24,8},{25... | collective-permute-start | bytes 589832 | tf_op jit(solution)/shard_map/ppermute | solution.py:1395
  222.9 19.8 %copy-start.13 = (bf16[864,1024]{1,0:T(8,128)(2,1)S(1)}, bf16[864,1024]{1,0:T(8,128)(2,1)}, u32[]{:S(2)}) copy-start(bf16[864,1024]{1,0:T(8,128)(2,1)} %get-tuple-element.643.o_ref) | copy-start | bytes 5308420
  222.9 19.8 %copy-start.52 = (f32[1,1024]{1,0:T(1,128)S(1)}, f32[1,1024]{1,0:T(1,128)}, u32[]{:S(2)}) copy-start(f32[1,1024]{1,0:T(1,128)} %get-tuple-element.709.short_upb) | copy-start | bytes 12292
  222.9 19.8 %copy-start.54 = (f32[1,512]{1,0:T(1,128)S(1)}, f32[1,512]{1,0:T(1,128)}, u32[]{:S(2)}) copy-start(f32[1,512]{1,0:T(1,128)} %get-tuple-element.707.short_downb) | copy-start | bytes 6148
  222.9 14.3 %copy-start.18 = (bf16[288,1024]{1,0:T(8,128)(2,1)S(1)}, bf16[288,1024]{1,0:T(8,128)(2,1)}, u32[]{:S(2)}) copy-start(bf16[288,1024]{1,0:T(8,128)(2,1)} %get-tuple-element.526.refs_3_.refs_2_) | copy-start | bytes 1769476 | tf_op jit(solution)/shard_map/cond
  222.9 14.3 %copy-start.19 = (bf16[288,1024]{1,0:T(8,128)(2,1)S(1)}, bf16[288,1024]{1,0:T(8,128)(2,1)}, u32[]{:S(2)}) copy-start(bf16[288,1024]{1,0:T(8,128)(2,1)} %get-tuple-element.538.refs_0_) | copy-start | bytes 1769476 | tf_op jit(solution)/shard_map/cond
  222.9 14.3 %copy-start.21 = (bf16[288,1024]{1,0:T(8,128)(2,1)S(1)}, bf16[288,1024]{1,0:T(8,128)(2,1)}, u32[]{:S(2)}) copy-start(bf16[288,1024]{1,0:T(8,128)(2,1)} %get-tuple-element.539.refs_1_) | copy-start | bytes 1769476 | tf_op jit(solution)/shard_map/cond
  223.0 14.3 %copy-start.30 = (bf16[288,1024]{1,0:T(8,128)(2,1)S(1)}, bf16[288,1024]{1,0:T(8,128)(2,1)}, u32[]{:S(2)}) copy-start(bf16[288,1024]{1,0:T(8,128)(2,1)} %get-tuple-element.543.refs_6_) | copy-start | bytes 1769476 | tf_op jit(solution)/shard_map/cond
  223.0 14.3 %copy-start.31 = (bf16[288,1024]{1,0:T(8,128)(2,1)S(1)}, bf16[288,1024]{1,0:T(8,128)(2,1)}, u32[]{:S(2)}) copy-start(bf16[288,1024]{1,0:T(8,128)(2,1)} %get-tuple-element.544.refs_7_) | copy-start | bytes 1769476 | tf_op jit(solution)/shard_map/cond
  (19 other events, 186.8 us)

commit v4 on v3

--- a/solution.py
+++ b/solution.py
@@ -721,74 +721,70 @@
     wco_ref, in_ref, out_ref, down_ref, up_ref, sems,
     *, steps, which,
 ):
-    step = pl.program_id(0)
     weights = Weights(
         {"wco": wco_hbm, "in": in_hbm, "out": out_hbm, "down": down_hbm, "up": up_hbm},
         {"wco": wco_ref, "in": in_ref, "out": out_ref, "down": down_ref, "up": up_ref},
         sems,
     )
 
-    @pl.when(step == 0)
-    def _():
-        weights.copy("wco").start()
-        for part in range(steps):
-            weights.copy("in", part).start()
-            weights.copy("out", part).start()
-        weights.copy("down").start()
-        weights.copy("up").start()
-        weights.wait("wco")
-        second = n_ref[...] + nn(catt_ref[...], wco_ref[...])
-        hat, scale = norm_rows(second)
-        middle = hat * cgain_ref[...]
-        acc_ref[...] = middle
-        low_ref[...] = middle.astype(BF)
-        scale_ref[:, 0:1] = scale
-
-    @pl.when(step < steps)
-    def _():
-        weights.wait("in", step)
-        weights.wait("out", step)
+    weights.copy("wco").start()
+    for part in range(steps):
+        weights.copy("in", part).start()
+        weights.copy("out", part).start()
+    weights.copy("down").start()
+    weights.copy("up").start()
+    weights.wait("wco")
+    second = n_ref[...] + nn(catt_ref[...], wco_ref[...])
+    hat, scale = norm_rows(second)
+    middle = hat * cgain_ref[...]
+    acc_ref[...] = middle
+    low_ref[...] = middle.astype(BF)
+    scale_ref[:, 0:1] = scale
+
+    def forward(part, carry):
+        weights.wait("in", part)
+        weights.wait("out", part)
         ffn_step(
-            low_ref, acc_ref, weights.part("in", step), weights.part("out", step),
-            slope_ref.at[step], None, None, None,
-        )
-
-    @pl.when(step == steps)
-    def _():
-        weights.wait("down")
-        weights.wait("up")
-        ffn_step(
-            low_ref, acc_ref, down_ref, up_ref, pre_slope_ref, act_ref, downb_ref, adapter_scale
-        )
-        gain = gain_ref[1:2]
-        hat, scale = norm_rows(acc_ref[...] + adapter_scale * upb_ref[...])
-        row = lax.broadcasted_iota(jnp.int32, (low_ref.shape[0], 1), 0)
-        valid = row < len_ref[0, which]
-        y_ref[...] = jnp.where(valid, hat * gain, 0.0).astype(BF)
-        cot = jnp.where(valid, cot_ref[...].astype(F32), 0.0)
-        grad = norm_rows_back(hat, scale, cot * gain)
-        acc_ref[...] = grad
-        grad_ref[...] = grad.astype(BF)
-        adapter_back(
-            grad_ref, acc_ref, low_ref, act_ref, pre_slope_ref, down_ref, up_ref,
-            (ddown_ref, ddownb_ref, dup_ref, dupb_ref), pre_ref,
-        )
-
-    @pl.when(step > steps)
-    def _():
-        part = step - steps - 1
+            low_ref, acc_ref, weights.part("in", part), weights.part("out", part),
+            slope_ref.at[part], None, None, None,
+        )
+        return carry
+
+    lax.fori_loop(0, steps, forward, 0)
+
+    weights.wait("down")
+    weights.wait("up")
+    ffn_step(
+        low_ref, acc_ref, down_ref, up_ref, pre_slope_ref, act_ref, downb_ref, adapter_scale
+    )
+    gain = gain_ref[1:2]
+    hat, scale = norm_rows(acc_ref[...] + adapter_scale * upb_ref[...])
+    row = lax.broadcasted_iota(jnp.int32, (low_ref.shape[0], 1), 0)
+    valid = row < len_ref[0, which]
+    y_ref[...] = jnp.where(valid, hat * gain, 0.0).astype(BF)
+    cot = jnp.where(valid, cot_ref[...].astype(F32), 0.0)
+    grad = norm_rows_back(hat, scale, cot * gain)
+    acc_ref[...] = grad
+    grad_ref[...] = grad.astype(BF)
+    adapter_back(
+        grad_ref, acc_ref, low_ref, act_ref, pre_slope_ref, down_ref, up_ref,
+        (ddown_ref, ddownb_ref, dup_ref, dupb_ref), pre_ref,
+    )
+
+    def backward(part, carry):
         ffn_back_step(
             grad_ref, acc_ref, weights.part("in", part), weights.part("out", part),
             slope_ref.at[part],
         )
-
-    @pl.when(step == 2 * steps)
-    def _():
-        gain = cgain_ref[...]
-        hat = low_ref[...].astype(F32) / gain
-        grad = norm_rows_back(hat, scale_ref[:, 0:1], acc_ref[...] * gain)
-        dsecond_ref[...] = grad
-        dcatt_ref[...] = nt(grad.astype(BF), wco_ref[...]).astype(BF)
+        return carry
+
+    lax.fori_loop(0, steps, backward, 0)
+
+    gain = cgain_ref[...]
+    hat = low_ref[...].astype(F32) / gain
+    grad = norm_rows_back(hat, scale_ref[:, 0:1], acc_ref[...] * gain)
+    dsecond_ref[...] = grad
+    dcatt_ref[...] = nt(grad.astype(BF), wco_ref[...]).astype(BF)
 
 
 def dec_ffn(lengths, n, catt, cot, w, cross, which):
@@ -798,7 +794,7 @@
     weights = [cross["out"], w["ffn_in"], w["ffn_out"], w["down"], w["up"]]
     return pl.pallas_call(
         functools.partial(dec_ffn_kernel, steps=steps, which=which),
-        grid=(2 * steps + 1,),
+        grid=(1,),
         in_specs=[
             pl.BlockSpec(memory_space=pltpu.SMEM),
             pl.BlockSpec((rows, width), lambda i: (which, 0)),
@@ -1436,18 +1432,18 @@
     part1 = at_encoder(lambda saved: enc_ffn(sources, saved[1], w, 1), saved)
     mem1 = to_decoder(part1[0])
 
-    def decoder_short(saved, mem2, cq, kept):
+    def decoder_short(mem2, cq, kept):
         kv2 = product(mem2, cross["pairs"])
         forward = cross_forward(source_lengths, cq, [kv2], 1)
         return kv2, forward, dec_ffn(
             target_lengths, kept[4], forward[0], cotangent, w, cross, 1
         )
 
-    part0, (kv2, short, short_ffn) = at_both(
-        lambda saved, *a: enc_ffn(sources, saved[1], w, 0),
-        decoder_short, saved, mem2, cq, kept,
-    )
-    mem0 = to_decoder(part0[0])
+    part0 = at_encoder(lambda saved: enc_ffn(sources, saved[1], w, 0), saved)
+    mem2, last = lax.optimization_barrier((mem2, part0[0]))
+    mem0 = to_decoder(last)
+    kv2, short, short_ffn = at_decoder(decoder_short, mem2, cq, kept)
+    mem1, kv2 = lax.optimization_barrier((mem1, kv2))
     kv1 = at_decoder(lambda mem1: product(mem1, cross["pairs"]), mem1)
 
     def decoder_long(mem0, kv1, kv2, cq, kept):

time: 319 us -> 298 us (0.934)
  starting transfers between devices: 29.2 us -> 11.6 us
  Pallas kernels: 188 us -> 182 us
    ppermute x3, starting transfers between devices: 24.1 us -> 6.38 us  [to_decoder(): return lax.ppermute(block, 'section', [(0, 1)])]
    pallas_call x1, Pallas kernels: 27.5 us -> 20.8 us  [attend(): pl.pallas_call(functools.partial(attend_kernel, group=group, segs=segs, p...]
    unnamed x47 -> x41, local copies, waits for them, and re-layouts: 6.6 us -> 6.6 us
  transfers between devices with their start and end apart: 7 -> 7, of which waited for: 2 -> 2; matrix products, arithmetic and copies ran while one was open for 0% -> 0% of each run, Pallas kernels for 18% -> 19%
where the time goes in v4:
time: 298 us; the launch traced here: 293 us
  Pallas kernels  182 us (61%)
  waiting for transfers between devices  84.6 us (28%)
  starting transfers between devices  11.6 us (4%)
  local copies, waits for them, and re-layouts  6.68 us (2%)
  other arithmetic  4.4 us (1%)
    ppermute x4, waiting for transfers between devices, to_encoder(): return lax.ppermute(block, 'section', [(1, 0)])  71.9 us
    pallas_call x1, Pallas kernels, finish(): pl.pallas_call(functools.partial(finish_kernel, devices=devices), grid=(p...  62.7 us
    pallas_call x3, Pallas kernels, enc_ffn(): pl.pallas_call(enc_ffn_kernel, grid=(1,), in_specs=[pl.BlockSpec((rows, w...  43.4 us
    pallas_call x3, Pallas kernels, enc_ffn_back(): pl.pallas_call(functools.partial(enc_ffn_back_kernel, pieces=len(dmems)),...  40.7 us
    pallas_call x1, Pallas kernels, attend(): pl.pallas_call(functools.partial(attend_kernel, group=group, segs=segs, p...  20.8 us
    ppermute x3, waiting for transfers between devices, to_decoder(): return lax.ppermute(block, 'section', [(0, 1)])  12.7 us
    pallas_call x1, Pallas kernels, product(): pl.pallas_call(product_kernel, grid=(width // tile,), in_specs=[whole((ro...  9.61 us
    unnamed x41, local copies, waits for them, and re-layouts  6.6 us
  transfers between devices with their start and end apart: 7, of which 2 were waited for; matrix products, arithmetic and copies ran while one was open for 0% of the time, Pallas kernels for 19%

profile of v4, /device:TPU:0, one launch (start us, length us, event | category | flops | bytes accessed | tf_op | source)
XLA Modules:
  0.0 292.6 jit_solution(1067954271439438569)
XLA Ops:
  1.6 45.2 %conditional.11 = (bf16[864,3072]{1,0:T(8,128)(2,1)}, bf16[864,1024]{1,0:T(8,128)(2,1)}, f32[864,1024]{1,0:T(8,128)}, bf16[16,800,768]{2,1,0:T(8,128)(2,1)}, bf1...) conditional(s32[]{:T(128)} %convert_element_type.4, ...), branch_computations={%region_0.1_spmd, %region_1.2_spmd} | conditional | bytes 16834880 | solution.py:1383
  1.8 9.6 %product.6.refs_0_.refs_1_.refs_2_ = bf16[864,3072]{1,0:T(8,128)(2,1)} custom-call(bf16[864,1024]{1,0:T(8,128)(2,1)} %get-tuple-element.323.x_ref, bf16[1024,3072]{1,0:T(8,128)(2,1)} %get-tuple-element.324.w_ref), custom_call_target="tpu_custom_call" | custom-call | tf_op jit(solution)/shard_map/cond/branch_1_fun/product/pallas_call | solution.py:92
  11.4 20.8 %attend.5 = (bf16[864,1024]{1,0:T(8,128)(2,1)}, f32[864,1024]{1,0:T(8,128)}, bf16[16,800,768]{2,1,0:T(8,128)(2,1)}, bf16[16,128,96]{2,1,0:T(8,128)(2,1)}) custom-call(s32[1,2]{1,0:T(1,128)} %get-tuple-element.325.len_ref, bf16[864,3072]{1,0:T(8,128)(2,1)} %product.6.refs_0_.refs_1_.refs_2_, bf16[864,3072]{1,0:T(8,128)(2,1)} %product.6.refs_0_.refs_1_.refs_2_, ...), custom_call_target="tpu_custom_call" | custom-call | tf_op jit(solution)/shard_map/cond/branch_1_fun/attend/pallas_call | solution.py:293
  32.3 14.5 %enc_ffn.3 = (bf16[288,1024]{1,0:T(8,128)(2,1)}, bf16[288,4096]{1,0:T(8,128)(2,1)}, bf16[288,512]{1,0:T(8,128)(2,1)}, bf16[288,512]{1,0:T(8,128)(2,1)}, bf16[288,1024]{1,0:T(8,128)(2,1)}, /*index=5*/f32[288,128]{1,0:T(8,128)}) custom-call(bf16[864,1024]{1,0:T(8,128)(2,1)} %get-tuple-element.323.x_ref, bf16[864,1024]{1,0:T(8,128)(2,1)} %get-tuple-element.740.att_ref, ...), custom_call_target="tpu_custom_call" | custom-call | tf_op jit(solution)/shard_map/cond/branch_1_fun/enc_ffn/pallas_call | solution.py:518
  46.8 2.1 collective-permute-start
  48.9 14.9 %conditional.13 = ((bf16[288,1024]{1,0:T(8,128)(2,1)}, bf16[288,4096]{1,0:T(8,128)(2,1)}, bf16[288,512]{1,0:T(8,128)(2,1)}, bf16[288,512]{1,0:T(8,128)(2,1)}, bf...) conditional(s32[]{:T(128)} %convert_element_type.4, () %tuple.91, (bf16[864,1024]{1,0:T(8,128)(2,1)}, ...), branch_computations={%region_4.5_spmd, %region_5.6_spmd} | conditional | bytes 8 | solution.py:1383
  49.3 14.5 %enc_ffn.5 = (bf16[288,1024]{1,0:T(8,128)(2,1)}, bf16[288,4096]{1,0:T(8,128)(2,1)}, bf16[288,512]{1,0:T(8,128)(2,1)}, bf16[288,512]{1,0:T(8,128)(2,1)}, bf16[288,1024]{1,0:T(8,128)(2,1)}, /*index=5*/f32[288,128]{1,0:T(8,128)}) custom-call(bf16[864,1024]{1,0:T(8,128)(2,1)} %get-tuple-element.364.x_ref, bf16[864,1024]{1,0:T(8,128)(2,1)} %get-tuple-element.365.att_ref, ...), custom_call_target="tpu_custom_call" | custom-call | tf_op jit(solution)/shard_map/cond/branch_1_fun/enc_ffn/pallas_call | solution.py:518
  63.8 2.1 collective-permute-start.2
  65.9 14.5 %conditional.12 = ((bf16[288,1024]{1,0:T(8,128)(2,1)}, bf16[288,4096]{1,0:T(8,128)(2,1)}, bf16[288,512]{1,0:T(8,128)(2,1)}, bf16[288,512]{1,0:T(8,128)(2,1)}, bf...) conditional(s32[]{:T(128)} %convert_element_type.4, () %tuple.88, (bf16[864,1024]{1,0:T(8,128)(2,1)}, ...), branch_computations={%region_2.3_spmd, %region_3.4_spmd} | conditional | bytes 8 | solution.py:1383
  65.9 14.5 %enc_ffn.4 = (bf16[288,1024]{1,0:T(8,128)(2,1)}, bf16[288,4096]{1,0:T(8,128)(2,1)}, bf16[288,512]{1,0:T(8,128)(2,1)}, bf16[288,512]{1,0:T(8,128)(2,1)}, bf16[288,1024]{1,0:T(8,128)(2,1)}, /*index=5*/f32[288,128]{1,0:T(8,128)}) custom-call(bf16[864,1024]{1,0:T(8,128)(2,1)} %get-tuple-element.354.x_ref, bf16[864,1024]{1,0:T(8,128)(2,1)} %get-tuple-element.355.att_ref, ...), custom_call_target="tpu_custom_call" | custom-call | tf_op jit(solution)/shard_map/cond/branch_1_fun/enc_ffn/pallas_call | solution.py:518
  80.4 2.1 collective-permute-start.1
  82.8 12.7 %collective-permute-done.1 = bf16[288,1024]{1,0:T(8,128)(2,1)} collective-permute-done((bf16[288,1024]{1,0:T(8,128)(2,1)}, bf16[288,1024]{1,0:T(8,128)(2,1)}, u32[]{:S(2)}, u32[]{:S(2)}) %collective-permute-start.1) | collective-permute-done | bytes 589856 | tf_op jit(solution)/shard_map/ppermute | solution.py:1387
  101.2 71.9 %collective-permute-done.3 = bf16[288,1024]{1,0:T(8,128)(2,1)} collective-permute-done((bf16[288,1024]{1,0:T(8,128)(2,1)}, bf16[288,1024]{1,0:T(8,128)(2,1)}, u32[]{:S(2)}, u32[]{:S(2)}) %collective-permute-start.3) | collective-permute-done | bytes 589856 | tf_op jit(solution)/shard_map/ppermute | solution.py:1391
  173.0 13.7 %conditional.19 = ((f32[288,1024]{1,0:T(8,128)}, bf16[288,1024]{1,0:T(8,128)(2,1)}, bf16[288,1024]{1,0:T(8,128)(2,1)}, bf16[288,512]{1,0:T(8,128)(2,1)})) conditional(s32[]{:T(128)} %convert_element_type.4, () %tuple.87, (bf16[288,1024]{1,0:T(8,128)(2,1)}, bf16[288,1024]{1,0:T(8,128)(2,1)}, bf16[288,1024]{1,0:T(8,128)(2,1)}, ...), branch_computations={%region_16.17_spmd, %region_17.18_spmd} | conditional | bytes 8 | solution.py:1383
  173.1 13.5 %enc_ffn_back.3 = (f32[288,1024]{1,0:T(8,128)}, bf16[288,1024]{1,0:T(8,128)(2,1)}, bf16[288,1024]{1,0:T(8,128)(2,1)}, bf16[288,512]{1,0:T(8,128)(2,1)}) custom-call(bf16[288,1024]{1,0:T(8,128)(2,1)} %get-tuple-element.470.refs_0_, bf16[288,1024]{1,0:T(8,128)(2,1)} %get-tuple-element.471.refs_1_, bf16[288,1024]{1,0:T(8,128)(2,1)} %get-tuple-element.472.refs_2_, ...), custom_call_target="tpu_custom_call" | custom-call | tf_op jit(solution)/shard_map/cond/branch_1_fun/enc_ffn_back/pallas_call | solution.py:635
  186.8 13.1 %conditional.20 = ((f32[288,1024]{1,0:T(8,128)}, bf16[288,1024]{1,0:T(8,128)(2,1)}, bf16[288,1024]{1,0:T(8,128)(2,1)}, bf16[288,512]{1,0:T(8,128)(2,1)})) conditional(s32[]{:T(128)} %convert_element_type.4, () %tuple.105, (bf16[288,1024]{1,0:T(8,128)(2,1)}, bf16[288,1024]{1,0:T(8,128)(2,1)S(1)}, bf16[288,1024]{1,0:T(8,128)(2,1)S(1)}, ...), branch_computations={%region_18.19_spmd, %region_19.20_spmd} | conditional | bytes 8 | solution.py:1383
  186.9 13.0 %enc_ffn_back.4 = (f32[288,1024]{1,0:T(8,128)}, bf16[288,1024]{1,0:T(8,128)(2,1)}, bf16[288,1024]{1,0:T(8,128)(2,1)}, bf16[288,512]{1,0:T(8,128)(2,1)}) custom-call(bf16[288,1024]{1,0:T(8,128)(2,1)} %get-tuple-element.482.refs_0_, bf16[288,1024]{1,0:T(8,128)(2,1)S(1)} %get-tuple-element.483.refs_1_, bf16[288,1024]{1,0:T(8,128)(2,1)S(1)} %get-tuple-element.484.refs_2_, ...), custom_call_target="tpu_custom_call" | custom-call | tf_op jit(solution)/shard_map/cond/branch_1_fun/enc_ffn_back/pallas_call | solution.py:635
  200.0 19.7 %conditional.21 = (f32[288,1024]{1,0:T(8,128)}, bf16[288,1024]{1,0:T(8,128)(2,1)}, f32[1024,512]{1,0:T(8,128)}, f32[1,512]{1,0:T(1,128)S(1)}, f32[512,1024]{1,0:T(8,128)}, /*index=5*/f32[1,1024]{1,0:T(1,128)S(1)}) conditional(s32[]{:T(128)} %convert_element_type.4, () %tuple.107, (bf16[192,1024]{1,0:T(8,128)(2,1)}, bf16[96,1024]{1,0:T(8,128)(2,1)}, ...), branch_computations={%region_20.21_spmd, %region_21.22_spmd} | conditional | bytes 15335724 | solution.py:1383
  200.1 14.1 %enc_ffn_back.5 = (f32[288,1024]{1,0:T(8,128)}, bf16[288,1024]{1,0:T(8,128)(2,1)}, bf16[288,1024]{1,0:T(8,128)(2,1)}, bf16[288,512]{1,0:T(8,128)(2,1)}) custom-call(bf16[192,1024]{1,0:T(8,128)(2,1)} %get-tuple-element.500.refs_0_, bf16[96,1024]{1,0:T(8,128)(2,1)} %get-tuple-element.501.refs_1_, bf16[288,1024]{1,0:T(8,128)(2,1)} %get-tuple-element.502.refs_2_, ...), custom_call_target="tpu_custom_call" | custom-call | tf_op jit(solution)/shard_map/cond/branch_1_fun/enc_ffn_back/pallas_call | solution.py:635
  214.3 5.2 %adapter_grads.1 = (f32[1024,512]{1,0:T(8,128)}, f32[1,512]{1,0:T(1,128)S(1)}, f32[512,1024]{1,0:T(8,128)}, f32[1,1024]{1,0:T(1,128)S(1)}) custom-call(bf16[288,1024]{1,0:T(8,128)(2,1)S(1)} %copy-done.21, bf16[288,1024]{1,0:T(8,128)(2,1)S(1)} %copy-done.20, bf16[288,1024]{1,0:T(8,128)(2,1)S(1)} %get-tuple-element.503.refs_3_.refs_2_, ...), custom_call_target="tpu_custom_call" | custom-call | tf_op jit(solution)/shard_map/cond/branch_1_fun/adapter_grads/pallas_call | solution.py:678
  219.7 62.7 %finish.1 = (bf16[864,512]{1,0:T(8,128)(2,1)}, bf16[512,512]{1,0:T(8,128)(2,1)}, bf16[512,512]{1,0:T(8,128)(2,1)}, bf16[512,1024]{1,0:T(8,128)(2,1)}, bf16[1024,...) custom-call(bf16[864,3072]{1,0:T(8,128)(2,1)} %get-tuple-element.623.q_ref.k_ref.v_ref, ...), custom_call_target="tpu_custom_call" | custom-call | tf_op jit(solution)/shard_map/finish/pallas_call | solution.py:1292
  282.4 1.9 copy.29
  284.3 2.8 bitcast_convert_fusion.1
  287.1 1.6 bitcast_convert_fusion
  (91 shorter events, 10.6 us)
Async XLA Ops:
  11.4 20.9 %copy-start.1 = (bf16[1024,1024]{1,0:T(8,128)(2,1)S(1)}, bf16[1024,1024]{1,0:T(8,128)(2,1)}, u32[]{:S(2)}) copy-start(bf16[1024,1024]{1,0:T(8,128)(2,1)} %get-tuple-element.335.wo_hbm) | copy-start | bytes 6291460 | tf_op jit(solution)/shard_map/cond
  11.4 20.9 %copy-start.6 = (bf16[1024,512]{1,0:T(8,128)(2,1)S(1)}, bf16[1024,512]{1,0:T(8,128)(2,1)}, u32[]{:S(2)}) copy-start(bf16[1024,512]{1,0:T(8,128)(2,1)} %get-tuple-element.338.down_hbm) | copy-start | bytes 3145732 | tf_op jit(solution)/shard_map/cond
  11.4 20.9 %copy-start.9 = (bf16[512,1024]{1,0:T(8,128)(2,1)S(1)}, bf16[512,1024]{1,0:T(8,128)(2,1)}, u32[]{:S(2)}) copy-start(bf16[512,1024]{1,0:T(8,128)(2,1)} %get-tuple-element.339.up_hbm) | copy-start | bytes 3145732 | tf_op jit(solution)/shard_map/cond
  11.4 20.9 %copy-start.26 = (f32[2,1024]{1,0:T(2,128)S(1)}, f32[2,1024]{1,0:T(2,128)}, u32[]{:S(2)}) copy-start(f32[2,1024]{1,0:T(2,128)} %get-tuple-element.332.gain_ref) | copy-start | bytes 24580 | tf_op jit(solution)/shard_map/cond
  11.4 20.9 %copy-start.41 = (f32[1,1024]{1,0:T(1,128)S(1)}, f32[1,1024]{1,0:T(1,128)}, u32[]{:S(2)}) copy-start(f32[1,1024]{1,0:T(1,128)} %get-tuple-element.334.upb_ref) | copy-start | bytes 12292 | tf_op jit(solution)/shard_map/cond
  11.4 20.9 %copy-start.44 = (f32[1,512]{1,0:T(1,128)S(1)}, f32[1,512]{1,0:T(1,128)}, u32[]{:S(2)}) copy-start(f32[1,512]{1,0:T(1,128)} %get-tuple-element.333.downb_ref) | copy-start | bytes 6148 | tf_op jit(solution)/shard_map/cond
  46.8 33.6 %collective-permute-start = (bf16[288,1024]{1,0:T(8,128)(2,1)}, bf16[288,1024]{1,0:T(8,128)(2,1)}, u32[]{:S(2)}, u32[]{:S(2)}) collective-permute-start(bf16[288,1024]{1,0:T(8,128)(2,1)} %get-tuple-element.626), channel_id=1, source_target_pairs={{0,16},{1,17},{2,18},{3,19},{4,20},{5,21},{6,22},{7,23},{8,24},{9,... | collective-permute-start | bytes 1769480 | tf_op jit(solution)/shard_map/ppermute | solution.py:1387
  63.8 18.9 %collective-permute-start.2 = (bf16[288,1024]{1,0:T(8,128)(2,1)}, bf16[288,1024]{1,0:T(8,128)(2,1)}, u32[]{:S(2)}, u32[]{:S(2)}) collective-permute-start(bf16[288,1024]{1,0:T(8,128)(2,1)} %get-tuple-element.630), channel_id=1, source_target_pairs={{0,16},{1,17},{2,18},{3,19},{4,20},{5,21},{6,22},{7,23},{8,24},{9,... | collective-permute-start | bytes 1769480 | tf_op jit(solution)/shard_map/ppermute | solution.py:1387
  80.4 15.1 %collective-permute-start.1 = (bf16[288,1024]{1,0:T(8,128)(2,1)}, bf16[288,1024]{1,0:T(8,128)(2,1)}, u32[]{:S(2)}, u32[]{:S(2)}) collective-permute-start(bf16[288,1024]{1,0:T(8,128)(2,1)} %get-tuple-element.628), channel_id=1, source_target_pairs={{0,16},{1,17},{2,18},{3,19},{4,20},{5,21},{6,22},{7,23},{8,24},{9,... | collective-permute-start | bytes 1769480 | tf_op jit(solution)/shard_map/ppermute | solution.py:1387
  95.9 77.1 %collective-permute-start.3 = (bf16[288,1024]{1,0:T(8,128)(2,1)}, bf16[288,1024]{1,0:T(8,128)(2,1)}, u32[]{:S(2)}, u32[]{:S(2)}) collective-permute-start(bf16[288,1024]{1,0:T(8,128)(2,1)} %get-tuple-element.636), channel_id=1, source_target_pairs={{16,0},{17,1},{18,2},{19,3},{20,4},{21,5},{22,6},{23,7},{24,8},{25... | collective-permute-start | bytes 1769480 | tf_op jit(solution)/shard_map/ppermute | solution.py:1391
  97.2 89.6 %collective-permute-start.4 = (bf16[288,1024]{1,0:T(8,128)(2,1)}, bf16[288,1024]{1,0:T(8,128)(2,1)}, u32[]{:S(2)}, u32[]{:S(2)}) collective-permute-start(bf16[288,1024]{1,0:T(8,128)(2,1)} %get-tuple-element.658), channel_id=1, source_target_pairs={{16,0},{17,1},{18,2},{19,3},{20,4},{21,5},{22,6},{23,7},{24,8},{25... | collective-permute-start | bytes 1769480 | tf_op jit(solution)/shard_map/ppermute | solution.py:1391
  98.5 101.4 %collective-permute-start.5 = (bf16[192,1024]{1,0:T(8,128)(2,1)}, bf16[192,1024]{1,0:T(8,128)(2,1)}, u32[]{:S(2)}, u32[]{:S(2)}) collective-permute-start(bf16[192,1024]{1,0:T(8,128)(2,1)} %get-tuple-element.664), channel_id=1, source_target_pairs={{16,0},{17,1},{18,2},{19,3},{20,4},{21,5},{22,6},{23,7},{24,8},{25... | collective-permute-start | bytes 1179656 | tf_op jit(solution)/shard_map/ppermute | solution.py:1391
  99.8 100.1 %collective-permute-start.6 = (bf16[96,1024]{1,0:T(8,128)(2,1)}, bf16[96,1024]{1,0:T(8,128)(2,1)}, u32[]{:S(2)}, u32[]{:S(2)}) collective-permute-start(bf16[96,1024]{1,0:T(8,128)(2,1)} %get-tuple-element.665), channel_id=1, source_target_pairs={{16,0},{17,1},{18,2},{19,3},{20,4},{21,5},{22,6},{23,7},{24,8},{25... | collective-permute-start | bytes 589832 | tf_op jit(solution)/shard_map/ppermute | solution.py:1391
  199.9 19.7 %copy-start.13 = (bf16[864,1024]{1,0:T(8,128)(2,1)S(1)}, bf16[864,1024]{1,0:T(8,128)(2,1)}, u32[]{:S(2)}) copy-start(bf16[864,1024]{1,0:T(8,128)(2,1)} %get-tuple-element.624.o_ref) | copy-start | bytes 5308420
  200.0 19.7 %copy-start.53 = (f32[1,1024]{1,0:T(1,128)S(1)}, f32[1,1024]{1,0:T(1,128)}, u32[]{:S(2)}) copy-start(f32[1,1024]{1,0:T(1,128)} %get-tuple-element.690.long_upb) | copy-start | bytes 12292
  200.0 19.7 %copy-start.54 = (f32[1,1024]{1,0:T(1,128)S(1)}, f32[1,1024]{1,0:T(1,128)}, u32[]{:S(2)}) copy-start(f32[1,1024]{1,0:T(1,128)} %get-tuple-element.694.short_upb) | copy-start | bytes 12292
  200.0 14.2 %copy-start.20 = (bf16[288,1024]{1,0:T(8,128)(2,1)S(1)}, bf16[288,1024]{1,0:T(8,128)(2,1)}, u32[]{:S(2)}) copy-start(bf16[288,1024]{1,0:T(8,128)(2,1)} %get-tuple-element.516.refs_1_) | copy-start | bytes 1769476 | tf_op jit(solution)/shard_map/cond
  200.0 14.2 %copy-start.21 = (bf16[288,1024]{1,0:T(8,128)(2,1)S(1)}, bf16[288,1024]{1,0:T(8,128)(2,1)}, u32[]{:S(2)}) copy-start(bf16[288,1024]{1,0:T(8,128)(2,1)} %get-tuple-element.515.refs_0_) | copy-start | bytes 1769476 | tf_op jit(solution)/shard_map/cond
  200.0 14.2 %copy-start.29 = (bf16[288,1024]{1,0:T(8,128)(2,1)S(1)}, bf16[288,1024]{1,0:T(8,128)(2,1)}, u32[]{:S(2)}) copy-start(bf16[288,1024]{1,0:T(8,128)(2,1)} %get-tuple-element.520.refs_6_) | copy-start | bytes 1769476 | tf_op jit(solution)/shard_map/cond
  200.0 14.2 %copy-start.30 = (bf16[288,1024]{1,0:T(8,128)(2,1)S(1)}, bf16[288,1024]{1,0:T(8,128)(2,1)}, u32[]{:S(2)}) copy-start(bf16[288,1024]{1,0:T(8,128)(2,1)} %get-tuple-element.521.refs_7_) | copy-start | bytes 1769476 | tf_op jit(solution)/shard_map/cond
  200.0 14.2 %copy-start.33 = (bf16[288,512]{1,0:T(8,128)(2,1)S(1)}, bf16[288,512]{1,0:T(8,128)(2,1)}, u32[]{:S(2)}) copy-start(bf16[288,512]{1,0:T(8,128)(2,1)} %get-tuple-element.519.refs_5_) | copy-start | bytes 884740 | tf_op jit(solution)/shard_map/cond
  200.0 14.2 %copy-start.34 = (bf16[288,512]{1,0:T(8,128)(2,1)S(1)}, bf16[288,512]{1,0:T(8,128)(2,1)}, u32[]{:S(2)}) copy-start(bf16[288,512]{1,0:T(8,128)(2,1)} %get-tuple-element.518.refs_4_) | copy-start | bytes 884740 | tf_op jit(solution)/shard_map/cond
  200.1 14.2 %copy-start.35 = (bf16[288,512]{1,0:T(8,128)(2,1)S(1)}, bf16[288,512]{1,0:T(8,128)(2,1)}, u32[]{:S(2)}) copy-start(bf16[288,512]{1,0:T(8,128)(2,1)} %get-tuple-element.517.refs_3_) | copy-start | bytes 884740 | tf_op jit(solution)/shard_map/cond
  200.1 14.2 %copy-start.36 = (bf16[288,512]{1,0:T(8,128)(2,1)S(1)}, bf16[288,512]{1,0:T(8,128)(2,1)}, u32[]{:S(2)}) copy-start(bf16[288,512]{1,0:T(8,128)(2,1)} %get-tuple-element.523.refs_9_) | copy-start | bytes 884740 | tf_op jit(solution)/shard_map/cond
  (15 other events, 136.7 us)
